TPU v7x, 32 devices: a whole 2x2x4 slice. The times are simulated.
32 devices in a mesh: seq: 16 (over z, y, x), head: 2 (over core).
Axes of the slice: x: 2, y: 2, z: 4, core: 2. Of those that a mesh axis runs over, the one named last changes fastest.
Arguments:
- x_in: bfloat16 [2, 4096, 1536], P(None, 'seq'), may hold values from -6 to 6
- cotangent: bfloat16 [2, 4096, 1536], P(None, 'seq'), may hold values from -6 to 6
- cond: bfloat16 [2, 8, 1536], replicated, may hold values from -6 to 6
- context: bfloat16 [2, 8, 128, 768], replicated, may hold values from -6 to 6
- clip_lengths: int32 [2, 8], replicated, may hold values from 204 to 2048, as said below
- pad_mask: int32 [2, 4096], replicated, may hold values 0 or 1
- owners: int32 [2, 1800], P('head'), may hold values from 0 to 15, as said below
- master: float32 [2, 2256, 128, 128], P('head', 'seq'), may hold values from -4 to 4, as said below
- first_moment: float32 [2, 2256, 128, 128], P('head', 'seq'), may hold values from -1048576 to 1048576
- second_moment: float32 [2, 2256, 128, 128], P('head', 'seq'), may hold values from 0 to 1048576, as said below
Outputs:
- out_block: bfloat16 [2, 4096, 1536], P(None, 'seq')
- grad_input: float32 [2, 4096, 1536], P(None, 'seq')
- new_master: float32 [2, 2256, 128, 128], P('head', 'seq')
- new_first: float32 [2, 2256, 128, 128], P('head', 'seq')
- new_second: float32 [2, 2256, 128, 128], P('head', 'seq')
Inputs may be any that keep to these rules, and one draw needn't show every extreme that they name: `clip_lengths`: the clips of a micro-batch fill its 4096 frames; each clip has 204 frames or more, and in every micro-batch one clip has exactly 2048. `owners`: every tile of a head shard has one owner; no owner holds more than 141 tiles of one shard, and in each shard one owner holds exactly 141. `master`: slots that hold no tile carry finite values. `second_moment`: every entry is positive.
All inputs are finite; a program needn't handle non-finite values.
Results may differ from a plain program's by a relative error of at most 0.035.
Values may be sent and summed in bfloat16 or wider, within the bound.
No kernel may reach another device: no remote copies, remote signals or barrier semaphores. Data moves between devices by JAX's collectives and lax.ppermute only.
A program may use at most 768 MiB of HBM per device.

v0:
```python
import jax
import jax.numpy as jnp
import numpy as np
from jax import lax
from jax.sharding import PartitionSpec as P

D = 1536
HD = 64
FF = 6144
DC = 768
CTX = 128
WIN = 128
TS = 128
STEP = 5
MINLEN = 204


PRECISE = lax.Precision.HIGHEST
EPS_NORM = 1e-06
BETA_ONE = 0.9
BETA_TWO = 0.95
ADAM_EPS = 1e-08
WEIGHT_DECAY = 0.1
LEARN_RATE = 0.5
MASKED = -1e30


def as_sent(shard):
    return jax.tree.map(lambda a: a.astype(jnp.bfloat16) if a.dtype == jnp.float32 else a, shard)


def padded(shard, sides, width):
    for axis, dim in sides:
        size, length = (lax.axis_size(axis), shard.shape[dim])
        up = [(i, (i + 1) % size) for i in range(size - 1)]
        down = [(j, i) for i, j in up]
        last = lax.slice_in_dim(shard, length - width, length, axis=dim)
        initial = lax.slice_in_dim(shard, 0, width, axis=dim)
        before = lax.ppermute(last, axis, up)
        after = lax.ppermute(initial, axis, down)
        shard = jnp.concatenate([before, shard, after], axis=dim)
    return shard


def piece_shapes(head_count):
    head_cols = D // head_count
    ff_cols = FF // head_count
    return [
        (D, 3 * head_cols),
        (head_cols, D),
        (D, head_cols),
        (DC, 2 * head_cols),
        (head_cols, D),
        (D, 2 * ff_cols),
        (ff_cols, D),
        (D, 6 * D // head_count),
    ]


def fan_inputs():
    return [D, D // 64, D, DC, D // 32, D, FF // 4, 4 * D]


def slot_layout(owner_row, seq_count, capacity):
    onehot = (owner_row[:, None] == jnp.arange(seq_count, dtype=jnp.int32)[None, :]).astype(
        jnp.int32
    )
    before = jnp.cumsum(onehot, axis=0) - onehot
    tile_place = owner_row * capacity + jnp.sum(before * onehot, axis=1)
    tile_count = owner_row.shape[0]
    slot_tile = (
        jnp.full((seq_count * capacity,), -1, jnp.int32)
        .at[tile_place]
        .set(jnp.arange(tile_count, dtype=jnp.int32))
    )
    return (tile_place, slot_tile)


def slot_rates(slot_tile, shapes):
    counts = [row_count * col_count // (TS * TS) for row_count, col_count in shapes]
    kind_ends = jnp.array([int(end_value) for end_value in np.cumsum(counts)[:-1]], dtype=jnp.int32)
    slot_kind = jnp.sum((slot_tile[:, None] >= kind_ends[None, :]).astype(jnp.int32), axis=1)
    rate_table = jnp.array(
        [LEARN_RATE * fan_in ** (-0.5) for fan_in in fan_inputs()], dtype=jnp.float32
    )
    onehot = (slot_kind[:, None] == jnp.arange(len(shapes), dtype=jnp.int32)[None, :]).astype(
        jnp.float32
    )
    return jnp.sum(onehot * rate_table[None, :], axis=1)


def split_pieces(flattened, shapes):
    pieces = []
    offset = 0
    for row_count, col_count in shapes:
        pieces.append(
            flattened[offset : offset + row_count * col_count].reshape(row_count, col_count)
        )
        offset = offset + row_count * col_count
    return pieces


def layer_norm(values):
    centred = values - jnp.mean(values, axis=-1, keepdims=True)
    inverse = lax.rsqrt(jnp.mean(centred * centred, axis=-1, keepdims=True) + EPS_NORM)
    return (centred * inverse, inverse)


def norm_back(grad, normed, inverse, scale_part):
    dnormed = grad * (1.0 + scale_part)
    dvalues = inverse * (
        dnormed
        - jnp.mean(dnormed, axis=-1, keepdims=True)
        - normed * jnp.mean(dnormed * normed, axis=-1, keepdims=True)
    )
    return (dvalues, grad * normed, grad)


def clip_ids(lengths, positions):
    clip_ends = jnp.cumsum(lengths)
    return jnp.sum((positions[:, None] >= clip_ends[None, :]).astype(jnp.int32), axis=1)


def window_mask(query_pos, key_pos, key_flag, lengths, frames):
    query_clip = clip_ids(lengths, query_pos)
    key_clip = clip_ids(lengths, key_pos)
    offset = key_pos[None, :] - query_pos[:, None]
    is_near = (offset <= WIN) & (offset >= -WIN)
    is_inside = (key_pos >= 0) & (key_pos < frames)
    same_clip = query_clip[:, None] == key_clip[None, :]
    is_kept = (key_flag[None, :] == 1) | (offset == 0)
    return is_near & is_inside[None, :] & same_clip & is_kept


def attend(queries, keys, values, allowed, head_count):
    row_count = queries.shape[0]
    query_heads = queries.reshape(row_count, head_count, HD)
    key_heads = keys.reshape(keys.shape[0], head_count, HD)
    value_heads = values.reshape(values.shape[0], head_count, HD)
    scores = jnp.einsum(
        "qhd,khd->hqk", query_heads, key_heads, preferred_element_type=jnp.float32
    ) * HD ** (-0.5)
    scores = jnp.where(allowed[None], scores, MASKED)
    highest = jnp.max(scores, axis=-1, keepdims=True)
    expo = jnp.exp(scores - highest)
    total = jnp.sum(expo, axis=-1, keepdims=True)
    probs = (expo / total).astype(jnp.bfloat16)
    result = jnp.einsum("hqk,khd->qhd", probs, value_heads, preferred_element_type=jnp.float32)
    return (result.reshape(row_count, -1), highest + jnp.log(total))


def attend_back(queries, keys, values, allowed, log_total, grad_out, head_count):
    row_count = queries.shape[0]
    scale = HD ** (-0.5)
    query_heads = queries.reshape(row_count, head_count, HD)
    key_heads = keys.reshape(keys.shape[0], head_count, HD)
    value_heads = values.reshape(values.shape[0], head_count, HD)
    grad_heads = grad_out.reshape(row_count, head_count, HD)
    scores = (
        jnp.einsum("qhd,khd->hqk", query_heads, key_heads, preferred_element_type=jnp.float32)
        * scale
    )
    probs = jnp.where(allowed[None], jnp.exp(scores - log_total), 0.0)
    dprobs = jnp.einsum("qhd,khd->hqk", grad_heads, value_heads, preferred_element_type=jnp.float32)
    dscores = (probs * (dprobs - jnp.sum(probs * dprobs, axis=-1, keepdims=True))).astype(
        jnp.bfloat16
    )
    dquery = (
        jnp.einsum("hqk,khd->qhd", dscores, key_heads, preferred_element_type=jnp.float32) * scale
    )
    dkey = (
        jnp.einsum("hqk,qhd->khd", dscores, query_heads, preferred_element_type=jnp.float32) * scale
    )
    dvalue = jnp.einsum(
        "hqk,qhd->khd", probs.astype(jnp.bfloat16), grad_heads, preferred_element_type=jnp.float32
    )
    return (
        dquery.reshape(row_count, -1),
        dkey.reshape(keys.shape[0], -1),
        dvalue.reshape(values.shape[0], -1),
    )


def add_branch(residual, partial_value):
    rounded = partial_value.astype(jnp.bfloat16)
    shares = lax.psum_scatter(rounded, "head", scatter_dimension=0, tiled=True).astype(jnp.float32)
    share_rows = shares.shape[0]
    own_rows = lax.dynamic_slice_in_dim(
        residual, lax.axis_index("head") * share_rows, share_rows, 0
    )
    return lax.all_gather(as_sent(own_rows + shares), "head", axis=0, tiled=True)


def input_grad(partial_value):
    return lax.psum(partial_value.astype(jnp.bfloat16), "head").astype(jnp.float32)


def adam_step(weight, first, second, grads, rate):
    first = BETA_ONE * first + (1.0 - BETA_ONE) * grads
    second = BETA_TWO * second + (1.0 - BETA_TWO) * grads * grads
    first_hat = first / (1.0 - BETA_ONE**STEP)
    second_hat = second / (1.0 - BETA_TWO**STEP)
    weight = weight - rate * (first_hat / (jnp.sqrt(second_hat) + ADAM_EPS) + WEIGHT_DECAY * weight)
    return (weight, first, second)


def on_device(
    x_in,
    cotangent,
    cond,
    context,
    clip_lengths,
    pad_mask,
    owners,
    master,
    first_moment,
    second_moment,
):
    seq_count = lax.axis_size("seq")
    head_count = lax.axis_size("head")
    capacity = master.shape[1]
    row_count = x_in.shape[1]
    micro_count = x_in.shape[0]
    frames = pad_mask.shape[1]
    clip_count = clip_lengths.shape[1]
    head_cols = D // head_count
    ff_cols = FF // head_count
    mod_cols = 6 * D // head_count
    local_heads = head_cols // HD
    first_row = lax.axis_index("seq") * row_count
    clip_span = min(clip_count, row_count // MINLEN + 2)
    tile_place, slot_tile = slot_layout(owners[0], seq_count, capacity)
    copies = lax.all_gather(master[0].astype(jnp.bfloat16), "seq", axis=0, tiled=True)
    shapes = piece_shapes(head_count)
    w_qkv, w_out, w_cq, w_ckv, w_cout, w_glu, w_down, w_mod = split_pieces(
        copies[tile_place].reshape(-1), shapes
    )
    cond_rows = cond.reshape(micro_count * clip_count, D)
    mod_part = jnp.dot(cond_rows, w_mod, preferred_element_type=jnp.float32)
    mod_all = (
        lax.all_gather(mod_part.astype(jnp.bfloat16), "head", axis=1, tiled=True)
        .astype(mod_part.dtype)
        .reshape(micro_count, clip_count, 6 * D)
    )
    grads = [jnp.zeros(shape_pair, jnp.float32) for shape_pair in shapes]
    outputs = []
    input_grads = []
    positions = first_row + jnp.arange(row_count, dtype=jnp.int32)
    ext_pos = first_row - WIN + jnp.arange(row_count + 2 * WIN, dtype=jnp.int32)
    mod_start = lax.axis_index("head") * mod_cols
    for micro_idx in range(micro_count):
        lengths = clip_lengths[micro_idx]
        clip_tok = clip_ids(lengths, positions)
        clip_start = jnp.minimum(clip_tok[0], clip_count - clip_span)
        key_clip = clip_start + jnp.arange(clip_span * CTX, dtype=jnp.int32) // CTX
        mask_pad = jnp.pad(pad_mask[micro_idx], (WIN, WIN))
        ext_flag = lax.dynamic_slice_in_dim(mask_pad, first_row, row_count + 2 * WIN, 0)
        near_keys = window_mask(positions, ext_pos, ext_flag, lengths, frames)
        clip_keys = clip_tok[:, None] == key_clip[None, :]
        onehot = (clip_tok[:, None] == jnp.arange(clip_count, dtype=jnp.int32)[None, :]).astype(
            jnp.float32
        )
        mod_frames = jnp.dot(onehot, mod_all[micro_idx], precision=PRECISE)
        shifts = [mod_frames[:, 2 * which * D : (2 * which + 1) * D] for which in range(3)]
        scales = [mod_frames[:, (2 * which + 1) * D : (2 * which + 2) * D] for which in range(3)]
        resid_zero = x_in[micro_idx].astype(jnp.float32)
        normed_one, inverse_one = layer_norm(resid_zero)
        input_one = (normed_one * (1.0 + scales[0]) + shifts[0]).astype(jnp.bfloat16)
        proj_qkv = jnp.dot(input_one, w_qkv, preferred_element_type=jnp.float32).astype(
            jnp.bfloat16
        )
        kv_ext = padded(proj_qkv[:, head_cols:], (("seq", 0),), WIN)
        attended, log_one = attend(
            proj_qkv[:, :head_cols],
            kv_ext[:, :head_cols],
            kv_ext[:, head_cols:],
            near_keys,
            local_heads,
        )
        attended = attended.astype(jnp.bfloat16)
        resid_one = add_branch(
            resid_zero, jnp.dot(attended, w_out, preferred_element_type=jnp.float32)
        )
        normed_two, inverse_two = layer_norm(resid_one)
        input_two = (normed_two * (1.0 + scales[1]) + shifts[1]).astype(jnp.bfloat16)
        cross_query = jnp.dot(input_two, w_cq, preferred_element_type=jnp.float32).astype(
            jnp.bfloat16
        )
        ctx_rows = lax.dynamic_slice_in_dim(context[micro_idx], clip_start, clip_span, 0).reshape(
            clip_span * CTX, DC
        )
        cross_kv = jnp.dot(ctx_rows, w_ckv, preferred_element_type=jnp.float32).astype(jnp.bfloat16)
        cross_out, log_two = attend(
            cross_query, cross_kv[:, :head_cols], cross_kv[:, head_cols:], clip_keys, local_heads
        )
        cross_out = cross_out.astype(jnp.bfloat16)
        resid_two = add_branch(
            resid_one, jnp.dot(cross_out, w_cout, preferred_element_type=jnp.float32)
        )
        normed_three, inverse_three = layer_norm(resid_two)
        input_three = (normed_three * (1.0 + scales[2]) + shifts[2]).astype(jnp.bfloat16)
        gate_up = jnp.dot(input_three, w_glu, preferred_element_type=jnp.float32)
        gate_part = gate_up[:, :ff_cols]
        up_part = gate_up[:, ff_cols:]
        sigmoid_gate = jax.nn.sigmoid(gate_part)
        silu_gate = gate_part * sigmoid_gate
        hidden = (silu_gate * up_part).astype(jnp.bfloat16)
        resid_three = add_branch(
            resid_two, jnp.dot(hidden, w_down, preferred_element_type=jnp.float32)
        )
        outputs.append(resid_three.astype(jnp.bfloat16))
        grad_three = cotangent[micro_idx].astype(jnp.float32)
        grad_low = grad_three.astype(jnp.bfloat16)
        grads[6] = grads[6] + jnp.dot(hidden.T, grad_low, preferred_element_type=jnp.float32)
        grad_hidden = jnp.dot(grad_low, w_down.T, preferred_element_type=jnp.float32)
        grad_glu = jnp.concatenate(
            [
                grad_hidden * up_part * sigmoid_gate * (1.0 + gate_part * (1.0 - sigmoid_gate)),
                grad_hidden * silu_gate,
            ],
            axis=1,
        ).astype(jnp.bfloat16)
        grads[5] = grads[5] + jnp.dot(input_three.T, grad_glu, preferred_element_type=jnp.float32)
        grad_in_three = input_grad(jnp.dot(grad_glu, w_glu.T, preferred_element_type=jnp.float32))
        back_three, dscale_three, dshift_three = norm_back(
            grad_in_three, normed_three, inverse_three, scales[2]
        )
        grad_two = grad_three + back_three
        grad_low = grad_two.astype(jnp.bfloat16)
        grads[4] = grads[4] + jnp.dot(cross_out.T, grad_low, preferred_element_type=jnp.float32)
        grad_cross = jnp.dot(grad_low, w_cout.T, preferred_element_type=jnp.float32).astype(
            jnp.bfloat16
        )
        dquery_two, dkey_two, dvalue_two = attend_back(
            cross_query,
            cross_kv[:, :head_cols],
            cross_kv[:, head_cols:],
            clip_keys,
            log_two,
            grad_cross,
            local_heads,
        )
        dquery_two = dquery_two.astype(jnp.bfloat16)
        grads[2] = grads[2] + jnp.dot(input_two.T, dquery_two, preferred_element_type=jnp.float32)
        grads[3] = grads[3] + jnp.dot(
            ctx_rows.astype(jnp.float32).T,
            jnp.concatenate([dkey_two, dvalue_two], axis=1),
            precision=PRECISE,
        )
        grad_in_two = input_grad(jnp.dot(dquery_two, w_cq.T, preferred_element_type=jnp.float32))
        back_two, dscale_two, dshift_two = norm_back(
            grad_in_two, normed_two, inverse_two, scales[1]
        )
        grad_one = grad_two + back_two
        grad_low = grad_one.astype(jnp.bfloat16)
        grads[1] = grads[1] + jnp.dot(attended.T, grad_low, preferred_element_type=jnp.float32)
        grad_attended = jnp.dot(grad_low, w_out.T, preferred_element_type=jnp.float32).astype(
            jnp.bfloat16
        )
        dquery_one, dkey_ext, dvalue_ext = attend_back(
            proj_qkv[:, :head_cols],
            kv_ext[:, :head_cols],
            kv_ext[:, head_cols:],
            near_keys,
            log_one,
            grad_attended,
            local_heads,
        )
        dkv_ext = jnp.concatenate([dkey_ext, dvalue_ext], axis=1)
        rims = jnp.concatenate([dkv_ext[:WIN], dkv_ext[row_count + WIN :]], axis=0)
        returned = padded(rims.astype(jnp.bfloat16), (("seq", 0),), WIN).astype(rims.dtype)
        dkv_own = dkv_ext[WIN : row_count + WIN]
        dkv_own = dkv_own.at[:WIN].add(returned[:WIN])
        dkv_own = dkv_own.at[row_count - WIN :].add(returned[3 * WIN :])
        grad_qkv = jnp.concatenate([dquery_one, dkv_own], axis=1).astype(jnp.bfloat16)
        grads[0] = grads[0] + jnp.dot(input_one.T, grad_qkv, preferred_element_type=jnp.float32)
        grad_in_one = input_grad(jnp.dot(grad_qkv, w_qkv.T, preferred_element_type=jnp.float32))
        back_one, dscale_one, dshift_one = norm_back(
            grad_in_one, normed_one, inverse_one, scales[0]
        )
        input_grads.append(grad_one + back_one)
        dmod_frames = jnp.concatenate(
            [dshift_one, dscale_one, dshift_two, dscale_two, dshift_three, dscale_three], axis=1
        )
        dmod_clips = jnp.dot(onehot.T, dmod_frames, precision=PRECISE)
        dmod_own = lax.dynamic_slice_in_dim(dmod_clips, mod_start, mod_cols, 1)
        grads[7] = grads[7] + jnp.dot(
            cond[micro_idx].astype(jnp.float32).T, dmod_own, precision=PRECISE
        )
    grad_tiles = jnp.concatenate([piece.reshape(-1) for piece in grads]).reshape(-1, TS, TS)
    slot_buffer = (
        jnp.zeros((seq_count * capacity, TS, TS), jnp.float32).at[tile_place].set(grad_tiles)
    )
    summed = lax.psum_scatter(
        slot_buffer.astype(jnp.bfloat16), "seq", scatter_dimension=0, tiled=True
    ).astype(jnp.float32)
    own_slots = lax.axis_index("seq") * capacity + jnp.arange(capacity, dtype=jnp.int32)
    rate = slot_rates(slot_tile[own_slots], shapes)[:, None, None]
    weight, first, second = adam_step(master[0], first_moment[0], second_moment[0], summed, rate)
    return (jnp.stack(outputs), jnp.stack(input_grads), weight[None], first[None], second[None])


def solution(mesh):
    placed = (
        P(None, "seq", None),
        P(None, "seq", None),
        P(),
        P(),
        P(),
        P(),
        P("head", None),
        P("head", "seq", None, None),
        P("head", "seq", None, None),
        P("head", "seq", None, None),
    )
    return jax.shard_map(
        on_device,
        mesh=mesh,
        in_specs=placed,
        out_specs=(
            P(None, "seq", None),
            P(None, "seq", None),
            P("head", "seq", None, None),
            P("head", "seq", None, None),
            P("head", "seq", None, None),
        ),
        check_vma=False,
    )
```

profile of v0, /device:TPU:0, one launch (start us, length us, event | category | flops | bytes accessed | tf_op | source)
XLA Modules:
  0.0 3319.3 jit_solution(7722203618675523506)
XLA Ops:
  31.0 719.0 %all-gather.2.cloned.1.call-done = bf16[2256,128,128]{2,1,0:T(8,128)(2,1)} async-done(((bf16[141,128,128]{2,1,0:T(8,128)(2,1)}), bf16[2256,128,128]{2,1,0:T(8,128)(2,1)}) %all-gather.2.cloned.1.call-update) | async-done | bytes 73924624 | tf_op jit(solution)/shard_map/all_gather | solution.py:233
  750.0 46.8 %gather_fusion = bf16[1800,128,128]{2,1,0:T(8,128)(2,1)} fusion(bf16[2256,128,128]{2,1,0:T(8,128)(2,1)} %all-gather.2.cloned.1.call-done, s32[2048]{0:T(1024)S(1)} %pad_clamp_fusion), kind=kCustom, calls=%fused_computation | custom fusion | bytes 117972000 | tf_op jit(solution)/shard_map/gather | solution.py:236
  796.8 9.0 slice.401
  805.8 13.1 slice.397
  818.9 13.8 reshape.882
  832.8 25.0 reshape.880
  857.8 7.0 fusion.5
  963.1 11.6 slice.421
  974.7 16.9 slice.418
  991.6 17.9 reshape.895
  1009.5 26.6 reshape.894
  1042.7 9.6 fusion.228
  1058.8 10.0 convolution_convert_fusion.7
  1069.1 17.2 all-reduce.17.cloned.1.call-done
  1103.1 20.5 all-reduce.19.cloned.1.call-done
  1147.0 14.2 collective-permute-done.6
  1172.6 14.2 all-reduce.21.cloned.1.call-done
  1202.9 15.5 collective-permute-done
  1254.6 9.5 reduce-scatter.12.cloned.1.call-done
  1271.8 9.6 fusion.227
  1287.8 10.0 convolution_convert_fusion.10
  1298.5 19.7 all-reduce.11.cloned.1.call-done
  1337.1 20.1 all-reduce.13.cloned.1.call-done
  1381.0 14.6 collective-permute-done.4
  1402.1 7.2 convolution_convert_fusion.11
  1420.9 7.6 fusion.149
  1428.6 15.0 fusion.55
  1443.6 8.0 fusion.110
  1451.6 28.4 add_bitcast_fusion
  1479.9 12.6 convolution_add_fusion.1
  1492.6 20.0 reshape.925
  1512.5 33.7 %copy.111 = f32[192,48,8,128]{3,1,2,0:T(8,128)} copy(f32[192,48,8,128]{3,2,1,0:T(8,128)} %add_bitcast_fusion) | data formatting | bytes 75497472
  1612.4 7.1 convolution_add_fusion
  1619.5 15.2 reshape.915
  1634.7 10.4 constant_dynamic-update-slice_fusion
  1657.3 30.5 constant_dynamic-update-slice_fusion.3
  1687.8 6.9 constant_dynamic-update-slice_fusion.2
  1705.6 14.8 fusion.147
  1720.5 25.8 add_bitcast_fusion.1
  1746.2 27.7 copy.107
  1774.0 27.7 reshape.926
  1801.7 19.7 constant_dynamic-update-slice_fusion.1
  1821.4 45.4 %broadcast_in_dim.75 = f32[2256,128,128]{2,1,0:T(8,128)} broadcast(f32[]{:T(128)} %constant.213.clone.1), dimensions={} | broadcast | bytes 147849216 | tf_op jit(solution)/shard_map/broadcast_in_dim | solution.py:392
  1866.8 323.1 %scatter_fusion = f32[2256,128,128]{2,1,0:T(8,128)} fusion(f32[2256,128,128]{2,1,0:T(8,128)} %broadcast_in_dim.75, s32[1800]{0:T(1024)S(1)} %copy-done.159, f32[1800,128,128]{2,1,0:T(8,128)} %bitcast.86), kind=kCustom, calls=%fused_computation.3 | custom fusion | bytes 353901600 | tf_op jit(solution)/shard_map/scatter | solution.py:392
  2189.9 70.9 %convert_element_type.629 = bf16[2256,128,128]{2,1,0:T(8,128)(2,1)} convert(f32[2256,128,128]{2,1,0:T(8,128)} %scatter_fusion) | non-fusion elementwise | flops 36962304 | bytes 221773824 | tf_op jit(solution)/shard_map/convert_element_type | solution.py:395
  2260.8 10.0 scatter_custom_fusion
  2283.0 1002.2 %reduce-scatter.22.cloned.1.call-done = bf16[141,128,128]{2,1,0:T(8,128)(2,1)} async-done(((bf16[2256,128,128]{2,1,0:T(8,128)(2,1)}), bf16[141,128,128]{2,1,0:T(8,128)(2,1)}) %reduce-scatter.22.cloned.1.call-update) | async-done | bytes 4620304
  3285.2 27.1 fusion.9
  (790 shorter events, 411.9 us)
Async XLA Ops:
  7.2 742.8 %all-gather.2.cloned.1.call-start = ((), (), s32[]{:S(2)}) async-start(), calls=%async_computation.7 | async-start | bytes 78544896 | tf_op jit(solution)/shard_map/all_gather | solution.py:233
  14.2 929.7 %reduce-scatter.16.cloned.1.call-start = ((), (), s32[]{:S(2)}) async-start(), calls=%async_computation.11 | async-start | bytes 1179648 | tf_op jit(solution)/shard_map/reduce_scatter | solution.py:186
  15.3 851.7 %copy-start.163 = (s32[256]{0:T(256)}, s32[256]{0:T(256)S(1)}, u32[]{:S(2)}) copy-start(s32[256]{0:T(256)S(1)} %get-tuple-element.71) | copy-start | bytes 3076
  24.8 844.3 %copy-start.177 = (f32[256]{0:T(256)}, f32[256]{0:T(256)S(1)}, u32[]{:S(2)}) copy-start(f32[256]{0:T(256)S(1)} %broadcast_multiply_fusion.12) | copy-start | bytes 3076
  25.2 844.0 %copy-start.181 = (f32[256]{0:T(256)}, f32[256]{0:T(256)S(1)}, u32[]{:S(2)}) copy-start(f32[256]{0:T(256)S(1)} %add_rsqrt_fusion) | copy-start | bytes 3076
  832.8 25.0 copy-start.149
  877.7 20.8 collective-permute-start.2
  881.1 19.3 collective-permute-start.3
  916.9 119.3 %reduce-scatter.18.cloned.1.call-start = ((), (), s32[]{:S(2)}) async-start(), calls=%async_computation.12 | async-start | bytes 1179648 | tf_op jit(solution)/shard_map/reduce_scatter | solution.py:186
  927.6 163.3 %copy-start.9 = (bf16[768,1536]{1,0:T(8,128)(2,1)}, bf16[768,1536]{1,0:T(8,128)(2,1)S(1)}, u32[]{:S(2)}) copy-start(bf16[768,1536]{1,0:T(8,128)(2,1)S(1)} %reshape.893) | copy-start | bytes 7077892
  947.6 88.5 %copy-start.21 = (bf16[256,1536]{1,0:T(8,128)(2,1)}, bf16[256,1536]{1,0:T(8,128)(2,1)S(1)}, u32[]{:S(2)}) copy-start(bf16[256,1536]{1,0:T(8,128)(2,1)S(1)} %all_gather.29) | copy-start | bytes 2359300
  962.9 123.5 %all-reduce.17.cloned.1.call-start = ((), (), s32[]{:S(2)}) async-start(), calls=%async_computation.17 | async-start | bytes 1572864 | tf_op jit(solution)/shard_map/psum | solution.py:195
  1039.6 49.1 %copy-start.15 = (bf16[256,1536]{1,0:T(8,128)(2,1)}, bf16[256,1536]{1,0:T(8,128)(2,1)S(1)}, u32[]{:S(2)}) copy-start(bf16[256,1536]{1,0:T(8,128)(2,1)S(1)} %all_gather.30) | copy-start | bytes 2359300
  1039.8 48.9 %copy-start.188 = (bf16[256]{0:T(256)(128)(2,1)}, bf16[256]{0:T(256)(128)(2,1)S(1)}, u32[]{:S(2)}) copy-start(bf16[256]{0:T(256)(128)(2,1)S(1)} %multiply_convert_fusion.11) | copy-start | bytes 1540
  1040.2 48.5 %copy-start.183 = (bf16[256]{0:T(256)(128)(2,1)}, bf16[256]{0:T(256)(128)(2,1)S(1)}, u32[]{:S(2)}) copy-start(bf16[256]{0:T(256)(128)(2,1)S(1)} %get-tuple-element.79) | copy-start | bytes 1540
  1068.8 54.8 %all-reduce.19.cloned.1.call-start = ((), (), s32[]{:S(2)}) async-start(), calls=%async_computation.18 | async-start | bytes 1572864 | tf_op jit(solution)/shard_map/psum | solution.py:195
  1069.1 28.0 copy-start.151
  1098.6 25.0 copy-start.22
  1098.6 25.0 copy-start.194
  1098.6 25.0 copy-start.200
  1103.0 83.7 %all-reduce.21.cloned.1.call-start = ((), (), s32[]{:S(2)}) async-start(), calls=%async_computation.19 | async-start | bytes 1572864 | tf_op jit(solution)/shard_map/psum | solution.py:195
  1140.1 21.0 collective-permute-start.6
  1144.0 19.2 collective-permute-start.7
  1167.4 70.4 %reduce-scatter.10.cloned.1.call-start = ((), (), s32[]{:S(2)}) async-start(), calls=%async_computation.8 | async-start | bytes 1179648 | tf_op jit(solution)/shard_map/reduce_scatter | solution.py:186
  1197.5 20.9 collective-permute-start
  1201.2 19.1 collective-permute-start.1
  1229.4 34.7 %reduce-scatter.12.cloned.1.call-start = ((), (), s32[]{:S(2)}) async-start(), calls=%async_computation.9 | async-start | bytes 1179648 | tf_op jit(solution)/shard_map/reduce_scatter | solution.py:186
  1254.5 63.8 %all-reduce.11.cloned.1.call-start = ((), (), s32[]{:S(2)}) async-start(), calls=%async_computation.14 | async-start | bytes 1572864 | tf_op jit(solution)/shard_map/psum | solution.py:195
  1267.7 52.9 %copy-start.18 = (bf16[256,1536]{1,0:T(8,128)(2,1)}, bf16[256,1536]{1,0:T(8,128)(2,1)S(1)}, u32[]{:S(2)}) copy-start(bf16[256,1536]{1,0:T(8,128)(2,1)S(1)} %all_gather.27) | copy-start | bytes 2359300
  1297.7 59.5 %all-reduce.13.cloned.1.call-start = ((), (), s32[]{:S(2)}) async-start(), calls=%async_computation.15 | async-start | bytes 1572864 | tf_op jit(solution)/shard_map/psum | solution.py:195
  1333.7 25.8 copy-start.131
  1336.6 358.1 %all-reduce.15.cloned.1.call-start = ((), (), s32[]{:S(2)}) async-start(), calls=%async_computation.16 | async-start | bytes 1572864 | tf_op jit(solution)/shard_map/psum | solution.py:195
  1374.6 21.0 collective-permute-start.4
  1378.4 19.1 collective-permute-start.5
  1401.8 870.7 %reduce-scatter.20.cloned.1.call-start = ((), (), s32[]{:S(2)}) async-start(), calls=%async_computation.13 | async-start | bytes 1179648 | tf_op jit(solution)/shard_map/reduce_scatter | solution.py:186
  1409.3 866.8 %reduce-scatter.14.cloned.1.call-start = ((), (), s32[]{:S(2)}) async-start(), calls=%async_computation.10 | async-start | bytes 1179648 | tf_op jit(solution)/shard_map/reduce_scatter | solution.py:186
  1492.6 53.7 %slice-start.25 = ((s8[9437184]{0:T(1024)(128)(4,1)}), s8[1048576]{0:T(1024)(128)(4,1)S(1)}, s32[]{:S(2)}) async-start(s8[9437184]{0:T(1024)(128)(4,1)} %bitcast.335), calls=%async_computation.46 | async-start | bytes 2097152
  1512.5 33.7 %slice-start.26 = ((s8[9437184]{0:T(1024)(128)(4,1)}), s8[4194304]{0:T(1024)(128)(4,1)S(1)}, s32[]{:S(2)}) async-start(s8[9437184]{0:T(1024)(128)(4,1)} %bitcast.335), calls=%async_computation.47 | async-start | bytes 8388608
  1512.5 33.7 %slice-start.27 = ((s8[9437184]{0:T(1024)(128)(4,1)}), s8[4194304]{0:T(1024)(128)(4,1)S(1)}, s32[]{:S(2)}) async-start(s8[9437184]{0:T(1024)(128)(4,1)} %bitcast.335), calls=%async_computation.48 | async-start | bytes 8388608
  1512.5 33.7 %copy-start.144 = (bf16[256,3072]{1,0:T(8,128)(2,1)S(1)}, bf16[256,3072]{1,0:T(8,128)(2,1)}, u32[]{:S(2)}) copy-start(bf16[256,3072]{1,0:T(8,128)(2,1)} %get-tuple-element.91) | copy-start | bytes 4718596
  1549.8 1735.4 %reduce-scatter.22.cloned.1.call-start = ((), (), s32[]{:S(2)}) async-start(), calls=%async_computation.20 | async-start | bytes 78544896
  1619.5 30.0 slice-start.17
  1654.7 33.0 slice-start.4
  1657.3 30.5 slice-start.5
  1657.3 30.5 slice-start.6
  1657.3 30.5 slice-start.7
  1657.3 30.5 slice-start.8
  1821.4 45.4 %copy-start.159 = (s32[1800]{0:T(1024)S(1)}, s32[1800]{0:T(1024)}, u32[]{:S(2)}) copy-start(s32[1800]{0:T(1024)} %copy-done.158) | copy-start | bytes 21604
  (222 other events, 1324.7 us)
Sparse Core Ops, SparseCore 0:
  14.3 735.6 all-gather.1
  917.0 6.4 reduce-scatter.15
  963.0 6.4 reduce-scatter.17
  1068.9 17.3 all-reduce.16
  1103.2 20.3 all-reduce.18
  1167.5 19.1 all-reduce.20
  1229.5 8.2 reduce-scatter.9
  1254.6 9.4 reduce-scatter.11
  1297.9 20.3 all-reduce.10
  1336.8 20.3 all-reduce.12
  1401.9 19.2 all-reduce.14
  1423.3 9.4 reduce-scatter.19
  1549.9 8.3 reduce-scatter.13
  2260.9 1024.2 reduce-scatter.21
where the time goes:
time: 3340 us; the launch traced here: 3320 us
  waiting for transfers between devices  1880 us (56%)
  local copies, waits for them, and re-layouts  874 us (26%)
  matrix products  312 us (9%)
  other arithmetic  195 us (6%)
    unnamed x15, waiting for transfers between devices  1000 us
    all_gather x1, waiting for transfers between devices, on_device(): lax.all_gather(master[0].astype(jnp.bfloat16), 'seq', axis=0, tiled=True)  719 us
    scatter x1, local copies, waits for them, and re-layouts, on_device(): jnp.zeros((seq_count * capacity, TS, TS), jnp.float32).at[tile_place]  323 us
    unnamed x503, local copies, waits for them, and re-layouts  125 us
    reshape x8, local copies, waits for them, and re-layouts, split_pieces(): flattened[offset:offset + row_count * col_count]  104 us
    psum x6, waiting for transfers between devices, input_grad(): lax.psum(partial_value.astype(jnp.bfloat16), 'head').astype(jnp.float32)  91.7 us
    reshape x7, local copies, waits for them, and re-layouts, on_device(): piece.reshape(-1)  85.9 us
    convert_element_type x1, other arithmetic, on_device(): slot_buffer.astype(jnp.bfloat16)  70.9 us
  transfers between devices with their start and end apart: 22, of which 17 were waited for; matrix products, arithmetic and copies ran while one was open for 31% of the time, Pallas kernels for 0%

commit v1 on v0

v1 whole, which is shorter than its diff:
```python
import math
from functools import partial

import jax
import jax.numpy as jnp
import numpy as np
from jax import lax
from jax.experimental import pallas as pl
from jax.experimental.pallas import tpu as pltpu
from jax.sharding import PartitionSpec as P

D = 1536
HD = 64
FF = 6144
DC = 768
CTX = 128
WIN = 128
TS = 128
STEP = 5
MINLEN = 204


PRECISE = lax.Precision.HIGHEST
EPS_NORM = 1e-06
BETA_ONE = 0.9
BETA_TWO = 0.95
ADAM_EPS = 1e-08
WEIGHT_DECAY = 0.1
LEARN_RATE = 0.5
MASKED = -1e30


def padded(shard, sides, width):
    for axis, dim in sides:
        size, length = (lax.axis_size(axis), shard.shape[dim])
        up = [(i, (i + 1) % size) for i in range(size - 1)]
        down = [(j, i) for i, j in up]
        last = lax.slice_in_dim(shard, length - width, length, axis=dim)
        initial = lax.slice_in_dim(shard, 0, width, axis=dim)
        before = lax.ppermute(last, axis, up)
        after = lax.ppermute(initial, axis, down)
        shard = jnp.concatenate([before, shard, after], axis=dim)
    return shard


def piece_shapes(head_count):
    head_cols = D // head_count
    ff_cols = FF // head_count
    return [
        (D, 3 * head_cols),
        (head_cols, D),
        (D, head_cols),
        (DC, 2 * head_cols),
        (head_cols, D),
        (D, 2 * ff_cols),
        (ff_cols, D),
        (D, 6 * D // head_count),
    ]


def fan_inputs():
    return [D, D // 64, D, DC, D // 32, D, FF // 4, 4 * D]


def slot_rates(slot_tile, shapes):
    counts = [row_count * col_count // (TS * TS) for row_count, col_count in shapes]
    kind_ends = jnp.array([int(end_value) for end_value in np.cumsum(counts)[:-1]], dtype=jnp.int32)
    slot_kind = jnp.sum((slot_tile[:, None] >= kind_ends[None, :]).astype(jnp.int32), axis=1)
    rate_table = jnp.array(
        [LEARN_RATE * fan_in ** (-0.5) for fan_in in fan_inputs()], dtype=jnp.float32
    )
    onehot = (slot_kind[:, None] == jnp.arange(len(shapes), dtype=jnp.int32)[None, :]).astype(
        jnp.float32
    )
    return jnp.sum(onehot * rate_table[None, :], axis=1)


def split_pieces(flattened, shapes):
    pieces = []
    offset = 0
    for row_count, col_count in shapes:
        pieces.append(
            flattened[offset : offset + row_count * col_count].reshape(row_count, col_count)
        )
        offset = offset + row_count * col_count
    return pieces


def layer_norm(values):
    centred = values - jnp.mean(values, axis=-1, keepdims=True)
    inverse = lax.rsqrt(jnp.mean(centred * centred, axis=-1, keepdims=True) + EPS_NORM)
    return (centred * inverse, inverse)


def norm_back(grad, normed, inverse, scale_part):
    dnormed = grad * (1.0 + scale_part)
    dvalues = inverse * (
        dnormed
        - jnp.mean(dnormed, axis=-1, keepdims=True)
        - normed * jnp.mean(dnormed * normed, axis=-1, keepdims=True)
    )
    return (dvalues, grad * normed, grad)


def clip_ids(lengths, positions):
    clip_ends = jnp.cumsum(lengths)
    return jnp.sum((positions[:, None] >= clip_ends[None, :]).astype(jnp.int32), axis=1)


def window_mask(query_pos, key_pos, key_flag, lengths, frames):
    query_clip = clip_ids(lengths, query_pos)
    key_clip = clip_ids(lengths, key_pos)
    offset = key_pos[None, :] - query_pos[:, None]
    is_near = (offset <= WIN) & (offset >= -WIN)
    is_inside = (key_pos >= 0) & (key_pos < frames)
    same_clip = query_clip[:, None] == key_clip[None, :]
    is_kept = (key_flag[None, :] == 1) | (offset == 0)
    return is_near & is_inside[None, :] & same_clip & is_kept


def adam_step(weight, first, second, grads, rate):
    first = BETA_ONE * first + (1.0 - BETA_ONE) * grads
    second = BETA_TWO * second + (1.0 - BETA_TWO) * grads * grads
    first_hat = first / (1.0 - BETA_ONE**STEP)
    second_hat = second / (1.0 - BETA_TWO**STEP)
    weight = weight - rate * (first_hat / (jnp.sqrt(second_hat) + ADAM_EPS) + WEIGHT_DECAY * weight)
    return (weight, first, second)


VMEM_BYTES = 48 * 1024 * 1024


def step_tiles(tile_count, col_count, offset=0):
    chunks = col_count // TS
    common = math.gcd(chunks, TS)
    group_tiles, group_rows = chunks // common, TS // common
    groups = tile_count // group_tiles
    best = 1
    for size in range(1, groups + 1):
        if groups % size or offset % (size * group_tiles) or (size * group_rows) % 16:
            continue
        best = size
        if size * group_tiles >= 24:
            break
    return best * group_tiles, best * group_rows


def fetch_matrix(sources, source_at, index_at, row_count, col_count):
    tile_count = row_count * col_count // (TS * TS)
    if col_count % TS:
        starts = np.cumsum([0] + [source.shape[0] for source in sources])
        index_at = index_at + jnp.array(starts[:-1], jnp.int32)[source_at]
        return jnp.concatenate(sources, axis=0)[index_at].reshape(row_count, col_count)
    chunks = col_count // TS
    tiles, rows = step_tiles(tile_count, col_count)
    steps = tile_count // tiles
    source_count = len(sources)

    def kernel(source_ref, index_ref, *refs):
        sources_in, out, land, wide, sems = refs[:source_count], *refs[source_count:]
        step = pl.program_id(0)

        def begin(which, slot):
            def one(tile, carry):
                at = which * tiles + tile
                source, index = source_ref[at], index_ref[at]

                def copy(low, high):
                    if high - low == 1:
                        pltpu.make_async_copy(
                            sources_in[low].at[index], land.at[slot, tile], sems.at[slot]
                        ).start()
                        return
                    middle = (low + high) // 2
                    pl.when(source < middle)(partial(copy, low, middle))
                    pl.when(source >= middle)(partial(copy, middle, high))

                copy(0, source_count)
                return carry

            lax.fori_loop(0, tiles, one, 0)

        @pl.when(step == 0)
        def _():
            begin(0, 0)

        @pl.when(step + 1 < steps)
        def _():
            begin(step + 1, lax.rem(step + 1, 2))

        slot = lax.rem(step, 2)
        pltpu.make_async_copy(land.at[slot], land.at[slot], sems.at[slot]).wait()
        wide[...] = land[slot].astype(jnp.float32).reshape(tiles * TS, TS)
        for chunk in range(chunks):
            out[:, chunk * TS : (chunk + 1) * TS] = wide[
                pl.ds(chunk, rows, stride=chunks), :
            ].astype(jnp.bfloat16)

    return pl.pallas_call(
        kernel,
        out_shape=jax.ShapeDtypeStruct((row_count, col_count), jnp.bfloat16),
        grid_spec=pltpu.PrefetchScalarGridSpec(
            num_scalar_prefetch=2,
            grid=(steps,),
            in_specs=[pl.BlockSpec(memory_space=pl.ANY)] * source_count,
            out_specs=pl.BlockSpec((rows, col_count), lambda i, *_: (i, 0)),
            scratch_shapes=[
                pltpu.VMEM((2, tiles, TS, TS), jnp.bfloat16),
                pltpu.VMEM((tiles * TS, TS), jnp.float32),
                pltpu.SemaphoreType.DMA((2,)),
            ],
        ),
        compiler_params=pltpu.CompilerParams(
            dimension_semantics=("arbitrary",), vmem_limit_bytes=VMEM_BYTES
        ),
        cost_estimate=pl.CostEstimate(
            flops=0, bytes_accessed=4 * row_count * col_count, transcendentals=0
        ),
        name="fetch_matrix",
    )(source_at, index_at, *sources)


def as_tiles(grad, into, offset):
    row_count, col_count = grad.shape
    grad = grad.astype(jnp.bfloat16)
    tile_count = row_count * col_count // (TS * TS)
    if col_count % TS:
        cut = grad.reshape(-1, TS, TS)
        if isinstance(into, int):
            into = jnp.zeros((into, TS, TS), jnp.bfloat16)
        return lax.dynamic_update_slice_in_dim(into, cut, offset, 0)
    chunks = col_count // TS
    tiles, rows = step_tiles(tile_count, col_count, offset)
    is_new = isinstance(into, int)

    def kernel(grad_ref, *refs):
        out, wide = refs[-2:]
        for chunk in range(chunks):
            wide[pl.ds(chunk, rows, stride=chunks), :] = grad_ref[
                :, chunk * TS : (chunk + 1) * TS
            ].astype(jnp.float32)
        out[...] = wide[...].reshape(tiles, TS, TS).astype(jnp.bfloat16)

    in_specs = [pl.BlockSpec((rows, col_count), lambda i: (i, 0))]
    return pl.pallas_call(
        kernel,
        out_shape=jax.ShapeDtypeStruct((into if is_new else into.shape[0], TS, TS), jnp.bfloat16),
        grid=(tile_count // tiles,),
        in_specs=in_specs if is_new else in_specs + [pl.BlockSpec(memory_space=pl.ANY)],
        out_specs=pl.BlockSpec((tiles, TS, TS), lambda i: (offset // tiles + i, 0, 0)),
        scratch_shapes=[pltpu.VMEM((tiles * TS, TS), jnp.float32)],
        input_output_aliases={} if is_new else {1: 0},
        compiler_params=pltpu.CompilerParams(
            dimension_semantics=("arbitrary",), vmem_limit_bytes=VMEM_BYTES
        ),
        cost_estimate=pl.CostEstimate(
            flops=0, bytes_accessed=4 * row_count * col_count, transcendentals=0
        ),
        name="as_tiles",
    )(*((grad,) if is_new else (grad, into)))


def ring_sizes(seq_count):
    return (4, seq_count // 8, 2)


def ring_send(block, sizes, dim):
    inner = math.prod(sizes[dim + 1 :])
    pairs = []
    for device in range(math.prod(sizes)):
        at = device // inner % sizes[dim]
        pairs.append((device, device + ((at + 1) % sizes[dim] - at) * inner))
    return lax.ppermute(block, "seq", pairs)


def nothing(*arrays):
    heads = [array.reshape(-1)[0] for array in arrays]
    return sum((head != head).astype(jnp.int32) for head in heads)


def sum_ticks(values, sizes):
    for dim, size in enumerate(sizes):
        moving = values
        for _ in range(size - 1):
            (moving,) = yield [ring_send(moving, sizes, dim)]
            values = values + moving
    return values


def added(left, right):
    return (left.astype(jnp.float32) + right.astype(jnp.float32)).astype(jnp.bfloat16)


def ring(parts, sizes, dim):
    moving = parts[1]
    for step in range(1, sizes[dim]):
        (came,) = yield [ring_send(moving, sizes, dim)]
        here = parts[(step + 1) % sizes[dim]]
        if step + 1 < sizes[dim]:
            moving = added(came, here)
    return came, here


def gather_ticks(block, sizes, order):
    parts = [block]
    for number, dim in enumerate(order):
        for _ in range(sizes[dim] - 1):
            parts += yield [ring_send(parts[-1], sizes, dim)]
        if number < 2:
            parts = [jnp.concatenate(parts, axis=0)]
    return parts


def scatter_ticks(terms, sizes, order):
    parts = [terms(step) for step in range(sizes[order[0]])]
    for number, dim in enumerate(order):
        came, here = yield from ring(parts, sizes, dim)
        if number < 2:
            parts = [added(came[at], here[at]) for at in range(sizes[order[number + 1]])]
    return added(came, here)


def together(*several):
    moving = [next(one) for one in several]
    results = [None] * len(several)
    while any(blocks is not None for blocks in moving):
        came = yield [block for blocks in moving if blocks is not None for block in blocks]
        for number, one in enumerate(several):
            if moving[number] is None:
                continue
            count = len(moving[number])
            mine, came = came[:count], came[count:]
            try:
                moving[number] = one.send(mine)
            except StopIteration as done:
                moving[number], results[number] = None, done.value
    return results


def gather_plane(block, sizes, order):
    parts = [block]
    for _ in range(sizes[order[0]] - 1):
        parts += yield [ring_send(parts[-1], sizes, order[0])]
    width = len(parts)
    for _ in range(sizes[order[1]] - 1):
        for part in parts[-width:]:
            parts = parts + (yield [ring_send(part, sizes, order[1])])
    return parts


def gather_pair(parts, width, sizes):
    while len(parts) < sizes[0]:
        parts += yield [ring_send(parts[-1], sizes, 0)]
    return (
        yield from together(
            gather_plane(jnp.concatenate([part[:width] for part in parts]), sizes, (1, 2)),
            gather_plane(jnp.concatenate([part[width:] for part in parts]), sizes, (2, 1)),
        )
    )


def scatter_plane(terms, sizes, order):
    first, second = order
    sums = [None] * sizes[second]
    for at in [*range(1, sizes[second]), 0]:
        sums[at] = added(
            *(yield from ring([terms(step, at) for step in range(sizes[first])], sizes, first))
        )
    return (yield from ring(sums, sizes, second))


def scatter_pair(terms, other_terms, sizes):
    left, right = yield from together(
        scatter_plane(terms, sizes, (2, 1)), scatter_plane(other_terms, sizes, (1, 2))
    )
    parts = [
        jnp.concatenate([added(came[at], here[at]) for came, here in (left, right)])
        for at in range(sizes[0])
    ]
    return added(*(yield from ring(parts, sizes, 0)))


class Ticks:
    def __init__(self):
        self.running = {}
        self.moving = {}
        self.results = {}

    def start(self, name, one):
        self.running[name] = one
        self.moving[name] = next(one)

    def tick(self, names, *others):
        names = [name for name in names if name in self.running]
        came = [self.moving[name] for name in names]
        if others:
            came, others = lax.optimization_barrier((came, others))
        for name, blocks in zip(names, came):
            try:
                self.moving[name] = self.running[name].send(blocks)
            except StopIteration as done:
                self.results[name] = done.value
                del self.running[name]
        return others[0] if len(others) == 1 else others

    def finish(self, names):
        while any(name in self.running for name in names):
            self.tick(names)
        return [self.results[name] for name in names]


GATHER_WIDE = (42, 34)


def portions(first, last, percent):
    wide = (percent * (last - first) + 50) // 100
    return first, min(first + wide, last), min(first + 2 * wide, last), last


def first_slots(tile_count, seq_count, capacity, percent):
    return min(capacity, -(-tile_count * percent // (100 * seq_count)))


def head_sum(partial_value):
    rounded = lax.optimization_barrier(partial_value.astype(jnp.bfloat16))
    if lax.axis_size("head") == 2:
        other = lax.ppermute(rounded, "head", [(0, 1), (1, 0)])
        return rounded.astype(jnp.float32) + other.astype(jnp.float32)
    return lax.psum(rounded, "head").astype(jnp.float32)


def adam_block(capacity):
    return max(size for size in (1, 2, 3, 4) if capacity % size == 0)


def first_pass_slot(cut_one, capacity):
    per = adam_block(capacity)
    return cut_one * 3 // 2 // per * per


def slot_cuts(seq_count, capacity, head_count, compact):
    shapes = piece_shapes(head_count)
    counts = [row_count * col_count // (TS * TS) for row_count, col_count in shapes]
    attn_tiles = sum(counts[:5])
    sent_tiles = sum(counts[:7])
    cut_one = first_slots(attn_tiles, seq_count, capacity, 126) if compact else capacity
    cut_two = first_slots(sent_tiles, seq_count, capacity, 112) if compact else capacity
    spare = (seq_count, 2 * seq_count) if compact else (0, 0)
    return attn_tiles, sent_tiles, cut_one, cut_two, spare


def layout_plan(owner_row, seq_count, capacity, head_count):
    attn_tiles, sent_tiles, cut_one, cut_two, spare = slot_cuts(
        seq_count, capacity, head_count, True
    )
    tile_count = owner_row.shape[0]
    tile_ids = jnp.arange(tile_count, dtype=jnp.int32)
    onehot = (owner_row[:, None] == jnp.arange(seq_count, dtype=jnp.int32)[None, :]).astype(
        jnp.int32
    )
    before = jnp.cumsum(onehot, axis=0) - onehot
    rank = jnp.sum(before * onehot, axis=1)
    is_attn = tile_ids < attn_tiles
    is_sent = tile_ids < sent_tiles
    over = [is_attn & (rank >= cut_one), is_sent & ~is_attn & (rank >= cut_two)]
    over_place = [jnp.cumsum(which.astype(jnp.int32)) - 1 for which in over]
    fits = (
        (jnp.sum(over[0].astype(jnp.int32)) <= spare[0])
        & (jnp.sum(over[1].astype(jnp.int32)) <= spare[1])
        & (jnp.max(jnp.where(is_attn, rank, 0)) < first_pass_slot(cut_one, capacity))
    )
    return (
        fits,
        rank,
        over[0] | over[1],
        jnp.where(over[0], over_place[0], spare[0] + over_place[1]),
    )


def listed_tiles(owner_row, rank, devices, cut):
    tile_ids = jnp.arange(owner_row.shape[0], dtype=jnp.float32)
    by_owner = (owner_row[None, :] == devices[:, None]).astype(jnp.float32)
    by_rank = (rank[:, None] == jnp.arange(cut, dtype=jnp.int32)[None, :]).astype(jnp.float32)
    return jnp.dot(by_owner * tile_ids[None, :], by_rank, precision=PRECISE).astype(jnp.int32)


def tile_factors(local, cond_ref, spread_ref, chunk_ref):
    conds, width = spread_ref.shape
    chunks = width // conds
    start = local * TS
    top = start // chunks
    place = start - top * chunks + lax.broadcasted_iota(jnp.int32, (TS, 1), 0)
    row_at = jnp.zeros((TS, 1), jnp.int32)
    for later in range(1, (TS + chunks - 2) // chunks + 1):
        row_at += (place >= later * chunks).astype(jnp.int32)
    chunk_at = place - row_at * chunks
    rows = 8 * ((TS + chunks - 2) // chunks // 8 + 1)
    picked = cond_ref[pl.ds(top, rows), :].astype(jnp.bfloat16)
    select = (row_at == lax.broadcasted_iota(jnp.int32, (TS, rows), 1)).astype(jnp.bfloat16)
    factor = jnp.dot(select, picked, preferred_element_type=jnp.float32).astype(jnp.bfloat16)
    wide = jnp.dot(factor, spread_ref[...], preferred_element_type=jnp.float32)
    return jnp.where(chunk_at == chunk_ref[...], wide, 0.0).astype(jnp.bfloat16)


def factor_tables(cond_rows, mod_cols):
    conds, chunks = cond_rows.shape[0], mod_cols // TS
    rows = 8 * ((TS + chunks - 2) // chunks // 8 + 1)
    columns = np.arange(conds * chunks)
    spread = (columns[None, :] % conds == np.arange(conds)[:, None]).astype(np.float32)
    return (
        jnp.pad(cond_rows.T.astype(jnp.float32), ((0, rows), (0, 0))),
        jnp.array(spread, jnp.bfloat16),
        jnp.array(columns[None, :] // conds, jnp.int32),
    )


def mod_product(tables, master, first_slot, slot_count, local):
    width = tables[1].shape[1]

    def kernel(meta_ref, local_ref, cond_ref, spread_ref, chunk_ref, master_ref, out, land, sems):
        first, count = meta_ref[0], meta_ref[1]

        def tile_copy(at):
            slot = lax.rem(at, 2)
            return pltpu.make_async_copy(master_ref.at[first + at], land.at[slot], sems.at[slot])

        out[...] = jnp.zeros_like(out)

        @pl.when(count > 0)
        def _():
            tile_copy(0).start()

        def one(at, carry):
            @pl.when(at + 1 < count)
            def _():
                tile_copy(at + 1).start()

            tile_copy(at).wait()
            factors = tile_factors(local_ref[first + at], cond_ref, spread_ref, chunk_ref)
            out[...] += lax.dot_general(
                factors,
                land[lax.rem(at, 2)].astype(jnp.bfloat16),
                (((0,), (0,)), ((), ())),
                preferred_element_type=jnp.float32,
            )
            return carry

        lax.fori_loop(0, count, one, 0)

    whole = pl.BlockSpec(memory_space=pltpu.VMEM)
    return pl.pallas_call(
        kernel,
        out_shape=jax.ShapeDtypeStruct((width, TS), jnp.float32),
        grid_spec=pltpu.PrefetchScalarGridSpec(
            num_scalar_prefetch=2,
            grid=(1,),
            in_specs=[whole, whole, whole, pl.BlockSpec(memory_space=pl.ANY)],
            out_specs=whole,
            scratch_shapes=[pltpu.VMEM((2, TS, TS), jnp.float32), pltpu.SemaphoreType.DMA((2,))],
        ),
        compiler_params=pltpu.CompilerParams(
            dimension_semantics=("arbitrary",), vmem_limit_bytes=VMEM_BYTES
        ),
        cost_estimate=pl.CostEstimate(
            flops=80 * width * TS * TS, bytes_accessed=40 * 4 * TS * TS, transcendentals=0
        ),
        name="mod_product",
    )(jnp.stack([first_slot, slot_count]), local, *tables, master)


def adam_slots(
    begin, end, into, tables, dmod, local, kind_of, over_at, rate, sums, over_sums, *state
):
    capacity = state[0].shape[0]
    per = adam_block(capacity)

    def kernel(*refs):
        local_ref, kind_ref, over_ref, rate_ref = refs[:4]
        cond_ref, spread_ref, chunk_ref, dmod_ref, over_sums_ref, sums_ref = refs[4:10]
        master_ref, first_ref, second_ref = refs[10:13]
        *outs, grad_ref = refs[-4:]
        step = pl.program_id(0) + begin // per
        for at in range(per):
            slot = step * per + at
            kind = kind_ref[slot]

            @pl.when(kind == 0)
            def _():
                grad_ref[...] = jnp.zeros_like(grad_ref)

            @pl.when(kind == 1)
            def _():
                grad_ref[...] = sums_ref[at].astype(jnp.float32)

            @pl.when(kind == 2)
            def _():
                grad_ref[...] = over_sums_ref[over_ref[slot]].astype(jnp.float32)

            @pl.when(kind == 3)
            def _():
                factors = tile_factors(local_ref[slot], cond_ref, spread_ref, chunk_ref)
                grad_ref[...] = jnp.dot(
                    factors, dmod_ref[...].astype(jnp.bfloat16), preferred_element_type=jnp.float32
                )

            results = adam_step(
                master_ref[at], first_ref[at], second_ref[at], grad_ref[...], rate_ref[slot]
            )
            for out, result in zip(outs, results):
                out[at] = result

    whole = pl.BlockSpec(memory_space=pltpu.VMEM)
    sums_block = pl.BlockSpec((per, TS, TS), lambda i, *_: (i, 0, 0))
    block = pl.BlockSpec((per, TS, TS), lambda i, *_: (i + begin // per, 0, 0))
    return pl.pallas_call(
        kernel,
        out_shape=[jax.ShapeDtypeStruct(state[0].shape, jnp.float32)] * 3,
        grid_spec=pltpu.PrefetchScalarGridSpec(
            num_scalar_prefetch=4,
            grid=((end - begin) // per,),
            in_specs=[whole] * 5
            + [sums_block]
            + [block] * 3
            + [pl.BlockSpec(memory_space=pl.ANY)] * len(into),
            out_specs=[block] * 3,
            scratch_shapes=[pltpu.VMEM((TS, TS), jnp.float32)],
        ),
        input_output_aliases={13 + number: number for number in range(len(into))},
        compiler_params=pltpu.CompilerParams(
            dimension_semantics=("arbitrary",), vmem_limit_bytes=VMEM_BYTES
        ),
        cost_estimate=pl.CostEstimate(
            flops=80 * spread_flops(tables),
            bytes_accessed=26 * (end - begin) * TS * TS,
            transcendentals=0,
        ),
        name="adam_slots",
    )(local, kind_of, over_at, rate, *tables, dmod, over_sums, sums, *state, *into)


def spread_flops(tables):
    return tables[1].shape[1] * TS * TS


def windowed(queries, keys, values, allowed, local_heads):
    micro_count, row_count = queries.shape[:2]
    query_heads = queries.reshape(micro_count, row_count, local_heads, HD)
    key_heads = keys.reshape(micro_count, -1, local_heads, HD)
    value_heads = values.reshape(micro_count, -1, local_heads, HD)
    scores = jnp.einsum(
        "mqhd,mkhd->mhqk", query_heads, key_heads, preferred_element_type=jnp.float32
    ) * HD ** (-0.5)
    scores = jnp.where(allowed[:, None], scores, MASKED)
    highest = jnp.max(scores, axis=-1, keepdims=True)
    expo = jnp.exp(scores - highest)
    total = jnp.sum(expo, axis=-1, keepdims=True)
    probs = (expo / total).astype(jnp.bfloat16)
    result = jnp.einsum("mhqk,mkhd->mqhd", probs, value_heads, preferred_element_type=jnp.float32)
    return (
        result.reshape(micro_count, row_count, -1).astype(jnp.bfloat16),
        highest + jnp.log(total),
    )


def windowed_back(queries, keys, values, allowed, log_total, grad_out, local_heads):
    micro_count, row_count = queries.shape[:2]
    scale = HD ** (-0.5)
    query_heads = queries.reshape(micro_count, row_count, local_heads, HD)
    key_heads = keys.reshape(micro_count, -1, local_heads, HD)
    value_heads = values.reshape(micro_count, -1, local_heads, HD)
    grad_heads = grad_out.reshape(micro_count, row_count, local_heads, HD)
    key_count = keys.shape[1]
    scores = (
        jnp.einsum("mqhd,mkhd->mhqk", query_heads, key_heads, preferred_element_type=jnp.float32)
        * scale
    )
    probs = jnp.where(allowed[:, None], jnp.exp(scores - log_total), 0.0)
    dprobs = jnp.einsum(
        "mqhd,mkhd->mhqk", grad_heads, value_heads, preferred_element_type=jnp.float32
    )
    dscores = (probs * (dprobs - jnp.sum(probs * dprobs, axis=-1, keepdims=True))).astype(
        jnp.bfloat16
    )
    dquery = (
        jnp.einsum("mhqk,mkhd->mqhd", dscores, key_heads, preferred_element_type=jnp.float32)
        * scale
    )
    dkey = (
        jnp.einsum("mhqk,mqhd->mkhd", dscores, query_heads, preferred_element_type=jnp.float32)
        * scale
    )
    dvalue = jnp.einsum(
        "mhqk,mqhd->mkhd",
        probs.astype(jnp.bfloat16),
        grad_heads,
        preferred_element_type=jnp.float32,
    )
    return (
        dquery.reshape(micro_count, row_count, -1),
        dkey.reshape(micro_count, key_count, -1),
        dvalue.reshape(micro_count, key_count, -1),
    )


def matmul(left, right):
    return jnp.dot(left, right, preferred_element_type=jnp.float32)


def one_step(
    compact,
    x_in,
    cotangent,
    cond,
    context,
    clip_lengths,
    pad_mask,
    owners,
    master,
    first_moment,
    second_moment,
    rank,
    over,
    over_place,
    second_step,
):
    seq_count = lax.axis_size("seq")
    head_count = lax.axis_size("head")
    me = lax.axis_index("seq")
    capacity = master.shape[1]
    micro_count, row_count = x_in.shape[:2]
    frames = pad_mask.shape[1]
    clip_count = clip_lengths.shape[1]
    head_cols = D // head_count
    ff_cols = FF // head_count
    mod_cols = 6 * D // head_count
    local_heads = head_cols // HD
    first_row = me * row_count
    token_count = micro_count * row_count
    clip_span = min(clip_count, row_count // MINLEN + 2)
    shapes = piece_shapes(head_count)

    owner_row = owners[0]
    cuts = slot_cuts(seq_count, capacity, head_count, compact)
    attn_tiles, sent_tiles, cut_one, cut_two, spare = cuts
    tile_ids = jnp.arange(owner_row.shape[0], dtype=jnp.int32)
    over_hit = over[None, :] & (
        over_place[None, :] == jnp.arange(sum(spare), dtype=jnp.int32)[:, None]
    )
    over_tile = jnp.sum(jnp.where(over_hit, tile_ids[None, :], 0), axis=1)
    over_mine = jnp.any(over_hit & (owner_row == me)[None, :], axis=1)
    slot_hit = (owner_row[None, :] == me) & (
        rank[None, :] == jnp.arange(capacity, dtype=jnp.int32)[:, None]
    )
    slot_used = jnp.any(slot_hit, axis=1)
    slot_tile = jnp.sum(jnp.where(slot_hit, tile_ids[None, :], 0), axis=1)
    slot_tile = jnp.where(slot_used, slot_tile, -1)

    own = master[0]
    sizes = ring_sizes(seq_count)
    offsets = [0]
    for row_total, col_total in shapes[:7]:
        offsets.append(offsets[-1] + row_total * col_total // (TS * TS))
    inner = [math.prod(sizes[dim + 1 :]) for dim in range(3)]
    back = [(me // inner[dim] - owner_row // inner[dim]) % sizes[dim] for dim in range(3)]
    over_rank = jnp.sum(jnp.where(over_hit, rank[None, :], 0), axis=1)
    steps_back = [
        (me // inner[dim] - jnp.arange(sizes[dim], dtype=jnp.int32)) % sizes[dim] * inner[dim]
        for dim in range(3)
    ]
    devices = (
        steps_back[0][:, None, None] + steps_back[1][None, :, None] + steps_back[2][None, None, :]
    ).reshape(-1)

    def by_home(listed):
        return listed.reshape(seq_count, -1)[devices].reshape(*sizes, -1)

    def home_of(place, each):
        device = place // each
        steps = [(me // inner[dim] - device // inner[dim]) % sizes[dim] for dim in range(3)]
        return steps, place - device * each

    ticks = Ticks()
    chunks = [(0, cut_one), (cut_one, cut_two)]
    gather_parts = [portions(*chunk, wide) for chunk, wide in zip(chunks, GATHER_WIDE)]
    scatter_parts = [portions(*chunk, 34) for chunk in chunks]
    if compact:

        def start_pair(number, *parts, shift=0.0):
            first, middle, second, _ = gather_parts[number]
            block = (own[first:second] + shift).astype(jnp.bfloat16)
            ticks.start(("pair", number), gather_pair([block, *parts], middle - first, sizes))

        def start_rest(number, *extra, shift=0.0):
            block = own[gather_parts[number][2] : gather_parts[number][3]]
            block = (block + shift).astype(jnp.bfloat16)
            block = jnp.concatenate([block, *extra], axis=0)
            ticks.start(("rest", number), gather_ticks(block, sizes, (2, 1, 0)))

        start_pair(0, second_step)
        over_low = jnp.where(
            by_home(over_mine)[..., None, None],
            own[by_home(over_rank)].astype(jnp.bfloat16),
            jnp.zeros((), jnp.bfloat16),
        ).transpose(2, 1, 0, 3, 4, 5)
        ticks.start("over", scatter_ticks(lambda step: over_low[step], sizes, (2, 1, 0)))
        start_rest(0, ticks.finish(["over"])[0])
        for _ in range(sizes[0] - 2):
            ticks.tick([("pair", 0)])
        on_plane = ticks.moving["pair", 0]
        ticks.tick([("pair", 0)])
        start_pair(1, shift=nothing(*on_plane).astype(jnp.float32))
        on_plane = ticks.moving["pair", 0]
        ticks.finish([("pair", 0), ("rest", 0)])
        start_rest(1, shift=nothing(*on_plane).astype(jnp.float32))

    cond_rows = cond.reshape(micro_count * clip_count, D)
    tables = factor_tables(cond_rows, mod_cols)
    local = jnp.maximum(slot_tile - sent_tiles, 0)
    is_mod = slot_tile >= sent_tiles
    mod_count = jnp.sum(is_mod.astype(jnp.int32))
    tiles_here = jnp.sum((owner_row == me).astype(jnp.int32))
    mod_part = mod_product(tables, own, tiles_here - mod_count, mod_count, local)
    mod_part = (
        mod_part.reshape(mod_cols // TS, micro_count * clip_count, TS)
        .transpose(1, 0, 2)
        .reshape(micro_count * clip_count, mod_cols)
    )
    mod_all = lax.all_gather(lax.psum(mod_part, "seq"), "head", axis=1, tiled=True)

    weights = {}

    def fetch(kinds, numbers):
        if compact:
            each = sum(spare) // seq_count
            pools, source_at, index_at = [], jnp.zeros_like(rank), jnp.zeros_like(rank)
            steps, at = home_of(over_place, each)
            for number in numbers:
                first, middle, second, last = gather_parts[number]
                extra = 0 if number else each
                here = ~over & (rank >= second) & (rank < last)
                slot, block = rank - second, back
                if not number:
                    here = here | over
                    slot = jnp.where(over, last - second + at, slot)
                    block = [jnp.where(over, steps[dim], back[dim]) for dim in range(3)]
                source_at = jnp.where(here, len(pools) + block[0], source_at)
                index_at = jnp.where(
                    here, (block[1] * sizes[2] + block[2]) * (last - second + extra) + slot, index_at
                )
                pools = pools + ticks.results["rest", number]
                for which, (low, high, one, two) in enumerate(
                    [(first, middle, 2, 1), (middle, second, 1, 2)]
                ):
                    here = ~over & (rank >= low) & (rank < high)
                    array_at = back[one] * sizes[two] + back[two]
                    source_at = jnp.where(here, len(pools) + array_at, source_at)
                    index_at = jnp.where(here, back[0] * (high - low) + rank - low, index_at)
                    pools = pools + ticks.results["pair", number][which]
        else:
            pools = [lax.all_gather(own.astype(jnp.bfloat16), "seq", axis=0, tiled=True)]
            source_at = jnp.zeros_like(rank)
            index_at = owner_row * capacity + rank
        for kind in kinds:
            begin, end = offsets[kind : kind + 2]
            weights[kind] = fetch_matrix(
                pools, source_at[begin:end], index_at[begin:end], *shapes[kind]
            )

    if compact:
        fetch(range(5), [0])
    else:
        fetch(range(7), None)
    w_qkv, w_out, w_cq, w_ckv, w_cout = [weights[kind] for kind in range(5)]

    positions = first_row + jnp.arange(row_count, dtype=jnp.int32)
    ext_pos = first_row - WIN + jnp.arange(row_count + 2 * WIN, dtype=jnp.int32)
    near_keys, clip_keys, onehots, ctx_rows = [], [], [], []
    for micro_idx in range(micro_count):
        lengths = clip_lengths[micro_idx]
        clip_tok = clip_ids(lengths, positions)
        clip_start = jnp.minimum(clip_tok[0], clip_count - clip_span)
        key_clip = clip_start + jnp.arange(clip_span * CTX, dtype=jnp.int32) // CTX
        mask_pad = jnp.pad(pad_mask[micro_idx], (WIN, WIN))
        ext_flag = lax.dynamic_slice_in_dim(mask_pad, first_row, row_count + 2 * WIN, 0)
        near_keys.append(window_mask(positions, ext_pos, ext_flag, lengths, frames))
        clip_keys.append(clip_tok[:, None] == key_clip[None, :])
        listed = micro_idx * clip_count + clip_tok
        onehots.append(
            listed[:, None] == jnp.arange(micro_count * clip_count, dtype=jnp.int32)[None, :]
        )
        ctx_rows.append(
            lax.dynamic_slice_in_dim(context[micro_idx], clip_start, clip_span, 0).reshape(
                clip_span * CTX, DC
            )
        )
    near_keys, clip_keys = jnp.stack(near_keys), jnp.stack(clip_keys)
    onehot = jnp.concatenate(onehots, axis=0).astype(jnp.float32)
    ctx_rows = jnp.concatenate(ctx_rows, axis=0)

    def by_micro(rows):
        return rows.reshape(micro_count, -1, rows.shape[-1])

    def flat(rows):
        return rows.reshape(-1, rows.shape[-1])

    mod_frames = jnp.dot(onehot, mod_all, precision=PRECISE)
    shifts = [mod_frames[:, 2 * which * D : (2 * which + 1) * D] for which in range(3)]
    scales = [mod_frames[:, (2 * which + 1) * D : (2 * which + 2) * D] for which in range(3)]
    resid_zero = flat(x_in).astype(jnp.float32)
    normed_one, inverse_one = layer_norm(resid_zero)
    input_one = (normed_one * (1.0 + scales[0]) + shifts[0]).astype(jnp.bfloat16)
    proj_qkv = by_micro(matmul(input_one, w_qkv).astype(jnp.bfloat16))
    queries = proj_qkv[:, :, :head_cols]
    kv_ext = padded(proj_qkv[:, :, head_cols:], (("seq", 1),), WIN)
    attended, log_one = windowed(
        queries, kv_ext[:, :, :head_cols], kv_ext[:, :, head_cols:], near_keys, local_heads
    )
    resid_one = resid_zero + head_sum(matmul(flat(attended), w_out))
    normed_two, inverse_two = layer_norm(resid_one)
    input_two = (normed_two * (1.0 + scales[1]) + shifts[1]).astype(jnp.bfloat16)
    cross_query = by_micro(matmul(input_two, w_cq).astype(jnp.bfloat16))
    cross_kv = by_micro(matmul(ctx_rows, w_ckv).astype(jnp.bfloat16))
    cross_out, log_two = windowed(
        cross_query, cross_kv[:, :, :head_cols], cross_kv[:, :, head_cols:], clip_keys, local_heads
    )
    resid_two = resid_one + head_sum(matmul(flat(cross_out), w_cout))
    if compact:
        ticks.finish([("pair", 1), ("rest", 1)])
        fetch((6, 5), [0, 1])
    w_glu, w_down = weights[5], weights[6]
    normed_three, inverse_three = layer_norm(resid_two)
    input_three = (normed_three * (1.0 + scales[2]) + shifts[2]).astype(jnp.bfloat16)
    gate_up = matmul(input_three, w_glu)
    gate_part = gate_up[:, :ff_cols]
    up_part = gate_up[:, ff_cols:]
    sigmoid_gate = jax.nn.sigmoid(gate_part)
    silu_gate = gate_part * sigmoid_gate
    hidden = (silu_gate * up_part).astype(jnp.bfloat16)

    grad_low = flat(cotangent)
    grad_three = grad_low.astype(jnp.float32)
    pool_ff = as_tiles(matmul(hidden.T, grad_low), sent_tiles, offsets[6])
    grad_hidden = matmul(grad_low, w_down.T)
    dglu = jnp.concatenate(
        [
            grad_hidden * up_part * sigmoid_gate * (1.0 + gate_part * (1.0 - sigmoid_gate)),
            grad_hidden * silu_gate,
        ],
        axis=1,
    ).astype(jnp.bfloat16)
    pool_ff = as_tiles(matmul(input_three.T, dglu), pool_ff, offsets[5])
    slots = listed_tiles(owner_row, rank, devices, cut_two)

    def start_scatter(number, pool, listed, gate=()):
        first, middle, second, last = scatter_parts[number]
        wanted = jnp.concatenate(
            [slots.reshape(*sizes, cut_two), by_home(listed)], axis=3
        )
        if number:
            wanted = jnp.maximum(wanted, attn_tiles)
        taken = []

        def pick(places, *before):
            return pool[places + nothing(*before)]


        def plane(low, high, order):
            here = wanted[..., low:high].transpose(*order, 0, 3)
            sent = [
                [pick(here[step, at], *gate) for at in range(sizes[order[1]])]
                for step in range(1, sizes[order[0]])
            ]
            kept = pick(here[0], *(() if gate else sum(sent, [])))
            taken.extend([*sum(sent, []), kept])
            return lambda step, at: sent[step - 1][at] if step else kept[at]

        one, two = plane(first, middle, (2, 1)), plane(middle, second, (1, 2))
        here = jnp.concatenate([wanted[..., second:last], wanted[..., cut_two:]], axis=3)
        sent = pick(here[1], *gate)
        kept = pick(jnp.concatenate([here[:1], here[2:]]), *(() if gate else (sent,)))
        taken.extend([sent, kept])
        ticks.start(("pair", number), scatter_pair(one, two, sizes))
        ticks.start(
            ("rest", number),
            scatter_ticks(
                lambda step: sent if step == 1 else kept[max(step - 1, 0)], sizes, (0, 1, 2)
            ),
        )
        return taken

    def start_out(number):
        total = ticks.finish([("rest", number)])[0]
        total = total[scatter_parts[number][3] - scatter_parts[number][2] :]
        ticks.start(("out", number), gather_ticks(total, sizes, (0, 1, 2)))

    if compact:
        taken = start_scatter(1, pool_ff, over_tile[spare[0] :])
        pool_ff, _ = lax.optimization_barrier((pool_ff, taken))
    back_three, dscale_three, dshift_three = norm_back(
        head_sum(matmul(dglu, w_glu.T)), normed_three, inverse_three, scales[2]
    )
    grad_two = grad_three + back_three
    grad_low = grad_two.astype(jnp.bfloat16)
    grad_cout = matmul(flat(cross_out).T, grad_low).astype(jnp.bfloat16)
    grad_cross = by_micro(matmul(grad_low, w_cout.T).astype(jnp.bfloat16))
    dquery_two, dkey_two, dvalue_two = windowed_back(
        cross_query,
        cross_kv[:, :, :head_cols],
        cross_kv[:, :, head_cols:],
        clip_keys,
        log_two,
        grad_cross,
        local_heads,
    )
    dquery_two = flat(dquery_two).astype(jnp.bfloat16)
    pool = as_tiles(grad_cout, pool_ff, offsets[4])
    pool = as_tiles(matmul(input_two.T, dquery_two), pool, offsets[2])
    dkv_two = flat(jnp.concatenate([dkey_two, dvalue_two], axis=2)).astype(jnp.bfloat16)
    pool = as_tiles(matmul(ctx_rows.T, dkv_two), pool, offsets[3])
    back_two, dscale_two, dshift_two = norm_back(
        head_sum(matmul(dquery_two, w_cq.T)), normed_two, inverse_two, scales[1]
    )
    grad_one = grad_two + back_two
    grad_low = grad_one.astype(jnp.bfloat16)
    pool = as_tiles(matmul(flat(attended).T, grad_low), pool, offsets[1])
    grad_attended = by_micro(matmul(grad_low, w_out.T).astype(jnp.bfloat16))
    dquery_one, dkey_ext, dvalue_ext = windowed_back(
        queries,
        kv_ext[:, :, :head_cols],
        kv_ext[:, :, head_cols:],
        near_keys,
        log_one,
        grad_attended,
        local_heads,
    )
    dkv_ext = jnp.concatenate([dkey_ext, dvalue_ext], axis=2)
    rims = jnp.concatenate([dkv_ext[:, :WIN], dkv_ext[:, row_count + WIN :]], axis=1)
    returned = padded(rims.astype(jnp.bfloat16), (("seq", 1),), WIN).astype(jnp.float32)
    dkv_own = dkv_ext[:, WIN : row_count + WIN]
    dkv_own = dkv_own.at[:, :WIN].add(returned[:, :WIN])
    dkv_own = dkv_own.at[:, row_count - WIN :].add(returned[:, 3 * WIN :])
    dqkv = flat(jnp.concatenate([dquery_one, dkv_own], axis=2).astype(jnp.bfloat16))
    pool = as_tiles(matmul(input_one.T, dqkv), pool, offsets[0])
    back_one, dscale_one, dshift_one = norm_back(
        head_sum(matmul(dqkv, w_qkv.T)), normed_one, inverse_one, scales[0]
    )
    grad_input = by_micro(grad_one + back_one)

    dmod = jnp.concatenate(
        [
            jnp.dot(onehot.T, rows, precision=PRECISE)
            for rows in (
                dshift_one,
                dscale_one,
                dshift_two,
                dscale_two,
                dshift_three,
                dscale_three,
            )
        ],
        axis=1,
    )
    dmod = lax.dynamic_slice_in_dim(dmod, lax.axis_index("head") * mod_cols, mod_cols, 1)
    ticks.start("dmod", sum_ticks(dmod, sizes))
    (dmod,) = ticks.finish(["dmod"])
    gate = [dmod]
    if compact:
        gate = start_scatter(0, pool, over_tile[: spare[0]], [dmod])
        start_out(1)
        ticks.finish([("out", 1)])
    late = (hidden.astype(jnp.float32) + nothing(gate[0]).astype(jnp.float32)).astype(jnp.bfloat16)
    out_block = by_micro((resid_two + head_sum(matmul(late, w_down))).astype(jnp.bfloat16))
    dmod = (
        dmod
        .reshape(micro_count * clip_count, mod_cols // TS, TS)
        .transpose(1, 0, 2)
        .reshape(-1, TS)
    )

    state = (own, first_moment[0], second_moment[0])
    rate = slot_rates(slot_tile, shapes)
    if compact:
        over_slot = slot_hit & over[None, :]
        slot_over = jnp.any(over_slot, axis=1)
        over_at = jnp.sum(jnp.where(over_slot, over_place[None, :], 0), axis=1)
        kind_of = jnp.where(is_mod, 3, jnp.where(slot_over, 2, slot_used.astype(jnp.int32)))
        slot = first_pass_slot(cut_one, capacity)

        def sums_of(number):
            first, _, second, last = scatter_parts[number]
            pair, rest = ticks.finish([("pair", number), ("rest", number)])
            return [pair, rest[: last - second]]

        def over_sums_of(number):
            each = spare[number] // seq_count
            place = over_at - (spare[0] if number else 0)
            steps, at = home_of(place, each)
            block = (steps[2] * sizes[1] + steps[1]) * sizes[0] + steps[0]
            (sums,) = ticks.finish([("out", number)])
            return jnp.concatenate(sums, axis=0), block * each + at

        later = jnp.concatenate(
            [*sums_of(1), jnp.zeros((capacity - cut_two, TS, TS), jnp.bfloat16)], axis=0
        )
        over_sums, over_index = over_sums_of(1)
        results = adam_slots(
            slot,
            capacity,
            (),
            tables,
            dmod,
            local,
            kind_of,
            jnp.clip(over_index, 0, over_sums.shape[0] - 1),
            rate,
            later[slot - cut_one :],
            over_sums,
            *state,
        )
        ticks.finish([("rest", 0)])
        start_out(0)
        sooner = jnp.concatenate([*sums_of(0), later[: slot - cut_one]], axis=0)
        over_sums, over_index = over_sums_of(0)
        results = adam_slots(
            0,
            slot,
            results,
            tables,
            dmod,
            local,
            kind_of,
            jnp.clip(over_index, 0, over_sums.shape[0] - 1),
            rate,
            sooner,
            over_sums,
            *state,
        )
    else:
        sums = lax.psum_scatter(
            pool[listed_tiles(owner_row, rank, jnp.arange(seq_count), capacity).reshape(-1)],
            "seq",
            scatter_dimension=0,
            tiled=True,
        )
        results = adam_slots(
            0,
            capacity,
            (),
            tables,
            dmod,
            local,
            jnp.where(is_mod, 3, slot_used.astype(jnp.int32)),
            jnp.zeros_like(slot_tile),
            rate,
            sums,
            jnp.zeros((1, TS, TS), jnp.bfloat16),
            *state,
        )
    weight, first, second = results
    return (out_block, grad_input, weight[None], first[None], second[None])


def on_device(*args):
    owner_row, own = args[6][0], args[7][0]
    seq_count, capacity = lax.axis_size("seq"), own.shape[0]
    head_count = lax.axis_size("head")
    first, _, second, _ = portions(
        0, slot_cuts(seq_count, capacity, head_count, True)[2], GATHER_WIDE[0]
    )
    block = own[first:second].astype(jnp.bfloat16)
    second_step = ring_send(block, ring_sizes(seq_count), 0)
    fits, *plan = layout_plan(owner_row, seq_count, capacity, head_count)
    misfits = lax.pmax(1 - fits.astype(jnp.int32), "head")
    return lax.cond(
        misfits == 0, partial(one_step, True), partial(one_step, False), *args, *plan, second_step
    )


def solution(mesh):
    placed = (
        P(None, "seq", None),
        P(None, "seq", None),
        P(),
        P(),
        P(),
        P(),
        P("head", None),
        P("head", "seq", None, None),
        P("head", "seq", None, None),
        P("head", "seq", None, None),
    )
    return jax.shard_map(
        on_device,
        mesh=mesh,
        in_specs=placed,
        out_specs=(
            P(None, "seq", None),
            P(None, "seq", None),
            P("head", "seq", None, None),
            P("head", "seq", None, None),
            P("head", "seq", None, None),
        ),
        check_vma=False,
    )
```

time: 3340 us -> 1600 us (0.48)
  waiting for transfers between devices: 1880 us -> 563 us
  local copies, waits for them, and re-layouts: 874 us -> 249 us
  Pallas kernels: 0 us -> 232 us
  matrix products: 312 us -> 197 us
  starting transfers between devices: 22.7 us -> 86.7 us
    unnamed x15 -> x0, waiting for transfers between devices: 1000 us -> none
    all_gather x1 -> x0, waiting for transfers between devices: 719 us -> none  [on_device(): lax.all_gather(master[0].astype(jnp.bfloat16), 'seq', axis=0, tiled=True)]
    ppermute x0 -> x82, waiting for transfers between devices: none -> 536 us  [the longest x76 536 us: ring_send(): return lax.ppermute(block, 'seq', pairs)]
    scatter x2 -> x0, local copies, waits for them, and re-layouts: 333 us -> none  [the longest x1 323 us: on_device(): jnp.zeros((seq_count * capacity, TS, TS), jnp.float32).at[tile_place]]
    pallas_call x0 -> x17, Pallas kernels: none -> 232 us  [the longest x7 106 us: fetch_matrix(): pl.pallas_call(kernel, out_shape=jax.ShapeDtypeStruct((row_count, col_cou...]
    reshape x15, local copies, waits for them, and re-layouts: 190 us -> 15.8 us  [the longest x1 3.54 us: windowed_back(): dkey.reshape(micro_count, key_count, -1)]
    unnamed x503 -> x11, local copies, waits for them, and re-layouts: 125 us -> 0.06 us
    dot_general x71 -> x40, matrix products: 312 us -> 197 us  [the longest x20 122 us: matmul(): return jnp.dot(left, right, preferred_element_type=jnp.float32)]
  transfers between devices with their start and end apart: 22 -> 87, of which waited for: 17 -> 43; matrix products, arithmetic and copies ran while one was open for 31% -> 35% of each run, Pallas kernels for 0% -> 8%
where the time goes in v1:
time: 1600 us; the launch traced here: 1580 us
  waiting for transfers between devices  563 us (35%)
  local copies, waits for them, and re-layouts  249 us (16%)
  Pallas kernels  232 us (14%)
  other arithmetic  203 us (13%)
  matrix products  197 us (12%)
  starting transfers between devices  86.7 us (5%)
  loops' own time  27.7 us (2%)
  between operations  17 us (1%)
    ppermute x76, waiting for transfers between devices, ring_send(): return lax.ppermute(block, 'seq', pairs)  536 us
    dot_general x20, matrix products, matmul(): return jnp.dot(left, right, preferred_element_type=jnp.float32)  122 us
    pallas_call x7, Pallas kernels, fetch_matrix(): pl.pallas_call(kernel, out_shape=jax.ShapeDtypeStruct((row_count, col_cou...  106 us
    gather x16, local copies, waits for them, and re-layouts, pick(): return pool[places + nothing(*before)]  91.5 us
    ppermute x76, starting transfers between devices, ring_send(): return lax.ppermute(block, 'seq', pairs)  75.1 us
    convert_element_type x33, other arithmetic, added(): (left.astype(jnp.float32) + right.astype(jnp.float32)).astype(jnp.bfloat16)  61.3 us
    pallas_call x7, Pallas kernels, as_tiles(): pl.pallas_call(kernel, out_shape=jax.ShapeDtypeStruct((into if is_new els...  60.1 us
    pallas_call x2, Pallas kernels, adam_slots(): pl.pallas_call(kernel, out_shape=[jax.ShapeDtypeStruct(state[0].shape, jn...  47.2 us
  transfers between devices with their start and end apart: 87, of which 43 were waited for; matrix products, arithmetic and copies ran while one was open for 35% of the time, Pallas kernels for 8%

profile of v1, /device:TPU:0, one launch (start us, length us, event | category | flops | bytes accessed | tf_op | source)
XLA Modules:
  0.0 1580.9 jit_solution(2715803519009813896)
XLA Ops:
  27.5 12.4 collective-permute-done.100
  40.0 1533.8 %conditional.1 = (bf16[2,256,1536]{2,1,0:T(8,128)(2,1)}, f32[2,256,1536]{2,1,0:T(8,128)}, f32[1,141,128,128]{3,2,1,0:T(8,128)}, f32[1,141,128,128]{3,2,1,0:T(8,128)}, f32[1,141,128,128]{3,2,1,0:T(8,128)}) conditional(s32[]{:T(128)} %convert_element_type.1261, (bf16[2,256,1536]{2,1,0:T(8,128)(2,1)S(1)}, s32[2,8]{1,0:T(2,128)S(1)}, ...), branch_computations={%region_11.44_spmd, %region_44.81_spmd} | conditional | flops 77727973376 | bytes 2822707968 | solution.py:1174
  56.2 18.8 %mod_product.3 = f32[576,128]{1,0:T(8,128)S(1)} custom-call(s32[2]{0:T(128)S(1)} %pad_add_fusion.4.meta_ref, s32[141]{0:T(256)S(1)} %get-tuple-element.498.local_ref.refs_0_, f32[1544,16]{1,0:T(8,128)S(1)} %pad_convert_fusion.cond_ref.refs_4_, bf16[16,576]{1,0:T(8,128)(2,1)} %get-tuple-element.137.spread_ref.refs_5_, ...), custom_call_target="tpu_custom_call" | custom-call | flops 754974720 | bytes 2621440 | tf_op jit(solution)/shard_map/cond/branch_1_fun/mod_product/pallas_call | solution.py:551
  107.9 8.8 collective-permute-start.16
  139.4 22.2 %collective-permute-done.19 = bf16[3,128,128]{2,1,0:T(8,128)(2,1)S(1)} collective-permute-done((bf16[3,128,128]{2,1,0:T(8,128)(2,1)S(1)}, bf16[3,128,128]{2,1,0:T(8,128)(2,1)S(1)}, u32[]{:S(2)}, u32[]{:S(2)}) %collective-permute-start.19) | collective-permute-done | bytes 98336 | tf_op jit(solution)/shard_map/cond/branch_1_fun/ppermute | solution.py:273
  176.9 8.3 collective-permute-done.21
  193.4 18.8 %collective-permute-done.22.refs_1_ = bf16[36,128,128]{2,1,0:T(8,128)(2,1)S(1)} collective-permute-done((bf16[36,128,128]{2,1,0:T(8,128)(2,1)S(1)}, bf16[36,128,128]{2,1,0:T(8,128)(2,1)S(1)}, u32[]{:S(2)}, u32[]{:S(2)}) %collective-permute-start.22) | collective-permute-done | bytes 1179680 | tf_op jit(solution)/shard_map/cond/branch_1_fun/ppermute | solution.py:273
  224.2 9.9 collective-permute-done.27.refs_5_
  245.9 29.2 %collective-permute-done.28.refs_6_ = bf16[68,128,128]{2,1,0:T(8,128)(2,1)} collective-permute-done((bf16[68,128,128]{2,1,0:T(8,128)(2,1)}, bf16[68,128,128]{2,1,0:T(8,128)(2,1)}, u32[]{:S(2)}, u32[]{:S(2)}) %collective-permute-start.28) | collective-permute-done | bytes 2228256 | tf_op jit(solution)/shard_map/cond/branch_1_fun/ppermute | solution.py:273
  276.5 10.7 fusion.253
  299.3 31.7 %collective-permute-done.37 = bf16[18,128,128]{2,1,0:T(8,128)(2,1)S(1)} collective-permute-done((bf16[18,128,128]{2,1,0:T(8,128)(2,1)S(1)}, bf16[18,128,128]{2,1,0:T(8,128)(2,1)S(1)}, u32[]{:S(2)}, u32[]{:S(2)}) %collective-permute-start.37) | collective-permute-done | bytes 589856 | tf_op jit(solution)/shard_map/cond/branch_1_fun/ppermute | solution.py:273
  332.1 12.6 fetch_matrix.21
  437.6 16.3 %collective-permute-done.44 = bf16[38,128,128]{2,1,0:T(8,128)(2,1)} collective-permute-done((bf16[38,128,128]{2,1,0:T(8,128)(2,1)}, bf16[38,128,128]{2,1,0:T(8,128)(2,1)}, u32[]{:S(2)}, u32[]{:S(2)}) %collective-permute-start.44) | collective-permute-done | bytes 1245216 | tf_op jit(solution)/shard_map/cond/branch_1_fun/ppermute | solution.py:273
  535.0 35.3 %collective-permute-done.46.refs_18_ = bf16[76,128,128]{2,1,0:T(8,128)(2,1)} collective-permute-done((bf16[76,128,128]{2,1,0:T(8,128)(2,1)}, bf16[76,128,128]{2,1,0:T(8,128)(2,1)}, u32[]{:S(2)}, u32[]{:S(2)}) %collective-permute-start.46) | collective-permute-done | bytes 2490400 | tf_op jit(solution)/shard_map/cond/branch_1_fun/ppermute | solution.py:273
  570.9 52.3 %collective-permute-done.47.refs_19_ = bf16[76,128,128]{2,1,0:T(8,128)(2,1)} collective-permute-done((bf16[76,128,128]{2,1,0:T(8,128)(2,1)}, bf16[76,128,128]{2,1,0:T(8,128)(2,1)}, u32[]{:S(2)}, u32[]{:S(2)}) %collective-permute-start.47) | collective-permute-done | bytes 2490400 | tf_op jit(solution)/shard_map/cond/branch_1_fun/ppermute | solution.py:273
  623.8 51.9 %fetch_matrix.26 = bf16[1536,6144]{1,0:T(8,128)(2,1)} custom-call(s32[576]{0:T(1024)S(1)} %slice.964.source_ref, s32[576]{0:T(1024)S(1)} %slice.965.index_ref, bf16[36,128,128]{2,1,0:T(8,128)(2,1)S(1)} %pad_maximum_fusion.18.refs_0_, bf16[36,128,128]{2,1,0:T(8,128)(2,1)S(1)} %collective-permute-done.22.refs_1_, ...), custom_call_target="tpu_custom_call" | custom-call | bytes 37748736 | tf_op jit(solution)/shard_map/cond/branch_1_fun/fetch_matrix/pallas_call | solution.py:199
  675.8 16.7 %fusion.445 = f32[512,6144]{1,0:T(8,128)} fusion(bf16[512,1536]{1,0:T(8,128)(2,1)S(1)} %fusion.39, bf16[1536,6144]{1,0:T(8,128)(2,1)} %fetch_matrix.26), kind=kOutput, calls=%fused_computation.1007 | convolution fusion | flops 9663676416 | bytes 33030144 | tf_op jit(solution)/shard_map/cond/branch_1_fun/dot_general | solution.py:706
  692.5 20.8 %fetch_matrix.27 = bf16[3072,1536]{1,0:T(8,128)(2,1)} custom-call(s32[288]{0:T(512)S(1)} %copy-done.20, s32[288]{0:T(512)S(1)} %copy-done.19, bf16[36,128,128]{2,1,0:T(8,128)(2,1)S(1)} %pad_maximum_fusion.18.refs_0_, bf16[36,128,128]{2,1,0:T(8,128)(2,1)S(1)} %collective-permute-done.22.refs_1_, bf16[36,128,128]{2,1,0:T(8,128)(2,1)S(1)} %collective-permute-done.23.refs_2_, ...), custom_call_target="tpu_custom_call" | custom-call | bytes 18874368 | tf_op jit(solution)/shard_map/cond/branch_1_fun/fetch_matrix/pallas_call | solution.py:199
  713.3 14.8 fusion.8
  728.1 15.8 fusion.59
  743.9 16.4 %convolution_convert_fusion.grad_ref = bf16[1536,6144]{1,0:T(8,128)(2,1)} fusion(bf16[512,1536]{1,0:T(8,128)(2,1)S(1)} %copy-done.168, bf16[512,3072]{1,0:T(8,128)(2,1)} %get-tuple-element.381, bf16[512,3072]{1,0:T(8,128)(2,1)} %get-tuple-element.380), kind=kOutput, calls=%fused_computation.22 | convolution fusion | flops 9685696512 | bytes 26738688 | tf_op jit(solution)/shard_map/cond/branch_1_fun/dot_general | solution.py:706
  760.3 9.3 convolution_convert_fusion.1.grad_ref
  769.7 12.6 as_tiles.21.refs_0_
  782.3 29.1 %as_tiles.22.refs_0_ = bf16[1368,128,128]{2,1,0:T(8,128)(2,1)} custom-call(bf16[1536,6144]{1,0:T(8,128)(2,1)} %convolution_convert_fusion.grad_ref, bf16[1368,128,128]{2,1,0:T(8,128)(2,1)} %as_tiles.21.refs_0_), custom_call_target="tpu_custom_call", output_to_operand_aliasing={{}: (1, {})} | custom-call | bytes 37748736 | tf_op jit(solution)/shard_map/cond/branch_1_fun/as_tiles/pallas_call | solution.py:245
  848.8 11.6 gather_fusion.7
  860.5 11.2 gather_fusion.10
  871.7 11.2 gather_fusion.12
  983.8 9.1 fusion.3
  992.9 10.1 multiply_reduce_fusion
  1006.5 9.8 multiply_convert_fusion
  1042.6 23.4 %collective-permute-done.53 = bf16[2,128,1536]{2,1,0:T(8,128)(2,1)} collective-permute-done((bf16[2,128,1536]{2,1,0:T(8,128)(2,1)}, bf16[2,128,1536]{2,1,0:T(8,128)(2,1)}, u32[]{:S(2)}, u32[]{:S(2)}) %collective-permute-start.53) | collective-permute-done | bytes 786464 | tf_op jit(solution)/shard_map/cond/branch_1_fun/ppermute | solution.py:40
  1092.3 8.8 as_tiles.27
  1110.4 11.0 gather_fusion.16
  1151.1 7.4 collective-permute-done.56
  1172.3 7.8 collective-permute-done.58
  1186.9 19.9 %collective-permute-done.87 = bf16[38,128,128]{2,1,0:T(8,128)(2,1)S(1)} collective-permute-done((bf16[38,128,128]{2,1,0:T(8,128)(2,1)S(1)}, bf16[38,128,128]{2,1,0:T(8,128)(2,1)S(1)}, u32[]{:S(2)}, u32[]{:S(2)}) %collective-permute-start.87) | collective-permute-done | bytes 1245216 | tf_op jit(solution)/shard_map/cond/branch_1_fun/ppermute | solution.py:273
  1240.2 49.6 %collective-permute-done.88 = bf16[38,128,128]{2,1,0:T(8,128)(2,1)} collective-permute-done((bf16[38,128,128]{2,1,0:T(8,128)(2,1)}, bf16[38,128,128]{2,1,0:T(8,128)(2,1)}, u32[]{:S(2)}, u32[]{:S(2)}) %collective-permute-start.88) | collective-permute-done | bytes 1245216 | tf_op jit(solution)/shard_map/cond/branch_1_fun/ppermute | solution.py:273
  1291.9 10.3 fusion.58
  1310.5 13.3 collective-permute-done.62
  1340.6 26.1 %collective-permute-done.74 = bf16[4,14,128,128]{3,2,1,0:T(8,128)(2,1)S(1)} collective-permute-done((bf16[4,14,128,128]{3,2,1,0:T(8,128)(2,1)S(1)}, bf16[4,14,128,128]{3,2,1,0:T(8,128)(2,1)S(1)}, u32[]{:S(2)}, u32[]{:S(2)}) %collective-permute-start.74) | collective-permute-done | bytes 1835040 | tf_op jit(solution)/shard_map/cond/branch_1_fun/ppermute | solution.py:273
  1376.2 29.9 %collective-permute-done.76 = bf16[4,14,128,128]{3,2,1,0:T(8,128)(2,1)S(1)} collective-permute-done((bf16[4,14,128,128]{3,2,1,0:T(8,128)(2,1)S(1)}, bf16[4,14,128,128]{3,2,1,0:T(8,128)(2,1)S(1)}, u32[]{:S(2)}, u32[]{:S(2)}) %collective-permute-start.76) | collective-permute-done | bytes 1835040 | tf_op jit(solution)/shard_map/cond/branch_1_fun/ppermute | solution.py:273
  1408.7 8.0 collective-permute-done.94
  1417.4 19.0 %collective-permute-done.64 = bf16[2,2,13,128,128]{4,3,2,1,0:T(8,128)(2,1)S(1)} collective-permute-done((bf16[2,2,13,128,128]{4,3,2,1,0:T(8,128)(2,1)S(1)}, bf16[2,2,13,128,128]{4,3,2,1,0:T(8,128)(2,1)S(1)}, u32[]{:S(2)}, u32[]{:S(2)}) %collective-permute-start.64) | collective-permute-done | bytes 1703968 | tf_op jit(solution)/shard_map/cond/branch_1_fun/ppermute | solution.py:273
  1439.9 13.6 collective-permute-done.78
  1454.2 21.5 %collective-permute-done.96 = bf16[2,128,128]{2,1,0:T(8,128)(2,1)S(1)} collective-permute-done((bf16[2,128,128]{2,1,0:T(8,128)(2,1)S(1)}, bf16[2,128,128]{2,1,0:T(8,128)(2,1)S(1)}, u32[]{:S(2)}, u32[]{:S(2)}) %collective-permute-start.96) | collective-permute-done | bytes 65568 | tf_op jit(solution)/shard_map/cond/branch_1_fun/ppermute | solution.py:273
  1500.2 8.5 collective-permute-done.67
  1508.7 29.8 %adam_slots.4 = (f32[141,128,128]{2,1,0:T(8,128)}, f32[141,128,128]{2,1,0:T(8,128)}, f32[141,128,128]{2,1,0:T(8,128)}) custom-call(s32[141]{0:T(256)S(1)} %copy-done.16, s32[141]{0:T(256)S(1)} %get-tuple-element.358.refs_1_, s32[141]{0:T(256)S(1)} %copy-done.21, f32[141]{0:T(256)S(1)} %select_reduce_fusion.6.refs_3_, f32[1544,16]{1,0:T(8,128)S(1)} %copy-done.5, ...), custom_call_target="tpu_custom_call" | custom-call | flops 754974720 | bytes 34504704 | tf_op jit(solution)/shard_map/cond/branch_1_fun/adam_slots/pallas_call | solution.py:615
  1556.2 17.4 %adam_slots.5 = (f32[141,128,128]{2,1,0:T(8,128)}, f32[141,128,128]{2,1,0:T(8,128)}, f32[141,128,128]{2,1,0:T(8,128)}) custom-call(s32[141]{0:T(256)S(1)} %copy-done.16, s32[141]{0:T(256)S(1)} %get-tuple-element.358.refs_1_, s32[141]{0:T(256)S(1)} %copy-done.22, ...), custom_call_target="tpu_custom_call", output_to_operand_aliasing={{0}: (13, {}), {1}: (14, {}), {2}: (15, {})} | custom-call | flops 754974720 | bytes 25559040 | tf_op jit(solution)/shard_map/cond/branch_1_fun/adam_slots/pallas_call | solution.py:615
  (934 shorter events, 673.3 us)
Async XLA Ops:
  48.0 188.3 %all-reduce.15.cloned.1.call-start = ((), (), s32[]{:S(2)}) async-start(), calls=%async_computation.4 | async-start | bytes 589824 | tf_op jit(solution)/shard_map/cond/branch_1_fun/psum | solution.py:828
  76.0 55.6 %collective-permute-start.25 = (bf16[34,128,128]{2,1,0:T(8,128)(2,1)S(1)}, bf16[34,128,128]{2,1,0:T(8,128)(2,1)}, u32[]{:S(2)}, u32[]{:S(2)}) collective-permute-start(bf16[34,128,128]{2,1,0:T(8,128)(2,1)S(1)} %copy-done.177), channel_id=1, source_target_pairs={{0,8},{2,10},{4,12},{6,14},{8,16},{10,18},{12,20},{14,22},{16,24},... | collective-permute-start | bytes 3342344 | tf_op jit(solution)/shard_map/cond/branch_1_fun/ppermute | solution.py:273
  170.8 63.3 %collective-permute-start.27 = (bf16[68,128,128]{2,1,0:T(8,128)(2,1)}, bf16[68,128,128]{2,1,0:T(8,128)(2,1)}, u32[]{:S(2)}, u32[]{:S(2)}) collective-permute-start(bf16[68,128,128]{2,1,0:T(8,128)(2,1)} %pad_maximum_fusion.12.refs_4_), channel_id=1, source_target_pairs={{0,4},{2,6},{4,0},{6,2},{8,12},{10,14},{12,8},{14,10},{16,20},{18,... | collective-permute-start | bytes 6684680 | tf_op jit(solution)/shard_map/cond/branch_1_fun/ppermute | solution.py:273
  174.5 61.4 %collective-permute-start.30 = (bf16[68,128,128]{2,1,0:T(8,128)(2,1)}, bf16[68,128,128]{2,1,0:T(8,128)(2,1)}, u32[]{:S(2)}, u32[]{:S(2)}) collective-permute-start(bf16[68,128,128]{2,1,0:T(8,128)(2,1)} %pad_maximum_fusion.13.refs_8_), channel_id=1, source_target_pairs={{0,2},{2,0},{4,6},{6,4},{8,10},{10,8},{12,14},{14,12},{16,18},{18,... | collective-permute-start | bytes 6684680 | tf_op jit(solution)/shard_map/cond/branch_1_fun/ppermute | solution.py:273
  186.0 89.1 %collective-permute-start.28 = (bf16[68,128,128]{2,1,0:T(8,128)(2,1)}, bf16[68,128,128]{2,1,0:T(8,128)(2,1)}, u32[]{:S(2)}, u32[]{:S(2)}) collective-permute-start(bf16[68,128,128]{2,1,0:T(8,128)(2,1)} %pad_maximum_fusion.12.refs_4_), channel_id=1, source_target_pairs={{0,2},{2,0},{4,6},{6,4},{8,10},{10,8},{12,14},{14,12},{16,18},{18,... | collective-permute-start | bytes 6684680 | tf_op jit(solution)/shard_map/cond/branch_1_fun/ppermute | solution.py:273
  190.6 99.0 %collective-permute-start.31 = (bf16[68,128,128]{2,1,0:T(8,128)(2,1)}, bf16[68,128,128]{2,1,0:T(8,128)(2,1)}, u32[]{:S(2)}, u32[]{:S(2)}) collective-permute-start(bf16[68,128,128]{2,1,0:T(8,128)(2,1)} %pad_maximum_fusion.13.refs_8_), channel_id=1, source_target_pairs={{0,4},{2,6},{4,0},{6,2},{8,12},{10,14},{12,8},{14,10},{16,20},{18,... | collective-permute-start | bytes 6684680 | tf_op jit(solution)/shard_map/cond/branch_1_fun/ppermute | solution.py:273
  212.2 62.9 %collective-permute-start.23 = (bf16[36,128,128]{2,1,0:T(8,128)(2,1)S(1)}, bf16[36,128,128]{2,1,0:T(8,128)(2,1)S(1)}, u32[]{:S(2)}, u32[]{:S(2)}) collective-permute-start(bf16[36,128,128]{2,1,0:T(8,128)(2,1)S(1)} %collective-permute-done.22.refs_1_), channel_id=1, source_target_pairs={{0,8},{2,10},{4,12},{6,14},{8,16},{10,18},{12,20},{14,22},{16,24},... | collective-permute-start | bytes 3538952 | tf_op jit(solution)/shard_map/cond/branch_1_fun/ppermute | solution.py:273
  234.1 98.0 %collective-permute-start.29 = (bf16[68,128,128]{2,1,0:T(8,128)(2,1)}, bf16[68,128,128]{2,1,0:T(8,128)(2,1)}, u32[]{:S(2)}, u32[]{:S(2)}) collective-permute-start(bf16[68,128,128]{2,1,0:T(8,128)(2,1)} %collective-permute-done.27.refs_5_), channel_id=1, source_target_pairs={{0,2},{2,0},{4,6},{6,4},{8,10},{10,8},{12,14},{14,12},{16,18},{18,... | collective-permute-start | bytes 6684680 | tf_op jit(solution)/shard_map/cond/branch_1_fun/ppermute | solution.py:273
  235.9 96.2 %collective-permute-start.32 = (bf16[68,128,128]{2,1,0:T(8,128)(2,1)}, bf16[68,128,128]{2,1,0:T(8,128)(2,1)}, u32[]{:S(2)}, u32[]{:S(2)}) collective-permute-start(bf16[68,128,128]{2,1,0:T(8,128)(2,1)} %collective-permute-done.30.refs_9_), channel_id=1, source_target_pairs={{0,4},{2,6},{4,0},{6,2},{8,12},{10,14},{12,8},{14,10},{16,20},{18,... | collective-permute-start | bytes 6684680 | tf_op jit(solution)/shard_map/cond/branch_1_fun/ppermute | solution.py:273
  275.0 56.4 %collective-permute-start.42 = (bf16[38,128,128]{2,1,0:T(8,128)(2,1)S(1)}, bf16[38,128,128]{2,1,0:T(8,128)(2,1)}, u32[]{:S(2)}, u32[]{:S(2)}) collective-permute-start(bf16[38,128,128]{2,1,0:T(8,128)(2,1)S(1)} %fusion.535), channel_id=1, source_target_pairs={{0,8},{2,10},{4,12},{6,14},{8,16},{10,18},{12,20},{14,22},{16,24},... | collective-permute-start | bytes 3735560 | tf_op jit(solution)/shard_map/cond/branch_1_fun/ppermute | solution.py:273
  275.0 57.1 %collective-permute-start.24 = (bf16[36,128,128]{2,1,0:T(8,128)(2,1)S(1)}, bf16[36,128,128]{2,1,0:T(8,128)(2,1)S(1)}, u32[]{:S(2)}, u32[]{:S(2)}) collective-permute-start(bf16[36,128,128]{2,1,0:T(8,128)(2,1)S(1)} %collective-permute-done.23.refs_2_), channel_id=1, source_target_pairs={{0,8},{2,10},{4,12},{6,14},{8,16},{10,18},{12,20},{14,22},{16,24},... | collective-permute-start | bytes 3538952 | tf_op jit(solution)/shard_map/cond/branch_1_fun/ppermute | solution.py:273
  331.4 54.5 %collective-permute-start.43 = (bf16[38,128,128]{2,1,0:T(8,128)(2,1)}, bf16[38,128,128]{2,1,0:T(8,128)(2,1)}, u32[]{:S(2)}, u32[]{:S(2)}) collective-permute-start(bf16[38,128,128]{2,1,0:T(8,128)(2,1)} %collective-permute-done.42), channel_id=1, source_target_pairs={{0,8},{2,10},{4,12},{6,14},{8,16},{10,18},{12,20},{14,22},{16,24},... | collective-permute-start | bytes 3735560 | tf_op jit(solution)/shard_map/cond/branch_1_fun/ppermute | solution.py:273
  366.1 92.5 %collective-permute-start.39 = (bf16[72,128,128]{2,1,0:T(8,128)(2,1)}, bf16[72,128,128]{2,1,0:T(8,128)(2,1)}, u32[]{:S(2)}, u32[]{:S(2)}) collective-permute-start(bf16[72,128,128]{2,1,0:T(8,128)(2,1)} %pad_maximum_fusion.10.refs_12_), channel_id=1, source_target_pairs={{0,8},{2,10},{4,12},{6,14},{8,16},{10,18},{12,20},{14,22},{16,24},... | collective-permute-start | bytes 7077896 | tf_op jit(solution)/shard_map/cond/branch_1_fun/ppermute | solution.py:273
  386.0 68.0 %collective-permute-start.44 = (bf16[38,128,128]{2,1,0:T(8,128)(2,1)}, bf16[38,128,128]{2,1,0:T(8,128)(2,1)}, u32[]{:S(2)}, u32[]{:S(2)}) collective-permute-start(bf16[38,128,128]{2,1,0:T(8,128)(2,1)} %collective-permute-done.43), channel_id=1, source_target_pairs={{0,8},{2,10},{4,12},{6,14},{8,16},{10,18},{12,20},{14,22},{16,24},... | collective-permute-start | bytes 3735560 | tf_op jit(solution)/shard_map/cond/branch_1_fun/ppermute | solution.py:273
  415.3 45.2 %collective-permute-start.35 = (bf16[512,1536]{1,0:T(8,128)(2,1)}, bf16[512,1536]{1,0:T(8,128)(2,1)}, u32[]{:S(2)}, u32[]{:S(2)}) collective-permute-start(bf16[512,1536]{1,0:T(8,128)(2,1)} %convolution_convert_fusion.12), channel_id=1, source_target_pairs={{0,1},{1,0},{2,3},{3,2},{4,5},{5,4},{6,7},{7,6},{8,9},{9,8},{10,11... | collective-permute-start | bytes 4718600 | tf_op jit(solution)/shard_map/cond/branch_1_fun/ppermute | solution.py:427
  456.9 58.8 %collective-permute-start.45 = (bf16[76,128,128]{2,1,0:T(8,128)(2,1)}, bf16[76,128,128]{2,1,0:T(8,128)(2,1)}, u32[]{:S(2)}, u32[]{:S(2)}) collective-permute-start(bf16[76,128,128]{2,1,0:T(8,128)(2,1)} %pad_maximum_fusion.8.refs_16_), channel_id=1, source_target_pairs={{0,4},{2,6},{4,0},{6,2},{8,12},{10,14},{12,8},{14,10},{16,20},{18,... | collective-permute-start | bytes 7471112 | tf_op jit(solution)/shard_map/cond/branch_1_fun/ppermute | solution.py:273
  458.6 57.1 %collective-permute-start.48 = (bf16[76,128,128]{2,1,0:T(8,128)(2,1)}, bf16[76,128,128]{2,1,0:T(8,128)(2,1)}, u32[]{:S(2)}, u32[]{:S(2)}) collective-permute-start(bf16[76,128,128]{2,1,0:T(8,128)(2,1)} %pad_maximum_fusion.9.refs_20_), channel_id=1, source_target_pairs={{0,2},{2,0},{4,6},{6,4},{8,10},{10,8},{12,14},{14,12},{16,18},{18,... | collective-permute-start | bytes 7471112 | tf_op jit(solution)/shard_map/cond/branch_1_fun/ppermute | solution.py:273
  458.6 59.8 %collective-permute-start.40 = (bf16[72,128,128]{2,1,0:T(8,128)(2,1)}, bf16[72,128,128]{2,1,0:T(8,128)(2,1)}, u32[]{:S(2)}, u32[]{:S(2)}) collective-permute-start(bf16[72,128,128]{2,1,0:T(8,128)(2,1)} %collective-permute-done.39.refs_13_), channel_id=1, source_target_pairs={{0,8},{2,10},{4,12},{6,14},{8,16},{10,18},{12,20},{14,22},{16,24},... | collective-permute-start | bytes 7077896 | tf_op jit(solution)/shard_map/cond/branch_1_fun/ppermute | solution.py:273
  513.1 57.2 %collective-permute-start.46 = (bf16[76,128,128]{2,1,0:T(8,128)(2,1)}, bf16[76,128,128]{2,1,0:T(8,128)(2,1)}, u32[]{:S(2)}, u32[]{:S(2)}) collective-permute-start(bf16[76,128,128]{2,1,0:T(8,128)(2,1)} %pad_maximum_fusion.8.refs_16_), channel_id=1, source_target_pairs={{0,2},{2,0},{4,6},{6,4},{8,10},{10,8},{12,14},{14,12},{16,18},{18,... | collective-permute-start | bytes 7471112 | tf_op jit(solution)/shard_map/cond/branch_1_fun/ppermute | solution.py:273
  513.7 57.2 %collective-permute-start.49 = (bf16[76,128,128]{2,1,0:T(8,128)(2,1)}, bf16[76,128,128]{2,1,0:T(8,128)(2,1)}, u32[]{:S(2)}, u32[]{:S(2)}) collective-permute-start(bf16[76,128,128]{2,1,0:T(8,128)(2,1)} %pad_maximum_fusion.9.refs_20_), channel_id=1, source_target_pairs={{0,4},{2,6},{4,0},{6,2},{8,12},{10,14},{12,8},{14,10},{16,20},{18,... | collective-permute-start | bytes 7471112 | tf_op jit(solution)/shard_map/cond/branch_1_fun/ppermute | solution.py:273
  515.7 107.5 %collective-permute-start.47 = (bf16[76,128,128]{2,1,0:T(8,128)(2,1)}, bf16[76,128,128]{2,1,0:T(8,128)(2,1)}, u32[]{:S(2)}, u32[]{:S(2)}) collective-permute-start(bf16[76,128,128]{2,1,0:T(8,128)(2,1)} %collective-permute-done.45.refs_17_), channel_id=1, source_target_pairs={{0,2},{2,0},{4,6},{6,4},{8,10},{10,8},{12,14},{14,12},{16,18},{18,... | collective-permute-start | bytes 7471112 | tf_op jit(solution)/shard_map/cond/branch_1_fun/ppermute | solution.py:273
  515.7 108.1 %collective-permute-start.50 = (bf16[76,128,128]{2,1,0:T(8,128)(2,1)}, bf16[76,128,128]{2,1,0:T(8,128)(2,1)}, u32[]{:S(2)}, u32[]{:S(2)}) collective-permute-start(bf16[76,128,128]{2,1,0:T(8,128)(2,1)} %collective-permute-done.48.refs_21_), channel_id=1, source_target_pairs={{0,4},{2,6},{4,0},{6,2},{8,12},{10,14},{12,8},{14,10},{16,20},{18,... | collective-permute-start | bytes 7471112 | tf_op jit(solution)/shard_map/cond/branch_1_fun/ppermute | solution.py:273
  518.4 105.4 %collective-permute-start.41 = (bf16[72,128,128]{2,1,0:T(8,128)(2,1)}, bf16[72,128,128]{2,1,0:T(8,128)(2,1)}, u32[]{:S(2)}, u32[]{:S(2)}) collective-permute-start(bf16[72,128,128]{2,1,0:T(8,128)(2,1)} %collective-permute-done.40.refs_14_), channel_id=1, source_target_pairs={{0,8},{2,10},{4,12},{6,14},{8,16},{10,18},{12,20},{14,22},{16,24},... | collective-permute-start | bytes 7077896 | tf_op jit(solution)/shard_map/cond/branch_1_fun/ppermute | solution.py:273
  760.3 136.1 %collective-permute-start.51 = (bf16[512,1536]{1,0:T(8,128)(2,1)S(1)}, bf16[512,1536]{1,0:T(8,128)(2,1)S(1)}, u32[]{:S(2)}, u32[]{:S(2)}) collective-permute-start(bf16[512,1536]{1,0:T(8,128)(2,1)S(1)} %fusion.59), channel_id=1, source_target_pairs={{0,1},{1,0},{2,3},{3,2},{4,5},{5,4},{6,7},{7,6},{8,9},{9,8},{10,11... | collective-permute-start | bytes 4718600 | tf_op jit(solution)/shard_map/cond/branch_1_fun/ppermute | solution.py:427
  837.3 120.9 %collective-permute-start.83 = (bf16[4,19,128,128]{3,2,1,0:T(8,128)(2,1)}, bf16[4,19,128,128]{3,2,1,0:T(8,128)(2,1)}, u32[]{:S(2)}, u32[]{:S(2)}) collective-permute-start(bf16[4,19,128,128]{3,2,1,0:T(8,128)(2,1)} %bitcast.814), channel_id=1, source_target_pairs={{0,2},{2,0},{4,6},{6,4},{8,10},{10,8},{12,14},{14,12},{16,18},{18,... | collective-permute-start | bytes 7471112 | tf_op jit(solution)/shard_map/cond/branch_1_fun/ppermute | solution.py:273
  838.4 109.0 %collective-permute-start.81 = (bf16[4,19,128,128]{3,2,1,0:T(8,128)(2,1)}, bf16[4,19,128,128]{3,2,1,0:T(8,128)(2,1)}, u32[]{:S(2)}, u32[]{:S(2)}) collective-permute-start(bf16[4,19,128,128]{3,2,1,0:T(8,128)(2,1)} %bitcast.816), channel_id=1, source_target_pairs={{0,2},{2,0},{4,6},{6,4},{8,10},{10,8},{12,14},{14,12},{16,18},{18,... | collective-permute-start | bytes 7471112 | tf_op jit(solution)/shard_map/cond/branch_1_fun/ppermute | solution.py:273
  839.3 123.5 %collective-permute-start.86 = (bf16[4,19,128,128]{3,2,1,0:T(8,128)(2,1)}, bf16[4,19,128,128]{3,2,1,0:T(8,128)(2,1)}, u32[]{:S(2)}, u32[]{:S(2)}) collective-permute-start(bf16[4,19,128,128]{3,2,1,0:T(8,128)(2,1)} %bitcast.810), channel_id=1, source_target_pairs={{0,4},{2,6},{4,0},{6,2},{8,12},{10,14},{12,8},{14,10},{16,20},{18,... | collective-permute-start | bytes 7471112 | tf_op jit(solution)/shard_map/cond/branch_1_fun/ppermute | solution.py:273
  841.0 110.8 %collective-permute-start.84 = (bf16[4,19,128,128]{3,2,1,0:T(8,128)(2,1)}, bf16[4,19,128,128]{3,2,1,0:T(8,128)(2,1)}, u32[]{:S(2)}, u32[]{:S(2)}) collective-permute-start(bf16[4,19,128,128]{3,2,1,0:T(8,128)(2,1)} %bitcast.812), channel_id=1, source_target_pairs={{0,4},{2,6},{4,0},{6,2},{8,12},{10,14},{12,8},{14,10},{16,20},{18,... | collective-permute-start | bytes 7471112 | tf_op jit(solution)/shard_map/cond/branch_1_fun/ppermute | solution.py:273
  896.4 180.4 %collective-permute-start.90 = (bf16[2,2,20,128,128]{4,3,2,1,0:T(8,128)(2,1)}, bf16[2,2,20,128,128]{4,3,2,1,0:T(8,128)(2,1)}, u32[]{:S(2)}, u32[]{:S(2)}) collective-permute-start(bf16[2,2,20,128,128]{4,3,2,1,0:T(8,128)(2,1)} %bitcast.130), channel_id=1, source_target_pairs={{0,8},{2,10},{4,12},{6,14},{8,16},{10,18},{12,20},{14,22},{16,24},... | collective-permute-start | bytes 7864328 | tf_op jit(solution)/shard_map/cond/branch_1_fun/ppermute | solution.py:273
  951.8 206.7 %collective-permute-start.82 = (bf16[4,19,128,128]{3,2,1,0:T(8,128)(2,1)}, bf16[4,19,128,128]{3,2,1,0:T(8,128)(2,1)}, u32[]{:S(2)}, u32[]{:S(2)}) collective-permute-start(bf16[4,19,128,128]{3,2,1,0:T(8,128)(2,1)} %fusion.21), channel_id=1, source_target_pairs={{0,4},{2,6},{4,0},{6,2},{8,12},{10,14},{12,8},{14,10},{16,20},{18,... | collective-permute-start | bytes 7471112 | tf_op jit(solution)/shard_map/cond/branch_1_fun/ppermute | solution.py:273
  958.1 210.4 %collective-permute-start.85 = (bf16[4,19,128,128]{3,2,1,0:T(8,128)(2,1)}, bf16[4,19,128,128]{3,2,1,0:T(8,128)(2,1)}, u32[]{:S(2)}, u32[]{:S(2)}) collective-permute-start(bf16[4,19,128,128]{3,2,1,0:T(8,128)(2,1)} %fusion.19), channel_id=1, source_target_pairs={{0,2},{2,0},{4,6},{6,4},{8,10},{10,8},{12,14},{14,12},{16,18},{18,... | collective-permute-start | bytes 7471112 | tf_op jit(solution)/shard_map/cond/branch_1_fun/ppermute | solution.py:273
  1076.8 49.2 %collective-permute-start.55 = (bf16[512,1536]{1,0:T(8,128)(2,1)}, bf16[512,1536]{1,0:T(8,128)(2,1)}, u32[]{:S(2)}, u32[]{:S(2)}) collective-permute-start(bf16[512,1536]{1,0:T(8,128)(2,1)} %convolution_convert_fusion.9), channel_id=1, source_target_pairs={{0,1},{1,0},{2,3},{3,2},{4,5},{5,4},{6,7},{7,6},{8,9},{9,8},{10,11... | collective-permute-start | bytes 4718600 | tf_op jit(solution)/shard_map/cond/branch_1_fun/ppermute | solution.py:427
  1081.6 100.8 %collective-permute-start.91 = (bf16[2,2,20,128,128]{4,3,2,1,0:T(8,128)(2,1)}, bf16[2,2,20,128,128]{4,3,2,1,0:T(8,128)(2,1)}, u32[]{:S(2)}, u32[]{:S(2)}) collective-permute-start(bf16[2,2,20,128,128]{4,3,2,1,0:T(8,128)(2,1)} %fusion.17), channel_id=1, source_target_pairs={{0,8},{2,10},{4,12},{6,14},{8,16},{10,18},{12,20},{14,22},{16,24},... | collective-permute-start | bytes 7864328 | tf_op jit(solution)/shard_map/cond/branch_1_fun/ppermute | solution.py:273
  1186.9 117.1 %collective-permute-start.92 = (bf16[2,2,20,128,128]{4,3,2,1,0:T(8,128)(2,1)}, bf16[2,2,20,128,128]{4,3,2,1,0:T(8,128)(2,1)}, u32[]{:S(2)}, u32[]{:S(2)}) collective-permute-start(bf16[2,2,20,128,128]{4,3,2,1,0:T(8,128)(2,1)} %fusion.16), channel_id=1, source_target_pairs={{0,8},{2,10},{4,12},{6,14},{8,16},{10,18},{12,20},{14,22},{16,24},... | collective-permute-start | bytes 7864328 | tf_op jit(solution)/shard_map/cond/branch_1_fun/ppermute | solution.py:273
  1208.3 81.4 %collective-permute-start.88 = (bf16[38,128,128]{2,1,0:T(8,128)(2,1)}, bf16[38,128,128]{2,1,0:T(8,128)(2,1)}, u32[]{:S(2)}, u32[]{:S(2)}) collective-permute-start(bf16[38,128,128]{2,1,0:T(8,128)(2,1)} %add_convert_fusion.7), channel_id=1, source_target_pairs={{0,8},{2,10},{4,12},{6,14},{8,16},{10,18},{12,20},{14,22},{16,24},... | collective-permute-start | bytes 3735560 | tf_op jit(solution)/shard_map/cond/branch_1_fun/ppermute | solution.py:273
  1222.0 101.7 %collective-permute-start.62 = (bf16[2,2,13,128,128]{4,3,2,1,0:T(8,128)(2,1)}, bf16[2,2,13,128,128]{4,3,2,1,0:T(8,128)(2,1)}, u32[]{:S(2)}, u32[]{:S(2)}) collective-permute-start(bf16[2,2,13,128,128]{4,3,2,1,0:T(8,128)(2,1)} %bitcast.824), channel_id=1, source_target_pairs={{0,8},{2,10},{4,12},{6,14},{8,16},{10,18},{12,20},{14,22},{16,24},... | collective-permute-start | bytes 5111816 | tf_op jit(solution)/shard_map/cond/branch_1_fun/ppermute | solution.py:273
  1238.0 93.2 %collective-permute-start.72 = (bf16[4,14,128,128]{3,2,1,0:T(8,128)(2,1)}, bf16[4,14,128,128]{3,2,1,0:T(8,128)(2,1)}, u32[]{:S(2)}, u32[]{:S(2)}) collective-permute-start(bf16[4,14,128,128]{3,2,1,0:T(8,128)(2,1)} %bitcast.822), channel_id=1, source_target_pairs={{0,2},{2,0},{4,6},{6,4},{8,10},{10,8},{12,14},{14,12},{16,18},{18,... | collective-permute-start | bytes 5505032 | tf_op jit(solution)/shard_map/cond/branch_1_fun/ppermute | solution.py:273
  1239.1 88.3 %collective-permute-start.75 = (bf16[4,14,128,128]{3,2,1,0:T(8,128)(2,1)}, bf16[4,14,128,128]{3,2,1,0:T(8,128)(2,1)}, u32[]{:S(2)}, u32[]{:S(2)}) collective-permute-start(bf16[4,14,128,128]{3,2,1,0:T(8,128)(2,1)} %bitcast.823), channel_id=1, source_target_pairs={{0,4},{2,6},{4,0},{6,2},{8,12},{10,14},{12,8},{14,10},{16,20},{18,... | collective-permute-start | bytes 5505032 | tf_op jit(solution)/shard_map/cond/branch_1_fun/ppermute | solution.py:273
  1289.7 46.2 %collective-permute-start.77 = (bf16[4,14,128,128]{3,2,1,0:T(8,128)(2,1)}, bf16[4,14,128,128]{3,2,1,0:T(8,128)(2,1)}, u32[]{:S(2)}, u32[]{:S(2)}) collective-permute-start(bf16[4,14,128,128]{3,2,1,0:T(8,128)(2,1)} %bitcast.821), channel_id=1, source_target_pairs={{0,4},{2,6},{4,0},{6,2},{8,12},{10,14},{12,8},{14,10},{16,20},{18,... | collective-permute-start | bytes 5505032 | tf_op jit(solution)/shard_map/cond/branch_1_fun/ppermute | solution.py:273
  1323.8 42.9 %collective-permute-start.74 = (bf16[4,14,128,128]{3,2,1,0:T(8,128)(2,1)S(1)}, bf16[4,14,128,128]{3,2,1,0:T(8,128)(2,1)S(1)}, u32[]{:S(2)}, u32[]{:S(2)}) collective-permute-start(bf16[4,14,128,128]{3,2,1,0:T(8,128)(2,1)S(1)} %bitcast.820), channel_id=1, source_target_pairs={{0,2},{2,0},{4,6},{6,4},{8,10},{10,8},{12,14},{14,12},{16,18},{18,... | collective-permute-start | bytes 5505032 | tf_op jit(solution)/shard_map/cond/branch_1_fun/ppermute | solution.py:273
  1327.5 46.4 %collective-permute-start.93 = (bf16[2,20,128,128]{3,2,1,0:T(8,128)(2,1)S(1)}, bf16[2,20,128,128]{3,2,1,0:T(8,128)(2,1)S(1)}, u32[]{:S(2)}, u32[]{:S(2)}) collective-permute-start(bf16[2,20,128,128]{3,2,1,0:T(8,128)(2,1)S(1)} %get-tuple-element.383), channel_id=1, source_target_pairs={{0,4},{2,6},{4,0},{6,2},{8,12},{10,14},{12,8},{14,10},{16,20},{18,... | collective-permute-start | bytes 3932168 | tf_op jit(solution)/shard_map/cond/branch_1_fun/ppermute | solution.py:273
  1333.8 72.2 %collective-permute-start.76 = (bf16[4,14,128,128]{3,2,1,0:T(8,128)(2,1)S(1)}, bf16[4,14,128,128]{3,2,1,0:T(8,128)(2,1)S(1)}, u32[]{:S(2)}, u32[]{:S(2)}) collective-permute-start(bf16[4,14,128,128]{3,2,1,0:T(8,128)(2,1)S(1)} %fusion.32), channel_id=1, source_target_pairs={{0,2},{2,0},{4,6},{6,4},{8,10},{10,8},{12,14},{14,12},{16,18},{18,... | collective-permute-start | bytes 5505032 | tf_op jit(solution)/shard_map/cond/branch_1_fun/ppermute | solution.py:273
  1335.9 71.1 %collective-permute-start.73 = (bf16[4,14,128,128]{3,2,1,0:T(8,128)(2,1)S(1)}, bf16[4,14,128,128]{3,2,1,0:T(8,128)(2,1)S(1)}, u32[]{:S(2)}, u32[]{:S(2)}) collective-permute-start(bf16[4,14,128,128]{3,2,1,0:T(8,128)(2,1)S(1)} %fusion.34), channel_id=1, source_target_pairs={{0,4},{2,6},{4,0},{6,2},{8,12},{10,14},{12,8},{14,10},{16,20},{18,... | collective-permute-start | bytes 5505032 | tf_op jit(solution)/shard_map/cond/branch_1_fun/ppermute | solution.py:273
  1373.8 62.6 %collective-permute-start.64 = (bf16[2,2,13,128,128]{4,3,2,1,0:T(8,128)(2,1)S(1)}, bf16[2,2,13,128,128]{4,3,2,1,0:T(8,128)(2,1)S(1)}, u32[]{:S(2)}, u32[]{:S(2)}) collective-permute-start(bf16[2,2,13,128,128]{4,3,2,1,0:T(8,128)(2,1)S(1)} %fusion.35), channel_id=1, source_target_pairs={{0,8},{2,10},{4,12},{6,14},{8,16},{10,18},{12,20},{14,22},{16,24},... | collective-permute-start | bytes 5111816 | tf_op jit(solution)/shard_map/cond/branch_1_fun/ppermute | solution.py:273
  1374.1 42.6 %collective-permute-start.94 = (bf16[20,128,128]{2,1,0:T(8,128)(2,1)S(1)}, bf16[20,128,128]{2,1,0:T(8,128)(2,1)S(1)}, u32[]{:S(2)}, u32[]{:S(2)}) collective-permute-start(bf16[20,128,128]{2,1,0:T(8,128)(2,1)S(1)} %fusion.125), channel_id=1, source_target_pairs={{0,2},{2,0},{4,6},{6,4},{8,10},{10,8},{12,14},{14,12},{16,18},{18,... | collective-permute-start | bytes 1966088 | tf_op jit(solution)/shard_map/cond/branch_1_fun/ppermute | solution.py:273
  1407.9 45.5 %collective-permute-start.78 = (bf16[28,128,128]{2,1,0:T(8,128)(2,1)S(1)}, bf16[28,128,128]{2,1,0:T(8,128)(2,1)S(1)}, u32[]{:S(2)}, u32[]{:S(2)}) collective-permute-start(bf16[28,128,128]{2,1,0:T(8,128)(2,1)S(1)} %pad_maximum_fusion.21), channel_id=1, source_target_pairs={{0,8},{2,10},{4,12},{6,14},{8,16},{10,18},{12,20},{14,22},{16,24},... | collective-permute-start | bytes 2752520 | tf_op jit(solution)/shard_map/cond/branch_1_fun/ppermute | solution.py:273
  1438.3 44.2 %collective-permute-start.65 = (bf16[2,13,128,128]{3,2,1,0:T(8,128)(2,1)S(1)}, bf16[2,13,128,128]{3,2,1,0:T(8,128)(2,1)S(1)}, u32[]{:S(2)}, u32[]{:S(2)}) collective-permute-start(bf16[2,13,128,128]{3,2,1,0:T(8,128)(2,1)S(1)} %get-tuple-element.387), channel_id=1, source_target_pairs={{0,4},{2,6},{4,0},{6,2},{8,12},{10,14},{12,8},{14,10},{16,20},{18,... | collective-permute-start | bytes 2555912 | tf_op jit(solution)/shard_map/cond/branch_1_fun/ppermute | solution.py:273
  1490.6 61.2 %collective-permute-start.80 = (bf16[28,128,128]{2,1,0:T(8,128)(2,1)S(1)}, bf16[28,128,128]{2,1,0:T(8,128)(2,1)S(1)}, u32[]{:S(2)}, u32[]{:S(2)}) collective-permute-start(bf16[28,128,128]{2,1,0:T(8,128)(2,1)S(1)} %add_convert_fusion.10), channel_id=1, source_target_pairs={{0,8},{2,10},{4,12},{6,14},{8,16},{10,18},{12,20},{14,22},{16,24},... | collective-permute-start | bytes 2752520 | tf_op jit(solution)/shard_map/cond/branch_1_fun/ppermute | solution.py:273
  (237 other events, 3509.3 us)
Sparse Core Ops, SparseCore 0:
  76.1 146.9 all-reduce.14

commit v2 on v1

--- a/solution.py
+++ b/solution.py
@@ -359,13 +359,10 @@
     )
 
 
-def scatter_plane(terms, sizes, order):
+def scatter_plane(parts, sizes, order):
     first, second = order
-    sums = [None] * sizes[second]
-    for at in [*range(1, sizes[second]), 0]:
-        sums[at] = added(
-            *(yield from ring([terms(step, at) for step in range(sizes[first])], sizes, first))
-        )
+    came, here = yield from ring(parts, sizes, first)
+    sums = [added(came[at], here[at]) for at in range(sizes[second])]
     return (yield from ring(sums, sizes, second))
 
 
@@ -390,18 +387,18 @@
         self.running[name] = one
         self.moving[name] = next(one)
 
-    def tick(self, names, *others):
+    def tick(self, names, value=None):
         names = [name for name in names if name in self.running]
         came = [self.moving[name] for name in names]
-        if others:
-            came, others = lax.optimization_barrier((came, others))
+        if value is not None and names:
+            value = value + nothing(*sum(came, [])).astype(value.dtype)
         for name, blocks in zip(names, came):
             try:
                 self.moving[name] = self.running[name].send(blocks)
             except StopIteration as done:
                 self.results[name] = done.value
                 del self.running[name]
-        return others[0] if len(others) == 1 else others
+        return value
 
     def finish(self, names):
         while any(name in self.running for name in names):
@@ -569,20 +566,31 @@
 
 
 def adam_slots(
-    begin, end, into, tables, dmod, local, kind_of, over_at, rate, sums, over_sums, *state
+    begin, skipped, into, tables, dmod, local, kind_of, over_at, rate, sums, over_sums, *state
 ):
     capacity = state[0].shape[0]
     per = adam_block(capacity)
 
+    def block_at(step, skip_ref):
+        block = step + begin // per
+        return jnp.where(
+            (block >= skip_ref[0]) & (block < skip_ref[1]),
+            jnp.where(skip_ref[1] < capacity // per, skip_ref[1], skip_ref[0] - 1),
+            block,
+        )
+
+
     def kernel(*refs):
-        local_ref, kind_ref, over_ref, rate_ref = refs[:4]
-        cond_ref, spread_ref, chunk_ref, dmod_ref, over_sums_ref, sums_ref = refs[4:10]
-        master_ref, first_ref, second_ref = refs[10:13]
+        skip_ref, local_ref, kind_ref, over_ref, rate_ref = refs[:5]
+        cond_ref, spread_ref, chunk_ref, dmod_ref, over_sums_ref, sums_ref = refs[5:11]
+        master_ref, first_ref, second_ref = refs[11:14]
         *outs, grad_ref = refs[-4:]
-        step = pl.program_id(0) + begin // per
+        step = pl.program_id(0)
+        block = block_at(step, skip_ref)
+        is_new = (step == 0) | (block != block_at(step - 1, skip_ref))
         for at in range(per):
-            slot = step * per + at
-            kind = kind_ref[slot]
+            slot = block * per + at
+            kind = jnp.where(is_new, kind_ref[slot], -1)
 
             @pl.when(kind == 0)
             def _():
@@ -603,39 +611,51 @@
                     factors, dmod_ref[...].astype(jnp.bfloat16), preferred_element_type=jnp.float32
                 )
 
-            results = adam_step(
-                master_ref[at], first_ref[at], second_ref[at], grad_ref[...], rate_ref[slot]
-            )
-            for out, result in zip(outs, results):
-                out[at] = result
+            @pl.when(is_new)
+            def _():
+                results = adam_step(
+                    master_ref[at], first_ref[at], second_ref[at], grad_ref[...], rate_ref[slot]
+                )
+                for out, result in zip(outs, results):
+                    out[at] = result
 
     whole = pl.BlockSpec(memory_space=pltpu.VMEM)
-    sums_block = pl.BlockSpec((per, TS, TS), lambda i, *_: (i, 0, 0))
-    block = pl.BlockSpec((per, TS, TS), lambda i, *_: (i + begin // per, 0, 0))
+    block = pl.BlockSpec((per, TS, TS), lambda i, skip_ref, *_: (block_at(i, skip_ref), 0, 0))
     return pl.pallas_call(
         kernel,
         out_shape=[jax.ShapeDtypeStruct(state[0].shape, jnp.float32)] * 3,
         grid_spec=pltpu.PrefetchScalarGridSpec(
-            num_scalar_prefetch=4,
-            grid=((end - begin) // per,),
+            num_scalar_prefetch=5,
+            grid=((capacity - begin) // per,),
             in_specs=[whole] * 5
-            + [sums_block]
-            + [block] * 3
+            + [block] * 4
             + [pl.BlockSpec(memory_space=pl.ANY)] * len(into),
             out_specs=[block] * 3,
             scratch_shapes=[pltpu.VMEM((TS, TS), jnp.float32)],
         ),
-        input_output_aliases={13 + number: number for number in range(len(into))},
+        input_output_aliases={14 + number: number for number in range(len(into))},
         compiler_params=pltpu.CompilerParams(
             dimension_semantics=("arbitrary",), vmem_limit_bytes=VMEM_BYTES
         ),
         cost_estimate=pl.CostEstimate(
             flops=80 * spread_flops(tables),
-            bytes_accessed=26 * (end - begin) * TS * TS,
+            bytes_accessed=13 * (capacity + begin) * TS * TS,
             transcendentals=0,
         ),
         name="adam_slots",
-    )(local, kind_of, over_at, rate, *tables, dmod, over_sums, sums, *state, *into)
+    )(
+        jnp.stack(skipped).astype(jnp.int32),
+        local,
+        kind_of,
+        over_at,
+        rate,
+        *tables,
+        dmod,
+        over_sums,
+        sums,
+        *state,
+        *into,
+    )
 
 
 def spread_flops(tables):
@@ -909,6 +929,7 @@
     resid_zero = flat(x_in).astype(jnp.float32)
     normed_one, inverse_one = layer_norm(resid_zero)
     input_one = (normed_one * (1.0 + scales[0]) + shifts[0]).astype(jnp.bfloat16)
+    second = [("pair", 1), ("rest", 1)] if compact else []
     proj_qkv = by_micro(matmul(input_one, w_qkv).astype(jnp.bfloat16))
     queries = proj_qkv[:, :, :head_cols]
     kv_ext = padded(proj_qkv[:, :, head_cols:], (("seq", 1),), WIN)
@@ -951,47 +972,53 @@
     pool_ff = as_tiles(matmul(input_three.T, dglu), pool_ff, offsets[5])
     slots = listed_tiles(owner_row, rank, devices, cut_two)
 
-    def start_scatter(number, pool, listed, gate=()):
+    def start_scatter(number, pool, listed, extra=None, before=()):
         first, middle, second, last = scatter_parts[number]
         wanted = jnp.concatenate(
             [slots.reshape(*sizes, cut_two), by_home(listed)], axis=3
         )
         if number:
             wanted = jnp.maximum(wanted, attn_tiles)
-        taken = []
-
-        def pick(places, *before):
-            return pool[places + nothing(*before)]
-
-
-        def plane(low, high, order):
-            here = wanted[..., low:high].transpose(*order, 0, 3)
-            sent = [
-                [pick(here[step, at], *gate) for at in range(sizes[order[1]])]
-                for step in range(1, sizes[order[0]])
+        home = wanted[..., cut_two:]
+        planes = [
+            (wanted[..., first:middle].transpose(2, 1, 0, 3), 2),
+            (wanted[..., middle:second].transpose(1, 2, 0, 3), 1),
+            (jnp.concatenate([wanted[..., second:last], home], axis=3), 0),
+        ]
+
+        def pick(parts, *before):
+            flats = [part.reshape(-1) for part in parts]
+            tiles = pool[jnp.concatenate(flats) + nothing(*before)]
+            edges = np.cumsum([0] + [flat.shape[0] for flat in flats])
+            return [
+                tiles[edges[at] : edges[at + 1]].reshape(*part.shape, TS, TS)
+                for at, part in enumerate(parts)
             ]
-            kept = pick(here[0], *(() if gate else sum(sent, [])))
-            taken.extend([*sum(sent, []), kept])
-            return lambda step, at: sent[step - 1][at] if step else kept[at]
-
-        one, two = plane(first, middle, (2, 1)), plane(middle, second, (1, 2))
-        here = jnp.concatenate([wanted[..., second:last], wanted[..., cut_two:]], axis=3)
-        sent = pick(here[1], *gate)
-        kept = pick(jnp.concatenate([here[:1], here[2:]]), *(() if gate else (sent,)))
-        taken.extend([sent, kept])
+
+        sent = pick([places[1] for places, _ in planes])
+        kept = [jnp.concatenate([places[:1], places[2:]]) for places, _ in planes]
+        kept = pick(kept, sent[0], *before)
+        taken = sent + kept
+        if extra is not None:
+            sent[2] = jnp.concatenate([sent[2], extra[1]], axis=2)
+            kept[2] = jnp.concatenate([kept[2], jnp.concatenate([extra[:1], extra[2:]])], axis=3)
+        parts = [[kept[at][0], sent[at], *kept[at][1:]] for at in range(3)]
+        one, two, three = parts
         ticks.start(("pair", number), scatter_pair(one, two, sizes))
         ticks.start(
             ("rest", number),
-            scatter_ticks(
-                lambda step: sent if step == 1 else kept[max(step - 1, 0)], sizes, (0, 1, 2)
-            ),
+            scatter_ticks(lambda step: three[step], sizes, (0, 1, 2)),
         )
         return taken
 
-    def start_out(number):
-        total = ticks.finish([("rest", number)])[0]
-        total = total[scatter_parts[number][3] - scatter_parts[number][2] :]
-        ticks.start(("out", number), gather_ticks(total, sizes, (0, 1, 2)))
+    def hand_out():
+        totals = [
+            ticks.finish([("rest", number)])[0][scatter_parts[number][3] - scatter_parts[number][2] :]
+            for number in range(2)
+        ]
+        block = jnp.concatenate(totals, axis=0)
+        ticks.start("out", gather_ticks(block, sizes, (0, 1, 2)))
+        return jnp.concatenate(ticks.finish(["out"])[0], axis=0)
 
     if compact:
         taken = start_scatter(1, pool_ff, over_tile[spare[0] :])
@@ -1020,7 +1047,7 @@
     back_two, dscale_two, dshift_two = norm_back(
         head_sum(matmul(dquery_two, w_cq.T)), normed_two, inverse_two, scales[1]
     )
-    grad_one = grad_two + back_two
+    grad_one = ticks.tick(second[1:], grad_two + back_two)
     grad_low = grad_one.astype(jnp.bfloat16)
     pool = as_tiles(matmul(flat(attended).T, grad_low), pool, offsets[1])
     grad_attended = by_micro(matmul(grad_low, w_out.T).astype(jnp.bfloat16))
@@ -1033,16 +1060,17 @@
         grad_attended,
         local_heads,
     )
-    dkv_ext = jnp.concatenate([dkey_ext, dvalue_ext], axis=2)
+    dkv_ext = ticks.tick(second, jnp.concatenate([dkey_ext, dvalue_ext], axis=2))
     rims = jnp.concatenate([dkv_ext[:, :WIN], dkv_ext[:, row_count + WIN :]], axis=1)
     returned = padded(rims.astype(jnp.bfloat16), (("seq", 1),), WIN).astype(jnp.float32)
     dkv_own = dkv_ext[:, WIN : row_count + WIN]
     dkv_own = dkv_own.at[:, :WIN].add(returned[:, :WIN])
     dkv_own = dkv_own.at[:, row_count - WIN :].add(returned[:, 3 * WIN :])
     dqkv = flat(jnp.concatenate([dquery_one, dkv_own], axis=2).astype(jnp.bfloat16))
+    dqkv = ticks.tick(second, dqkv)
     pool = as_tiles(matmul(input_one.T, dqkv), pool, offsets[0])
     back_one, dscale_one, dshift_one = norm_back(
-        head_sum(matmul(dqkv, w_qkv.T)), normed_one, inverse_one, scales[0]
+        ticks.tick(second, head_sum(matmul(dqkv, w_qkv.T))), normed_one, inverse_one, scales[0]
     )
     grad_input = by_micro(grad_one + back_one)
 
@@ -1061,22 +1089,23 @@
         axis=1,
     )
     dmod = lax.dynamic_slice_in_dim(dmod, lax.axis_index("head") * mod_cols, mod_cols, 1)
-    ticks.start("dmod", sum_ticks(dmod, sizes))
-    (dmod,) = ticks.finish(["dmod"])
-    gate = [dmod]
+    dmod = (
+        dmod.reshape(micro_count * clip_count, mod_cols // TS, TS)
+        .transpose(1, 0, 2)
+        .reshape(-1, TS)
+    )
+    gate = [dqkv]
     if compact:
-        gate = start_scatter(0, pool, over_tile[: spare[0]], [dmod])
-        start_out(1)
-        ticks.finish([("out", 1)])
+        each = dmod.shape[0] // seq_count
+        extra = dmod.astype(jnp.bfloat16).reshape(seq_count, each, TS)[devices]
+        extra = jnp.pad(extra, ((0, 0), (0, TS - each), (0, 0))).reshape(*sizes, 1, TS, TS)
+        ticks.tick(second)
+        before = sum([ticks.moving[name] for name in second if name in ticks.running], [])
+        gate = start_scatter(0, pool, over_tile[: spare[0]], extra, before)
+    else:
+        dmod = lax.psum(dmod, "seq")
     late = (hidden.astype(jnp.float32) + nothing(gate[0]).astype(jnp.float32)).astype(jnp.bfloat16)
     out_block = by_micro((resid_two + head_sum(matmul(late, w_down))).astype(jnp.bfloat16))
-    dmod = (
-        dmod
-        .reshape(micro_count * clip_count, mod_cols // TS, TS)
-        .transpose(1, 0, 2)
-        .reshape(-1, TS)
-    )
-
     state = (own, first_moment[0], second_moment[0])
     rate = slot_rates(slot_tile, shapes)
     if compact:
@@ -1084,54 +1113,45 @@
         slot_over = jnp.any(over_slot, axis=1)
         over_at = jnp.sum(jnp.where(over_slot, over_place[None, :], 0), axis=1)
         kind_of = jnp.where(is_mod, 3, jnp.where(slot_over, 2, slot_used.astype(jnp.int32)))
-        slot = first_pass_slot(cut_one, capacity)
 
         def sums_of(number):
             first, _, second, last = scatter_parts[number]
             pair, rest = ticks.finish([("pair", number), ("rest", number)])
             return [pair, rest[: last - second]]
 
-        def over_sums_of(number):
-            each = spare[number] // seq_count
-            place = over_at - (spare[0] if number else 0)
-            steps, at = home_of(place, each)
-            block = (steps[2] * sizes[1] + steps[1]) * sizes[0] + steps[0]
-            (sums,) = ticks.finish([("out", number)])
-            return jnp.concatenate(sums, axis=0), block * each + at
-
-        later = jnp.concatenate(
-            [*sums_of(1), jnp.zeros((capacity - cut_two, TS, TS), jnp.bfloat16)], axis=0
-        )
-        over_sums, over_index = over_sums_of(1)
+        over_sums = hand_out()
+        each = [count // seq_count for count in spare]
+        width = sum(each) + 1
+
+        def home_block(steps):
+            return (steps[2] * sizes[1] + steps[1]) * sizes[0] + steps[0]
+
+        homes = home_block(home_of(np.arange(seq_count), 1)[0])
+        count = dmod.shape[0] // seq_count
+        dmod = over_sums[homes * width + each[0], :count].reshape(dmod.shape)
+        steps, at = home_of(over_at, each[0])
+        index = home_block(steps) * width + at
+        steps, at = home_of(over_at - spare[0], each[1])
+        other = home_block(steps) * width + each[0] + 1 + at
+        index = jnp.where(over_at < spare[0], index, other)
         results = adam_slots(
-            slot,
-            capacity,
+            0,
+            (jnp.int32(0), jnp.int32(0)),
             (),
             tables,
-            dmod,
+            dmod.astype(jnp.float32),
             local,
             kind_of,
-            jnp.clip(over_index, 0, over_sums.shape[0] - 1),
+            jnp.clip(index, 0, over_sums.shape[0] - 1),
             rate,
-            later[slot - cut_one :],
-            over_sums,
-            *state,
-        )
-        ticks.finish([("rest", 0)])
-        start_out(0)
-        sooner = jnp.concatenate([*sums_of(0), later[: slot - cut_one]], axis=0)
-        over_sums, over_index = over_sums_of(0)
-        results = adam_slots(
-            0,
-            slot,
-            results,
-            tables,
-            dmod,
-            local,
-            kind_of,
-            jnp.clip(over_index, 0, over_sums.shape[0] - 1),
-            rate,
-            sooner,
+            jnp.concatenate(
+                [
+                    *sums_of(0),
+                    *sums_of(1),
+                    jnp.zeros((capacity - cut_two, TS, TS), jnp.bfloat16),
+                ],
+                axis=0,
+            ),
             over_sums,
             *state,
         )
@@ -1144,7 +1164,7 @@
         )
         results = adam_slots(
             0,
-            capacity,
+            (jnp.int32(0), jnp.int32(0)),
             (),
             tables,
             dmod,

time: 1600 us -> 1560 us (0.975)
  waiting for transfers between devices: 563 us -> 535 us
    ppermute x76 -> x62, waiting for transfers between devices: 536 us -> 481 us  [ring_send(): return lax.ppermute(block, 'seq', pairs)]
    slice x14 -> x23, local copies, waits for them, and re-layouts: 23.3 us -> 50.8 us  [the longest x6 29.2 us: pick(): tiles[edges[at]:edges[at + 1]].reshape(*part.shape, TS, TS)]
    gather x16 -> x6, local copies, waits for them, and re-layouts: 91.5 us -> 67.4 us  [the longest x4 64.9 us: pick(): tiles = pool[jnp.concatenate(flats) + nothing(*before)]]
    ppermute x2, waiting for transfers between devices: 2.91 us -> 19.6 us  [padded(): after = lax.ppermute(initial, axis, down)]
    ppermute x76 -> x62, starting transfers between devices: 75.1 us -> 60.2 us  [ring_send(): return lax.ppermute(block, 'seq', pairs)]
    convert_element_type x33 -> x27, other arithmetic: 61.3 us -> 71.8 us  [added(): (left.astype(jnp.float32) + right.astype(jnp.float32)).astype(jnp.bfloat16)]
    pallas_call x2 -> x1, Pallas kernels: 47.2 us -> 51.7 us  [adam_slots(): pl.pallas_call(kernel, out_shape=[jax.ShapeDtypeStruct(state[0].shape, jn...]
  transfers between devices with their start and end apart: 87 -> 73, of which waited for: 43 -> 32; matrix products, arithmetic and copies ran while one was open for 35% -> 36% of each run, Pallas kernels for 8% -> 6%
where the time goes in v2:
time: 1560 us; the launch traced here: 1550 us
  waiting for transfers between devices  535 us (34%)
  local copies, waits for them, and re-layouts  258 us (17%)
  Pallas kernels  238 us (15%)
  other arithmetic  199 us (13%)
  matrix products  188 us (12%)
  starting transfers between devices  70.9 us (5%)
  loops' own time  34.9 us (2%)
  between operations  17.1 us (1%)
    ppermute x62, waiting for transfers between devices, ring_send(): return lax.ppermute(block, 'seq', pairs)  481 us
    dot_general x20, matrix products, matmul(): return jnp.dot(left, right, preferred_element_type=jnp.float32)  119 us
    pallas_call x7, Pallas kernels, fetch_matrix(): pl.pallas_call(kernel, out_shape=jax.ShapeDtypeStruct((row_count, col_cou...  107 us
    convert_element_type x27, other arithmetic, added(): (left.astype(jnp.float32) + right.astype(jnp.float32)).astype(jnp.bfloat16)  71.8 us
    gather x4, local copies, waits for them, and re-layouts, pick(): tiles = pool[jnp.concatenate(flats) + nothing(*before)]  64.9 us
    ppermute x62, starting transfers between devices, ring_send(): return lax.ppermute(block, 'seq', pairs)  60.2 us
    pallas_call x7, Pallas kernels, as_tiles(): pl.pallas_call(kernel, out_shape=jax.ShapeDtypeStruct((into if is_new els...  60.1 us
    pallas_call x1, Pallas kernels, adam_slots(): pl.pallas_call(kernel, out_shape=[jax.ShapeDtypeStruct(state[0].shape, jn...  51.7 us
  transfers between devices with their start and end apart: 73, of which 32 were waited for; matrix products, arithmetic and copies ran while one was open for 36% of the time, Pallas kernels for 6%

profile of v2, /device:TPU:0, one launch (start us, length us, event | category | flops | bytes accessed | tf_op | source)
XLA Modules:
  0.0 1546.0 jit_solution(9085805947484054603)
XLA Ops:
  26.7 12.3 collective-permute-done.81
  39.6 1499.3 %conditional.1 = (bf16[2,256,1536]{2,1,0:T(8,128)(2,1)}, f32[2,256,1536]{2,1,0:T(8,128)}, f32[1,141,128,128]{3,2,1,0:T(8,128)}, f32[1,141,128,128]{3,2,1,0:T(8,128)}, f32[1,141,128,128]{3,2,1,0:T(8,128)}) conditional(s32[]{:T(128)} %convert_element_type.1340, (bf16[2,256,1536]{2,1,0:T(8,128)(2,1)S(1)}, s32[2,8]{1,0:T(2,128)S(1)}, ...), branch_computations={%region_11.45_spmd, %region_45.82_spmd} | conditional | flops 76979298304 | bytes 2855730176 | solution.py:1194
  57.0 19.4 %mod_product.3 = f32[576,128]{1,0:T(8,128)S(1)} custom-call(s32[2]{0:T(128)S(1)} %pad_add_fusion.8.meta_ref, s32[141]{0:T(256)S(1)} %get-tuple-element.558.local_ref.refs_1_, f32[1544,16]{1,0:T(8,128)S(1)} %pad_convert_fusion.cond_ref.refs_5_, bf16[16,576]{1,0:T(8,128)(2,1)S(1)} %get-tuple-element.143.spread_ref.refs_6_, ...), custom_call_target="tpu_custom_call" | custom-call | flops 754974720 | bytes 2621440 | tf_op jit(solution)/shard_map/cond/branch_1_fun/mod_product/pallas_call | solution.py:548
  99.2 9.5 collective-permute-done.10
  111.0 9.8 collective-permute-done.11
  138.3 23.5 %collective-permute-done.14 = bf16[3,128,128]{2,1,0:T(8,128)(2,1)S(1)} collective-permute-done((bf16[3,128,128]{2,1,0:T(8,128)(2,1)S(1)}, bf16[3,128,128]{2,1,0:T(8,128)(2,1)S(1)}, u32[]{:S(2)}, u32[]{:S(2)}) %collective-permute-start.14) | collective-permute-done | bytes 98336 | tf_op jit(solution)/shard_map/cond/branch_1_fun/ppermute | solution.py:273
  177.0 10.6 collective-permute-done.16
  200.3 15.6 %collective-permute-done.17.refs_1_ = bf16[36,128,128]{2,1,0:T(8,128)(2,1)S(1)} collective-permute-done((bf16[36,128,128]{2,1,0:T(8,128)(2,1)S(1)}, bf16[36,128,128]{2,1,0:T(8,128)(2,1)S(1)}, u32[]{:S(2)}, u32[]{:S(2)}) %collective-permute-start.17) | collective-permute-done | bytes 1179680 | tf_op jit(solution)/shard_map/cond/branch_1_fun/ppermute | solution.py:273
  229.0 7.4 collective-permute-done.22.refs_5_
  246.7 30.5 %collective-permute-done.23.refs_6_ = bf16[68,128,128]{2,1,0:T(8,128)(2,1)} collective-permute-done((bf16[68,128,128]{2,1,0:T(8,128)(2,1)}, bf16[68,128,128]{2,1,0:T(8,128)(2,1)}, u32[]{:S(2)}, u32[]{:S(2)}) %collective-permute-start.23) | collective-permute-done | bytes 2228256 | tf_op jit(solution)/shard_map/cond/branch_1_fun/ppermute | solution.py:273
  277.7 10.6 fusion.259
  299.0 35.1 %collective-permute-done.32 = bf16[18,128,128]{2,1,0:T(8,128)(2,1)S(1)} collective-permute-done((bf16[18,128,128]{2,1,0:T(8,128)(2,1)S(1)}, bf16[18,128,128]{2,1,0:T(8,128)(2,1)S(1)}, u32[]{:S(2)}, u32[]{:S(2)}) %collective-permute-start.32) | collective-permute-done | bytes 589856 | tf_op jit(solution)/shard_map/cond/branch_1_fun/ppermute | solution.py:273
  334.6 12.6 fetch_matrix.21
  439.9 17.9 %collective-permute-done.39 = bf16[38,128,128]{2,1,0:T(8,128)(2,1)} collective-permute-done((bf16[38,128,128]{2,1,0:T(8,128)(2,1)}, bf16[38,128,128]{2,1,0:T(8,128)(2,1)}, u32[]{:S(2)}, u32[]{:S(2)}) %collective-permute-start.39) | collective-permute-done | bytes 1245216 | tf_op jit(solution)/shard_map/cond/branch_1_fun/ppermute | solution.py:273
  504.2 13.7 collective-permute-done.40.refs_17_
  544.9 28.1 %collective-permute-done.41.refs_18_ = bf16[76,128,128]{2,1,0:T(8,128)(2,1)} collective-permute-done((bf16[76,128,128]{2,1,0:T(8,128)(2,1)}, bf16[76,128,128]{2,1,0:T(8,128)(2,1)}, u32[]{:S(2)}, u32[]{:S(2)}) %collective-permute-start.41) | collective-permute-done | bytes 2490400 | tf_op jit(solution)/shard_map/cond/branch_1_fun/ppermute | solution.py:273
  573.1 47.1 %collective-permute-done.42.refs_19_ = bf16[76,128,128]{2,1,0:T(8,128)(2,1)} collective-permute-done((bf16[76,128,128]{2,1,0:T(8,128)(2,1)}, bf16[76,128,128]{2,1,0:T(8,128)(2,1)}, u32[]{:S(2)}, u32[]{:S(2)}) %collective-permute-start.42) | collective-permute-done | bytes 2490400 | tf_op jit(solution)/shard_map/cond/branch_1_fun/ppermute | solution.py:273
  620.2 51.8 %fetch_matrix.26 = bf16[1536,6144]{1,0:T(8,128)(2,1)} custom-call(s32[576]{0:T(1024)S(1)} %slice.1008.source_ref, s32[576]{0:T(1024)S(1)} %slice.1009.index_ref, bf16[36,128,128]{2,1,0:T(8,128)(2,1)S(1)} %pad_maximum_fusion.13.refs_0_, bf16[36,128,128]{2,1,0:T(8,128)(2,1)S(1)} %collective-permute-done.17.refs_1_, ...), custom_call_target="tpu_custom_call" | custom-call | bytes 37748736 | tf_op jit(solution)/shard_map/cond/branch_1_fun/fetch_matrix/pallas_call | solution.py:199
  672.0 16.6 %fusion.459 = f32[512,6144]{1,0:T(8,128)} fusion(bf16[512,1536]{1,0:T(8,128)(2,1)S(1)} %fusion.37, bf16[1536,6144]{1,0:T(8,128)(2,1)} %fetch_matrix.26), kind=kOutput, calls=%fused_computation.990 | convolution fusion | flops 9663676416 | bytes 33030144 | tf_op jit(solution)/shard_map/cond/branch_1_fun/dot_general | solution.py:726
  688.5 21.3 %fetch_matrix.27 = bf16[3072,1536]{1,0:T(8,128)(2,1)} custom-call(s32[288]{0:T(512)S(1)} %slice.1024.source_ref, s32[288]{0:T(512)S(1)} %slice.1025.index_ref, bf16[36,128,128]{2,1,0:T(8,128)(2,1)S(1)} %pad_maximum_fusion.13.refs_0_, bf16[36,128,128]{2,1,0:T(8,128)(2,1)S(1)} %collective-permute-done.17.refs_1_, ...), custom_call_target="tpu_custom_call" | custom-call | bytes 18874368 | tf_op jit(solution)/shard_map/cond/branch_1_fun/fetch_matrix/pallas_call | solution.py:199
  709.9 14.6 fusion.7
  724.5 15.8 %fusion.57 = bf16[512,1536]{1,0:T(8,128)(2,1)S(1)} fusion(bf16[1536,6144]{1,0:T(8,128)(2,1)} %fetch_matrix.26, bf16[512,3072]{1,0:T(8,128)(2,1)} %get-tuple-element.429, bf16[512,3072]{1,0:T(8,128)(2,1)} %get-tuple-element.428), kind=kOutput, calls=%fused_computation.134 | convolution fusion | flops 9677045760 | bytes 26738688 | tf_op jit(solution)/shard_map/cond/branch_1_fun/dot_general | solution.py:726
  740.3 16.4 %convolution_convert_fusion.grad_ref = bf16[1536,6144]{1,0:T(8,128)(2,1)} fusion(bf16[512,1536]{1,0:T(8,128)(2,1)S(1)} %copy-done.173, bf16[512,3072]{1,0:T(8,128)(2,1)} %get-tuple-element.429, bf16[512,3072]{1,0:T(8,128)(2,1)} %get-tuple-element.428), kind=kOutput, calls=%fused_computation.12 | convolution fusion | flops 9685696512 | bytes 26738688 | tf_op jit(solution)/shard_map/cond/branch_1_fun/dot_general | solution.py:726
  756.7 9.3 convolution_convert_fusion.2.grad_ref
  766.1 12.6 as_tiles.21.refs_0_
  778.7 29.1 %as_tiles.22.refs_0_ = bf16[1368,128,128]{2,1,0:T(8,128)(2,1)} custom-call(bf16[1536,6144]{1,0:T(8,128)(2,1)} %convolution_convert_fusion.grad_ref, bf16[1368,128,128]{2,1,0:T(8,128)(2,1)} %as_tiles.21.refs_0_), custom_call_target="tpu_custom_call", output_to_operand_aliasing={{}: (1, {})} | custom-call | bytes 37748736 | tf_op jit(solution)/shard_map/cond/branch_1_fun/as_tiles/pallas_call | solution.py:245
  807.8 14.0 gather_fusion.5
  821.8 12.3 fusion.435
  843.1 21.3 %gather_fusion.6 = bf16[544,128,128]{2,1,0:T(8,128)(2,1)} fusion(bf16[1368,128,128]{2,1,0:T(8,128)(2,1)} %as_tiles.22.refs_0_, s32[1024]{0:T(1024)S(1)} %pad_clamp_fusion.2), kind=kCustom, calls=%fused_computation.6 | custom fusion | bytes 35653760 | tf_op jit(solution)/shard_map/cond/branch_1_fun/gather | solution.py:991
  874.9 7.6 fusion.433
  960.5 8.0 multiply_reduce_fusion
  987.7 9.7 fusion.17
  1036.4 33.3 %collective-permute-done.52 = bf16[2,128,1536]{2,1,0:T(8,128)(2,1)} collective-permute-done((bf16[2,128,1536]{2,1,0:T(8,128)(2,1)}, bf16[2,128,1536]{2,1,0:T(8,128)(2,1)}, u32[]{:S(2)}, u32[]{:S(2)}) %collective-permute-start.52) | collective-permute-done | bytes 786464 | tf_op jit(solution)/shard_map/cond/branch_1_fun/ppermute | solution.py:40
  1069.7 17.6 %collective-permute-done.53 = bf16[2,128,1536]{2,1,0:T(8,128)(2,1)} collective-permute-done((bf16[2,128,1536]{2,1,0:T(8,128)(2,1)}, bf16[2,128,1536]{2,1,0:T(8,128)(2,1)}, u32[]{:S(2)}, u32[]{:S(2)}) %collective-permute-start.53) | collective-permute-done | bytes 786464 | tf_op jit(solution)/shard_map/cond/branch_1_fun/ppermute | solution.py:41
  1124.5 8.8 as_tiles.27
  1133.3 17.7 %gather_fusion.8 = bf16[276,128,128]{2,1,0:T(8,128)(2,1)} fusion(bf16[1368,128,128]{2,1,0:T(8,128)(2,1)} %as_tiles.27, s32[1024]{0:T(1024)S(1)} %copy-done.287), kind=kCustom, calls=%fused_computation.8 | custom fusion | bytes 18089040 | tf_op jit(solution)/shard_map/cond/branch_1_fun/gather | solution.py:991
  1151.0 9.5 fusion.437
  1191.6 8.7 collective-permute-done.62
  1208.2 57.0 %collective-permute-done.63 = bf16[38,128,128]{2,1,0:T(8,128)(2,1)S(1)} collective-permute-done((bf16[38,128,128]{2,1,0:T(8,128)(2,1)}, bf16[38,128,128]{2,1,0:T(8,128)(2,1)S(1)}, u32[]{:S(2)}, u32[]{:S(2)}) %collective-permute-start.63) | collective-permute-done | bytes 1245216 | tf_op jit(solution)/shard_map/cond/branch_1_fun/ppermute | solution.py:273
  1267.1 11.9 gather_fusion.10
  1301.1 30.1 %collective-permute-done.64 = bf16[2,2,14,128,128]{4,3,2,1,0:T(8,128)(2,1)} collective-permute-done((bf16[2,2,14,128,128]{4,3,2,1,0:T(8,128)(2,1)}, bf16[2,2,14,128,128]{4,3,2,1,0:T(8,128)(2,1)}, u32[]{:S(2)}, u32[]{:S(2)}) %collective-permute-start.64) | collective-permute-done | bytes 1835040 | tf_op jit(solution)/shard_map/cond/branch_1_fun/ppermute | solution.py:273
  1339.1 8.4 fusion.56
  1352.0 24.7 %collective-permute-done.65 = bf16[2,2,14,128,128]{4,3,2,1,0:T(8,128)(2,1)S(1)} collective-permute-done((bf16[2,2,14,128,128]{4,3,2,1,0:T(8,128)(2,1)}, bf16[2,2,14,128,128]{4,3,2,1,0:T(8,128)(2,1)S(1)}, u32[]{:S(2)}, u32[]{:S(2)}) %collective-permute-start.65) | collective-permute-done | bytes 1835040 | tf_op jit(solution)/shard_map/cond/branch_1_fun/ppermute | solution.py:273
  1382.3 15.8 %collective-permute-done.66 = bf16[2,14,128,128]{3,2,1,0:T(8,128)(2,1)S(1)} collective-permute-done((bf16[2,14,128,128]{3,2,1,0:T(8,128)(2,1)S(1)}, bf16[2,14,128,128]{3,2,1,0:T(8,128)(2,1)S(1)}, u32[]{:S(2)}, u32[]{:S(2)}) %collective-permute-start.66) | collective-permute-done | bytes 917536 | tf_op jit(solution)/shard_map/cond/branch_1_fun/ppermute | solution.py:273
  1412.6 14.9 collective-permute-done.69
  1436.1 17.1 %collective-permute-done.71 = bf16[4,128,128]{2,1,0:T(8,128)(2,1)S(1)} collective-permute-done((bf16[4,128,128]{2,1,0:T(8,128)(2,1)S(1)}, bf16[4,128,128]{2,1,0:T(8,128)(2,1)S(1)}, u32[]{:S(2)}, u32[]{:S(2)}) %collective-permute-start.71) | collective-permute-done | bytes 131104 | tf_op jit(solution)/shard_map/cond/branch_1_fun/ppermute | solution.py:273
  1464.8 17.4 %collective-permute-done.73 = bf16[32,128,128]{2,1,0:T(8,128)(2,1)S(1)} collective-permute-done((bf16[32,128,128]{2,1,0:T(8,128)(2,1)S(1)}, bf16[32,128,128]{2,1,0:T(8,128)(2,1)S(1)}, u32[]{:S(2)}, u32[]{:S(2)}) %collective-permute-start.73) | collective-permute-done | bytes 1048608 | tf_op jit(solution)/shard_map/cond/branch_1_fun/ppermute | solution.py:273
  1486.9 51.7 %adam_slots.3 = (f32[141,128,128]{2,1,0:T(8,128)}, f32[141,128,128]{2,1,0:T(8,128)}, f32[141,128,128]{2,1,0:T(8,128)}) custom-call(s32[2]{0:T(128)S(1)} %broadcast.1797.refs_0_, s32[141]{0:T(256)S(1)} %copy-done.17, s32[141]{0:T(256)S(1)} %copy-done.18, s32[141]{0:T(256)S(1)} %fusion.218.refs_3_, f32[141]{0:T(256)S(1)} %select_reduce_fusion.6.refs_4_, ...), custom_call_target="tpu_custom_call" | custom-call | flops 754974720 | bytes 30031872 | tf_op jit(solution)/shard_map/cond/branch_1_fun/adam_slots/pallas_call | solution.py:624
  (887 shorter events, 585.3 us)
Async XLA Ops:
  47.6 189.6 %all-reduce.20.cloned.1.call-start = ((), (), s32[]{:S(2)}) async-start(), calls=%async_computation.5 | async-start | bytes 589824 | tf_op jit(solution)/shard_map/cond/branch_1_fun/psum | solution.py:848
  77.4 52.9 %collective-permute-start.20 = (bf16[34,128,128]{2,1,0:T(8,128)(2,1)}, bf16[34,128,128]{2,1,0:T(8,128)(2,1)}, u32[]{:S(2)}, u32[]{:S(2)}) collective-permute-start(bf16[34,128,128]{2,1,0:T(8,128)(2,1)} %get-tuple-element.148), channel_id=1, source_target_pairs={{0,8},{2,10},{4,12},{6,14},{8,16},{10,18},{12,20},{14,22},{16,24},... | collective-permute-start | bytes 3342344 | tf_op jit(solution)/shard_map/cond/branch_1_fun/ppermute | solution.py:273
  130.3 41.1 %collective-permute-start.21 = (bf16[34,128,128]{2,1,0:T(8,128)(2,1)}, bf16[34,128,128]{2,1,0:T(8,128)(2,1)S(1)}, u32[]{:S(2)}, u32[]{:S(2)}) collective-permute-start(bf16[34,128,128]{2,1,0:T(8,128)(2,1)} %collective-permute-done.20), channel_id=1, source_target_pairs={{0,8},{2,10},{4,12},{6,14},{8,16},{10,18},{12,20},{14,22},{16,24},... | collective-permute-start | bytes 3342344 | tf_op jit(solution)/shard_map/cond/branch_1_fun/ppermute | solution.py:273
  173.2 63.1 %collective-permute-start.22 = (bf16[68,128,128]{2,1,0:T(8,128)(2,1)}, bf16[68,128,128]{2,1,0:T(8,128)(2,1)}, u32[]{:S(2)}, u32[]{:S(2)}) collective-permute-start(bf16[68,128,128]{2,1,0:T(8,128)(2,1)} %pad_maximum_fusion.9.refs_4_), channel_id=1, source_target_pairs={{0,4},{2,6},{4,0},{6,2},{8,12},{10,14},{12,8},{14,10},{16,20},{18,... | collective-permute-start | bytes 6684680 | tf_op jit(solution)/shard_map/cond/branch_1_fun/ppermute | solution.py:273
  176.7 59.9 %collective-permute-start.25 = (bf16[68,128,128]{2,1,0:T(8,128)(2,1)}, bf16[68,128,128]{2,1,0:T(8,128)(2,1)}, u32[]{:S(2)}, u32[]{:S(2)}) collective-permute-start(bf16[68,128,128]{2,1,0:T(8,128)(2,1)} %pad_maximum_fusion.10.refs_8_), channel_id=1, source_target_pairs={{0,2},{2,0},{4,6},{6,4},{8,10},{10,8},{12,14},{14,12},{16,18},{18,... | collective-permute-start | bytes 6684680 | tf_op jit(solution)/shard_map/cond/branch_1_fun/ppermute | solution.py:273
  192.2 85.1 %collective-permute-start.23 = (bf16[68,128,128]{2,1,0:T(8,128)(2,1)}, bf16[68,128,128]{2,1,0:T(8,128)(2,1)}, u32[]{:S(2)}, u32[]{:S(2)}) collective-permute-start(bf16[68,128,128]{2,1,0:T(8,128)(2,1)} %pad_maximum_fusion.9.refs_4_), channel_id=1, source_target_pairs={{0,2},{2,0},{4,6},{6,4},{8,10},{10,8},{12,14},{14,12},{16,18},{18,... | collective-permute-start | bytes 6684680 | tf_op jit(solution)/shard_map/cond/branch_1_fun/ppermute | solution.py:273
  199.6 91.3 %collective-permute-start.26 = (bf16[68,128,128]{2,1,0:T(8,128)(2,1)}, bf16[68,128,128]{2,1,0:T(8,128)(2,1)}, u32[]{:S(2)}, u32[]{:S(2)}) collective-permute-start(bf16[68,128,128]{2,1,0:T(8,128)(2,1)} %pad_maximum_fusion.10.refs_8_), channel_id=1, source_target_pairs={{0,4},{2,6},{4,0},{6,2},{8,12},{10,14},{12,8},{14,10},{16,20},{18,... | collective-permute-start | bytes 6684680 | tf_op jit(solution)/shard_map/cond/branch_1_fun/ppermute | solution.py:273
  215.9 61.4 %collective-permute-start.18 = (bf16[36,128,128]{2,1,0:T(8,128)(2,1)S(1)}, bf16[36,128,128]{2,1,0:T(8,128)(2,1)S(1)}, u32[]{:S(2)}, u32[]{:S(2)}) collective-permute-start(bf16[36,128,128]{2,1,0:T(8,128)(2,1)S(1)} %collective-permute-done.17.refs_1_), channel_id=1, source_target_pairs={{0,8},{2,10},{4,12},{6,14},{8,16},{10,18},{12,20},{14,22},{16,24},... | collective-permute-start | bytes 3538952 | tf_op jit(solution)/shard_map/cond/branch_1_fun/ppermute | solution.py:273
  236.3 98.2 %collective-permute-start.24 = (bf16[68,128,128]{2,1,0:T(8,128)(2,1)}, bf16[68,128,128]{2,1,0:T(8,128)(2,1)}, u32[]{:S(2)}, u32[]{:S(2)}) collective-permute-start(bf16[68,128,128]{2,1,0:T(8,128)(2,1)} %collective-permute-done.22.refs_5_), channel_id=1, source_target_pairs={{0,2},{2,0},{4,6},{6,4},{8,10},{10,8},{12,14},{14,12},{16,18},{18,... | collective-permute-start | bytes 6684680 | tf_op jit(solution)/shard_map/cond/branch_1_fun/ppermute | solution.py:273
  236.6 98.0 %collective-permute-start.27 = (bf16[68,128,128]{2,1,0:T(8,128)(2,1)}, bf16[68,128,128]{2,1,0:T(8,128)(2,1)}, u32[]{:S(2)}, u32[]{:S(2)}) collective-permute-start(bf16[68,128,128]{2,1,0:T(8,128)(2,1)} %collective-permute-done.25.refs_9_), channel_id=1, source_target_pairs={{0,4},{2,6},{4,0},{6,2},{8,12},{10,14},{12,8},{14,10},{16,20},{18,... | collective-permute-start | bytes 6684680 | tf_op jit(solution)/shard_map/cond/branch_1_fun/ppermute | solution.py:273
  277.3 57.3 %collective-permute-start.37 = (bf16[38,128,128]{2,1,0:T(8,128)(2,1)S(1)}, bf16[38,128,128]{2,1,0:T(8,128)(2,1)}, u32[]{:S(2)}, u32[]{:S(2)}) collective-permute-start(bf16[38,128,128]{2,1,0:T(8,128)(2,1)S(1)} %fusion.548), channel_id=1, source_target_pairs={{0,8},{2,10},{4,12},{6,14},{8,16},{10,18},{12,20},{14,22},{16,24},... | collective-permute-start | bytes 3735560 | tf_op jit(solution)/shard_map/cond/branch_1_fun/ppermute | solution.py:273
  277.3 57.3 %collective-permute-start.19 = (bf16[36,128,128]{2,1,0:T(8,128)(2,1)S(1)}, bf16[36,128,128]{2,1,0:T(8,128)(2,1)S(1)}, u32[]{:S(2)}, u32[]{:S(2)}) collective-permute-start(bf16[36,128,128]{2,1,0:T(8,128)(2,1)S(1)} %collective-permute-done.18.refs_2_), channel_id=1, source_target_pairs={{0,8},{2,10},{4,12},{6,14},{8,16},{10,18},{12,20},{14,22},{16,24},... | collective-permute-start | bytes 3538952 | tf_op jit(solution)/shard_map/cond/branch_1_fun/ppermute | solution.py:273
  294.7 39.4 %collective-permute-start.32 = (bf16[18,128,128]{2,1,0:T(8,128)(2,1)S(1)}, bf16[18,128,128]{2,1,0:T(8,128)(2,1)S(1)}, u32[]{:S(2)}, u32[]{:S(2)}) collective-permute-start(bf16[18,128,128]{2,1,0:T(8,128)(2,1)S(1)} %fusion.135), channel_id=1, source_target_pairs={{0,2},{2,0},{4,6},{6,4},{8,10},{10,8},{12,14},{14,12},{16,18},{18,... | collective-permute-start | bytes 1769480 | tf_op jit(solution)/shard_map/cond/branch_1_fun/ppermute | solution.py:273
  334.6 52.5 %collective-permute-start.38 = (bf16[38,128,128]{2,1,0:T(8,128)(2,1)}, bf16[38,128,128]{2,1,0:T(8,128)(2,1)}, u32[]{:S(2)}, u32[]{:S(2)}) collective-permute-start(bf16[38,128,128]{2,1,0:T(8,128)(2,1)} %collective-permute-done.37), channel_id=1, source_target_pairs={{0,8},{2,10},{4,12},{6,14},{8,16},{10,18},{12,20},{14,22},{16,24},... | collective-permute-start | bytes 3735560 | tf_op jit(solution)/shard_map/cond/branch_1_fun/ppermute | solution.py:273
  367.8 94.6 %collective-permute-start.34 = (bf16[72,128,128]{2,1,0:T(8,128)(2,1)}, bf16[72,128,128]{2,1,0:T(8,128)(2,1)}, u32[]{:S(2)}, u32[]{:S(2)}) collective-permute-start(bf16[72,128,128]{2,1,0:T(8,128)(2,1)} %pad_maximum_fusion.8.refs_12_), channel_id=1, source_target_pairs={{0,8},{2,10},{4,12},{6,14},{8,16},{10,18},{12,20},{14,22},{16,24},... | collective-permute-start | bytes 7077896 | tf_op jit(solution)/shard_map/cond/branch_1_fun/ppermute | solution.py:273
  387.1 70.7 %collective-permute-start.39 = (bf16[38,128,128]{2,1,0:T(8,128)(2,1)}, bf16[38,128,128]{2,1,0:T(8,128)(2,1)}, u32[]{:S(2)}, u32[]{:S(2)}) collective-permute-start(bf16[38,128,128]{2,1,0:T(8,128)(2,1)} %collective-permute-done.38), channel_id=1, source_target_pairs={{0,8},{2,10},{4,12},{6,14},{8,16},{10,18},{12,20},{14,22},{16,24},... | collective-permute-start | bytes 3735560 | tf_op jit(solution)/shard_map/cond/branch_1_fun/ppermute | solution.py:273
  417.9 45.1 %collective-permute-start.30 = (bf16[512,1536]{1,0:T(8,128)(2,1)}, bf16[512,1536]{1,0:T(8,128)(2,1)}, u32[]{:S(2)}, u32[]{:S(2)}) collective-permute-start(bf16[512,1536]{1,0:T(8,128)(2,1)} %convolution_convert_fusion.12), channel_id=1, source_target_pairs={{0,1},{1,0},{2,3},{3,2},{4,5},{5,4},{6,7},{7,6},{8,9},{9,8},{10,11... | collective-permute-start | bytes 4718600 | tf_op jit(solution)/shard_map/cond/branch_1_fun/ppermute | solution.py:424
  460.8 57.2 %collective-permute-start.40 = (bf16[76,128,128]{2,1,0:T(8,128)(2,1)}, bf16[76,128,128]{2,1,0:T(8,128)(2,1)}, u32[]{:S(2)}, u32[]{:S(2)}) collective-permute-start(bf16[76,128,128]{2,1,0:T(8,128)(2,1)} %pad_maximum_fusion.6.refs_16_), channel_id=1, source_target_pairs={{0,4},{2,6},{4,0},{6,2},{8,12},{10,14},{12,8},{14,10},{16,20},{18,... | collective-permute-start | bytes 7471112 | tf_op jit(solution)/shard_map/cond/branch_1_fun/ppermute | solution.py:273
  462.4 57.3 %collective-permute-start.43 = (bf16[76,128,128]{2,1,0:T(8,128)(2,1)}, bf16[76,128,128]{2,1,0:T(8,128)(2,1)}, u32[]{:S(2)}, u32[]{:S(2)}) collective-permute-start(bf16[76,128,128]{2,1,0:T(8,128)(2,1)} %pad_maximum_fusion.7.refs_20_), channel_id=1, source_target_pairs={{0,2},{2,0},{4,6},{6,4},{8,10},{10,8},{12,14},{14,12},{16,18},{18,... | collective-permute-start | bytes 7471112 | tf_op jit(solution)/shard_map/cond/branch_1_fun/ppermute | solution.py:273
  462.4 61.4 %collective-permute-start.35 = (bf16[72,128,128]{2,1,0:T(8,128)(2,1)}, bf16[72,128,128]{2,1,0:T(8,128)(2,1)}, u32[]{:S(2)}, u32[]{:S(2)}) collective-permute-start(bf16[72,128,128]{2,1,0:T(8,128)(2,1)} %collective-permute-done.34.refs_13_), channel_id=1, source_target_pairs={{0,8},{2,10},{4,12},{6,14},{8,16},{10,18},{12,20},{14,22},{16,24},... | collective-permute-start | bytes 7077896 | tf_op jit(solution)/shard_map/cond/branch_1_fun/ppermute | solution.py:273
  500.3 72.8 %collective-permute-start.41 = (bf16[76,128,128]{2,1,0:T(8,128)(2,1)}, bf16[76,128,128]{2,1,0:T(8,128)(2,1)}, u32[]{:S(2)}, u32[]{:S(2)}) collective-permute-start(bf16[76,128,128]{2,1,0:T(8,128)(2,1)} %pad_maximum_fusion.6.refs_16_), channel_id=1, source_target_pairs={{0,2},{2,0},{4,6},{6,4},{8,10},{10,8},{12,14},{14,12},{16,18},{18,... | collective-permute-start | bytes 7471112 | tf_op jit(solution)/shard_map/cond/branch_1_fun/ppermute | solution.py:273
  502.2 70.8 %collective-permute-start.44 = (bf16[76,128,128]{2,1,0:T(8,128)(2,1)}, bf16[76,128,128]{2,1,0:T(8,128)(2,1)}, u32[]{:S(2)}, u32[]{:S(2)}) collective-permute-start(bf16[76,128,128]{2,1,0:T(8,128)(2,1)} %pad_maximum_fusion.7.refs_20_), channel_id=1, source_target_pairs={{0,4},{2,6},{4,0},{6,2},{8,12},{10,14},{12,8},{14,10},{16,20},{18,... | collective-permute-start | bytes 7471112 | tf_op jit(solution)/shard_map/cond/branch_1_fun/ppermute | solution.py:273
  517.9 102.3 %collective-permute-start.42 = (bf16[76,128,128]{2,1,0:T(8,128)(2,1)}, bf16[76,128,128]{2,1,0:T(8,128)(2,1)}, u32[]{:S(2)}, u32[]{:S(2)}) collective-permute-start(bf16[76,128,128]{2,1,0:T(8,128)(2,1)} %collective-permute-done.40.refs_17_), channel_id=1, source_target_pairs={{0,2},{2,0},{4,6},{6,4},{8,10},{10,8},{12,14},{14,12},{16,18},{18,... | collective-permute-start | bytes 7471112 | tf_op jit(solution)/shard_map/cond/branch_1_fun/ppermute | solution.py:273
  519.7 100.5 %collective-permute-start.45 = (bf16[76,128,128]{2,1,0:T(8,128)(2,1)}, bf16[76,128,128]{2,1,0:T(8,128)(2,1)}, u32[]{:S(2)}, u32[]{:S(2)}) collective-permute-start(bf16[76,128,128]{2,1,0:T(8,128)(2,1)} %collective-permute-done.43.refs_21_), channel_id=1, source_target_pairs={{0,4},{2,6},{4,0},{6,2},{8,12},{10,14},{12,8},{14,10},{16,20},{18,... | collective-permute-start | bytes 7471112 | tf_op jit(solution)/shard_map/cond/branch_1_fun/ppermute | solution.py:273
  523.8 96.4 %collective-permute-start.36 = (bf16[72,128,128]{2,1,0:T(8,128)(2,1)}, bf16[72,128,128]{2,1,0:T(8,128)(2,1)}, u32[]{:S(2)}, u32[]{:S(2)}) collective-permute-start(bf16[72,128,128]{2,1,0:T(8,128)(2,1)} %collective-permute-done.35.refs_14_), channel_id=1, source_target_pairs={{0,8},{2,10},{4,12},{6,14},{8,16},{10,18},{12,20},{14,22},{16,24},... | collective-permute-start | bytes 7077896 | tf_op jit(solution)/shard_map/cond/branch_1_fun/ppermute | solution.py:273
  756.7 125.7 %collective-permute-start.46 = (bf16[512,1536]{1,0:T(8,128)(2,1)S(1)}, bf16[512,1536]{1,0:T(8,128)(2,1)S(1)}, u32[]{:S(2)}, u32[]{:S(2)}) collective-permute-start(bf16[512,1536]{1,0:T(8,128)(2,1)S(1)} %fusion.57), channel_id=1, source_target_pairs={{0,1},{1,0},{2,3},{3,2},{4,5},{5,4},{6,7},{7,6},{8,9},{9,8},{10,11... | collective-permute-start | bytes 4718600 | tf_op jit(solution)/shard_map/cond/branch_1_fun/ppermute | solution.py:424
  837.8 93.2 %collective-permute-start.48 = (bf16[2,2,20,128,128]{4,3,2,1,0:T(8,128)(2,1)}, bf16[2,2,20,128,128]{4,3,2,1,0:T(8,128)(2,1)}, u32[]{:S(2)}, u32[]{:S(2)}) collective-permute-start(bf16[2,2,20,128,128]{4,3,2,1,0:T(8,128)(2,1)} %bitcast.114), channel_id=1, source_target_pairs={{0,8},{2,10},{4,12},{6,14},{8,16},{10,18},{12,20},{14,22},{16,24},... | collective-permute-start | bytes 7864328 | tf_op jit(solution)/shard_map/cond/branch_1_fun/ppermute | solution.py:273
  838.2 144.8 %collective-permute-start.49 = (bf16[2,4,19,128,128]{4,3,2,1,0:T(8,128)(2,1)}, bf16[2,4,19,128,128]{4,3,2,1,0:T(8,128)(2,1)}, u32[]{:S(2)}, u32[]{:S(2)}) collective-permute-start(bf16[2,4,19,128,128]{4,3,2,1,0:T(8,128)(2,1)} %bitcast.122), channel_id=1, source_target_pairs={{0,2},{2,0},{4,6},{6,4},{8,10},{10,8},{12,14},{14,12},{16,18},{18,... | collective-permute-start | bytes 14942216 | tf_op jit(solution)/shard_map/cond/branch_1_fun/ppermute | solution.py:273
  839.4 145.8 %collective-permute-start.50 = (bf16[2,4,19,128,128]{4,3,2,1,0:T(8,128)(2,1)}, bf16[2,4,19,128,128]{4,3,2,1,0:T(8,128)(2,1)}, u32[]{:S(2)}, u32[]{:S(2)}) collective-permute-start(bf16[2,4,19,128,128]{4,3,2,1,0:T(8,128)(2,1)} %bitcast.124), channel_id=1, source_target_pairs={{0,4},{2,6},{4,0},{6,2},{8,12},{10,14},{12,8},{14,10},{16,20},{18,... | collective-permute-start | bytes 14942216 | tf_op jit(solution)/shard_map/cond/branch_1_fun/ppermute | solution.py:273
  938.4 68.5 %collective-permute-start.51 = (bf16[2,2,20,128,128]{4,3,2,1,0:T(8,128)(2,1)}, bf16[2,2,20,128,128]{4,3,2,1,0:T(8,128)(2,1)}, u32[]{:S(2)}, u32[]{:S(2)}) collective-permute-start(bf16[2,2,20,128,128]{4,3,2,1,0:T(8,128)(2,1)} %fusion.16), channel_id=1, source_target_pairs={{0,8},{2,10},{4,12},{6,14},{8,16},{10,18},{12,20},{14,22},{16,24},... | collective-permute-start | bytes 7864328 | tf_op jit(solution)/shard_map/cond/branch_1_fun/ppermute | solution.py:273
  997.5 92.8 %collective-permute-start.55 = (bf16[4,19,128,128]{3,2,1,0:T(8,128)(2,1)}, bf16[4,19,128,128]{3,2,1,0:T(8,128)(2,1)}, u32[]{:S(2)}, u32[]{:S(2)}) collective-permute-start(bf16[4,19,128,128]{3,2,1,0:T(8,128)(2,1)} %get-tuple-element.460), channel_id=1, source_target_pairs={{0,2},{2,0},{4,6},{6,4},{8,10},{10,8},{12,14},{14,12},{16,18},{18,... | collective-permute-start | bytes 7471112 | tf_op jit(solution)/shard_map/cond/branch_1_fun/ppermute | solution.py:273
  1006.3 86.7 %collective-permute-start.54 = (bf16[4,19,128,128]{3,2,1,0:T(8,128)(2,1)}, bf16[4,19,128,128]{3,2,1,0:T(8,128)(2,1)}, u32[]{:S(2)}, u32[]{:S(2)}) collective-permute-start(bf16[4,19,128,128]{3,2,1,0:T(8,128)(2,1)} %get-tuple-element.458), channel_id=1, source_target_pairs={{0,4},{2,6},{4,0},{6,2},{8,12},{10,14},{12,8},{14,10},{16,20},{18,... | collective-permute-start | bytes 7471112 | tf_op jit(solution)/shard_map/cond/branch_1_fun/ppermute | solution.py:273
  1013.9 93.5 %collective-permute-start.56 = (bf16[2,2,20,128,128]{4,3,2,1,0:T(8,128)(2,1)}, bf16[2,2,20,128,128]{4,3,2,1,0:T(8,128)(2,1)}, u32[]{:S(2)}, u32[]{:S(2)}) collective-permute-start(bf16[2,2,20,128,128]{4,3,2,1,0:T(8,128)(2,1)} %fusion.15), channel_id=1, source_target_pairs={{0,8},{2,10},{4,12},{6,14},{8,16},{10,18},{12,20},{14,22},{16,24},... | collective-permute-start | bytes 7864328 | tf_op jit(solution)/shard_map/cond/branch_1_fun/ppermute | solution.py:273
  1019.0 50.8 %collective-permute-start.52 = (bf16[2,128,1536]{2,1,0:T(8,128)(2,1)}, bf16[2,128,1536]{2,1,0:T(8,128)(2,1)}, u32[]{:S(2)}, u32[]{:S(2)}) collective-permute-start(bf16[2,128,1536]{2,1,0:T(8,128)(2,1)} %get-tuple-element.476), channel_id=1, source_target_pairs={{0,2},{2,4},{4,6},{6,8},{8,10},{10,12},{12,14},{14,16},{16,18},{18... | collective-permute-start | bytes 2359304 | tf_op jit(solution)/shard_map/cond/branch_1_fun/ppermute | solution.py:40
  1023.4 63.8 %collective-permute-start.53 = (bf16[2,128,1536]{2,1,0:T(8,128)(2,1)}, bf16[2,128,1536]{2,1,0:T(8,128)(2,1)}, u32[]{:S(2)}, u32[]{:S(2)}) collective-permute-start(bf16[2,128,1536]{2,1,0:T(8,128)(2,1)} %get-tuple-element.477), channel_id=1, source_target_pairs={{2,0},{4,2},{6,4},{8,6},{10,8},{12,10},{14,12},{16,14},{18,16},{20... | collective-permute-start | bytes 2359304 | tf_op jit(solution)/shard_map/cond/branch_1_fun/ppermute | solution.py:41
  1104.1 58.5 %collective-permute-start.59 = (bf16[38,128,128]{2,1,0:T(8,128)(2,1)}, bf16[38,128,128]{2,1,0:T(8,128)(2,1)}, u32[]{:S(2)}, u32[]{:S(2)}) collective-permute-start(bf16[38,128,128]{2,1,0:T(8,128)(2,1)} %pad_maximum_fusion.12), channel_id=1, source_target_pairs={{0,8},{2,10},{4,12},{6,14},{8,16},{10,18},{12,20},{14,22},{16,24},... | collective-permute-start | bytes 3735560 | tf_op jit(solution)/shard_map/cond/branch_1_fun/ppermute | solution.py:273
  1113.8 59.0 %collective-permute-start.58 = (bf16[512,1536]{1,0:T(8,128)(2,1)S(1)}, bf16[512,1536]{1,0:T(8,128)(2,1)S(1)}, u32[]{:S(2)}, u32[]{:S(2)}) collective-permute-start(bf16[512,1536]{1,0:T(8,128)(2,1)S(1)} %convolution_convert_fusion.9), channel_id=1, source_target_pairs={{0,1},{1,0},{2,3},{3,2},{4,5},{5,4},{6,7},{7,6},{8,9},{9,8},{10,11... | collective-permute-start | bytes 4718600 | tf_op jit(solution)/shard_map/cond/branch_1_fun/ppermute | solution.py:424
  1118.4 51.9 %collective-permute-start.60 = (bf16[2,20,128,128]{3,2,1,0:T(8,128)(2,1)}, bf16[2,20,128,128]{3,2,1,0:T(8,128)(2,1)}, u32[]{:S(2)}, u32[]{:S(2)}) collective-permute-start(bf16[2,20,128,128]{3,2,1,0:T(8,128)(2,1)} %get-tuple-element.483), channel_id=1, source_target_pairs={{0,4},{2,6},{4,0},{6,2},{8,12},{10,14},{12,8},{14,10},{16,20},{18,... | collective-permute-start | bytes 3932168 | tf_op jit(solution)/shard_map/cond/branch_1_fun/ppermute | solution.py:273
  1160.5 132.5 %collective-permute-start.76 = (bf16[2,4,14,128,128]{4,3,2,1,0:T(8,128)(2,1)}, bf16[2,4,14,128,128]{4,3,2,1,0:T(8,128)(2,1)}, u32[]{:S(2)}, u32[]{:S(2)}) collective-permute-start(bf16[2,4,14,128,128]{4,3,2,1,0:T(8,128)(2,1)} %bitcast.190), channel_id=1, source_target_pairs={{0,4},{2,6},{4,0},{6,2},{8,12},{10,14},{12,8},{14,10},{16,20},{18,... | collective-permute-start | bytes 11010056 | tf_op jit(solution)/shard_map/cond/branch_1_fun/ppermute | solution.py:273
  1189.8 94.9 %collective-permute-start.61 = (bf16[2,2,14,128,128]{4,3,2,1,0:T(8,128)(2,1)}, bf16[2,2,14,128,128]{4,3,2,1,0:T(8,128)(2,1)}, u32[]{:S(2)}, u32[]{:S(2)}) collective-permute-start(bf16[2,2,14,128,128]{4,3,2,1,0:T(8,128)(2,1)} %pad_maximum_fusion.11), channel_id=1, source_target_pairs={{0,8},{2,10},{4,12},{6,14},{8,16},{10,18},{12,20},{14,22},{16,24},... | collective-permute-start | bytes 5505032 | tf_op jit(solution)/shard_map/cond/branch_1_fun/ppermute | solution.py:273
  1203.1 62.1 %collective-permute-start.63 = (bf16[38,128,128]{2,1,0:T(8,128)(2,1)}, bf16[38,128,128]{2,1,0:T(8,128)(2,1)S(1)}, u32[]{:S(2)}, u32[]{:S(2)}) collective-permute-start(bf16[38,128,128]{2,1,0:T(8,128)(2,1)} %add_convert_fusion.6), channel_id=1, source_target_pairs={{0,8},{2,10},{4,12},{6,14},{8,16},{10,18},{12,20},{14,22},{16,24},... | collective-permute-start | bytes 3735560 | tf_op jit(solution)/shard_map/cond/branch_1_fun/ppermute | solution.py:273
  1203.6 131.1 %collective-permute-start.74 = (bf16[2,4,14,128,128]{4,3,2,1,0:T(8,128)(2,1)}, bf16[2,4,14,128,128]{4,3,2,1,0:T(8,128)(2,1)}, u32[]{:S(2)}, u32[]{:S(2)}) collective-permute-start(bf16[2,4,14,128,128]{4,3,2,1,0:T(8,128)(2,1)} %bitcast.184), channel_id=1, source_target_pairs={{0,2},{2,0},{4,6},{6,4},{8,10},{10,8},{12,14},{14,12},{16,18},{18,... | collective-permute-start | bytes 11010056 | tf_op jit(solution)/shard_map/cond/branch_1_fun/ppermute | solution.py:273
  1288.1 43.1 %collective-permute-start.64 = (bf16[2,2,14,128,128]{4,3,2,1,0:T(8,128)(2,1)}, bf16[2,2,14,128,128]{4,3,2,1,0:T(8,128)(2,1)}, u32[]{:S(2)}, u32[]{:S(2)}) collective-permute-start(bf16[2,2,14,128,128]{4,3,2,1,0:T(8,128)(2,1)} %fusion.35), channel_id=1, source_target_pairs={{0,8},{2,10},{4,12},{6,14},{8,16},{10,18},{12,20},{14,22},{16,24},... | collective-permute-start | bytes 5505032 | tf_op jit(solution)/shard_map/cond/branch_1_fun/ppermute | solution.py:273
  1299.4 79.1 %collective-permute-start.77 = (bf16[4,14,128,128]{3,2,1,0:T(8,128)(2,1)}, bf16[4,14,128,128]{3,2,1,0:T(8,128)(2,1)}, u32[]{:S(2)}, u32[]{:S(2)}) collective-permute-start(bf16[4,14,128,128]{3,2,1,0:T(8,128)(2,1)} %get-tuple-element.474), channel_id=1, source_target_pairs={{0,2},{2,0},{4,6},{6,4},{8,10},{10,8},{12,14},{14,12},{16,18},{18,... | collective-permute-start | bytes 5505032 | tf_op jit(solution)/shard_map/cond/branch_1_fun/ppermute | solution.py:273
  1334.6 42.1 %collective-permute-start.65 = (bf16[2,2,14,128,128]{4,3,2,1,0:T(8,128)(2,1)}, bf16[2,2,14,128,128]{4,3,2,1,0:T(8,128)(2,1)S(1)}, u32[]{:S(2)}, u32[]{:S(2)}) collective-permute-start(bf16[2,2,14,128,128]{4,3,2,1,0:T(8,128)(2,1)} %fusion.34), channel_id=1, source_target_pairs={{0,8},{2,10},{4,12},{6,14},{8,16},{10,18},{12,20},{14,22},{16,24},... | collective-permute-start | bytes 5505032 | tf_op jit(solution)/shard_map/cond/branch_1_fun/ppermute | solution.py:273
  1338.3 42.3 %collective-permute-start.75 = (bf16[4,14,128,128]{3,2,1,0:T(8,128)(2,1)S(1)}, bf16[4,14,128,128]{3,2,1,0:T(8,128)(2,1)S(1)}, u32[]{:S(2)}, u32[]{:S(2)}) collective-permute-start(bf16[4,14,128,128]{3,2,1,0:T(8,128)(2,1)S(1)} %get-tuple-element.472), channel_id=1, source_target_pairs={{0,4},{2,6},{4,0},{6,2},{8,12},{10,14},{12,8},{14,10},{16,20},{18,... | collective-permute-start | bytes 5505032 | tf_op jit(solution)/shard_map/cond/branch_1_fun/ppermute | solution.py:273
  1347.5 106.6 %collective-permute-start.57 = (bf16[512,1536]{1,0:T(8,128)(2,1)}, bf16[512,1536]{1,0:T(8,128)(2,1)S(1)}, u32[]{:S(2)}, u32[]{:S(2)}) collective-permute-start(bf16[512,1536]{1,0:T(8,128)(2,1)} %fusion.56), channel_id=1, source_target_pairs={{0,1},{1,0},{2,3},{3,2},{4,5},{5,4},{6,7},{7,6},{8,9},{9,8},{10,11... | collective-permute-start | bytes 4718600 | tf_op jit(solution)/shard_map/cond/branch_1_fun/ppermute | solution.py:424
  1348.7 52.7 %collective-permute-start.68 = (bf16[20,128,128]{2,1,0:T(8,128)(2,1)S(1)}, bf16[20,128,128]{2,1,0:T(8,128)(2,1)S(1)}, u32[]{:S(2)}, u32[]{:S(2)}) collective-permute-start(bf16[20,128,128]{2,1,0:T(8,128)(2,1)S(1)} %fusion.125), channel_id=1, source_target_pairs={{0,2},{2,0},{4,6},{6,4},{8,10},{10,8},{12,14},{14,12},{16,18},{18,... | collective-permute-start | bytes 1966088 | tf_op jit(solution)/shard_map/cond/branch_1_fun/ppermute | solution.py:273
  (225 other events, 3294.5 us)
Sparse Core Ops, SparseCore 0:
  77.5 143.6 all-reduce.19
